TPU v7x, 256 devices: a whole 4x4x8 slice. The times are simulated.
256 devices in a mesh: cube: 32 (over y, z_lo, x), col: 8 (over z_hi, core).
Axes of the slice: x: 4, y: 4, z: 8 (z_hi: 4, z_lo: 2; z = z_hi * 2 + z_lo), core: 2. Of those that a mesh axis runs over, the one named last changes fastest.
Arguments:
- ginv: float32 [8192, 8192], P('cube'), may hold values from -6 to 6
- ufactor: float32 [2, 4096, 2048], P(None, 'cube', 'col'), may hold values from -0.09375 to 0.09375
- dinv: float32 [2, 2048], P(None, 'col'), may hold values from 0.5 to 2
- tile_map: int32 [2, 16], replicated, may hold values from 0 to 31, as said below
- counts: int32 [2], replicated, may hold values from 1 to 4096, as said below
- assign: int32 [2], replicated, may hold values from 0 to 1, each once
Outputs:
- cross: float32 [2, 8192, 2048], P(None, 'cube', 'col')
- resist: float32 [2, 8192, 2048], P(None, 'cube', 'col')
- sigma_ff: float32 [2048, 2, 2048], P('cube', None, 'col')
Inputs may be any that keep to these rules, and one draw needn't show every extreme that they name: `tile_map`: the two rows together hold every tile 0 to 31 exactly once. `counts`: one of the two fronts has all 4096 rows live.
All inputs are finite; a program needn't handle non-finite values.
Results may differ from a plain program's by a relative error of at most 0.0001.
Values sent between devices are 32-bit elements; how exact they have to be, the bound alone decides.
No kernel may reach another device: no remote copies, remote signals or barrier semaphores. Data moves between devices by JAX's collectives and lax.ppermute only.
A program may use at most 128 MiB of HBM per device.

v0:
```python
import jax
import jax.numpy as jnp
from jax import lax
from jax.sharding import PartitionSpec as P


def body(ginv, ufactor, dinv, tile_map, counts, assign):
    highest = lax.Precision.HIGHEST
    rows = ginv.shape[0]
    tiles = ginv.shape[1] // rows
    fronts = ufactor.shape[0]
    width = ufactor.shape[2]
    k_tiles = tile_map.shape[1]
    sep_rows = k_tiles * rows
    mine = lax.axis_index("cube")
    col_me = lax.axis_index("col")
    slots = jnp.arange(fronts, dtype=jnp.int32)
    pick = (assign[:, None] == slots[None, :]).astype(jnp.float32)
    u_local = jnp.einsum("fs,src->frc", pick, ufactor, precision=highest)
    d_local = jnp.dot(pick, dinv, precision=highest)
    live_rows = (jnp.arange(sep_rows, dtype=jnp.int32)[None, :] < counts[:, None]).astype(
        jnp.float32
    )
    live_tiles = live_rows.reshape(fronts, k_tiles, rows)
    is_own = (tile_map == mine).astype(jnp.float32)
    own = jnp.sum(is_own, axis=1)
    own_mask = jnp.einsum("fj,fjr->fr", is_own, live_tiles)
    own_row = jnp.sum(own_mask, axis=0)
    gtiles = ginv.reshape(rows, tiles, rows)
    gsel = jnp.take(gtiles, tile_map.reshape(-1), axis=1)
    gsel = gsel.reshape(rows, fronts, k_tiles, rows) * live_tiles[None, :, :, :]
    gsel = gsel.reshape(rows, fronts, sep_rows)
    gathered = lax.all_gather(u_local, "cube", axis=1, tiled=True)
    v_all = jnp.einsum("rfk,fkc->frc", gsel, gathered, precision=highest)
    blocks = gathered.reshape(fronts, k_tiles, rows, width)
    u_own = jnp.einsum("fj,fjrc->rc", is_own, blocks, precision=highest)
    u_own = u_own * own_row[:, None]
    v_own = jnp.einsum("f,frc->rc", own, v_all, precision=highest)
    u_wide = lax.all_gather(u_own, "col", axis=1, tiled=True)
    panel = u_wide.shape[1]
    cube_count = lax.axis_size("cube")
    row_share = panel // cube_count
    product = jnp.dot(u_wide.T, v_own, precision=highest)
    sigma = lax.psum_scatter(
        product[:, None, :] * own[None, :, None], "cube", scatter_dimension=0, tiled=True
    )
    row_global = mine * row_share + jnp.arange(row_share, dtype=jnp.int32)
    col_global = col_me * width + jnp.arange(width, dtype=jnp.int32)
    on_diag = (row_global[:, None] == col_global[None, :]).astype(jnp.float32)
    sigma = sigma + on_diag[:, None, :] * d_local[None, :, :]
    diag_piece = jnp.sum(sigma * on_diag[:, None, :], axis=0)
    ff_diag = lax.psum(diag_piece, "cube")
    g_block = lax.dynamic_slice_in_dim(ginv, mine * rows, rows, 1)
    g_diag = jnp.diagonal(g_block)
    resist = own_mask[:, :, None] * (ff_diag[:, None, :] + g_diag[None, :, None] + 2.0 * v_all)
    return (-v_all, resist, sigma)


def solution(mesh):
    in_specs = (P("cube", None), P(None, "cube", "col"), P(None, "col"), P(), P(), P())
    out_specs = (P(None, "cube", "col"), P(None, "cube", "col"), P("cube", None, "col"))
    return jax.shard_map(body, mesh=mesh, in_specs=in_specs, out_specs=out_specs, check_vma=False)
```

profile of v0, /device:TPU:2, one launch (start us, length us, event | category | flops | bytes accessed | tf_op | source)
XLA Modules:
  0.0 676.8 jit_solution(10733291234144268602)
XLA Ops:
  7.2 0.0 copy-start
  7.2 0.0 all-gather.3.cloned.1.call-start
  7.2 0.9 copy-done
  8.1 2.1 fusion.10
  10.2 0.0 all-gather.3.cloned.1.call-update
  10.2 0.0 all-gather.5.cloned.1.call-start
  10.3 0.8 reshape.130
  11.1 0.8 convert_reduce_fusion
  11.9 0.8 fusion.12
  12.7 0.7 compare_and_fusion
  13.4 170.0 %all-gather.3.cloned.1.call-done = f32[2,4096,256]{2,0,1:T(2,128)} async-done(((f32[2,128,256]{2,0,1:T(2,128)}), f32[2,4096,256]{2,0,1:T(2,128)}) %all-gather.3.cloned.1.call-update) | async-done | bytes 8388624 | tf_op jit(solution)/shard_map/all_gather | solution.py:33
  183.4 10.8 %fusion.1 = f32[1,256,256,1]{2,0,3,1:T(1,128)S(1)} fusion(f32[2,16,256,256]{3,0,2,1:T(2,128)} %bitcast.39, pred[2,16,1,1]{1,0,2,3:T(4,128)(4,1)S(1)} %bitcast.47), kind=kOutput, calls=%fused_computation.4 | convolution fusion | flops 25165824 | bytes 8650784 | tf_op jit(solution)/shard_map/fj,fjrc->rc/dot_general | solution.py:36
  194.2 0.8 bitcast_multiply_fusion
  195.0 0.0 all-gather.5.cloned.1.call-update
  195.0 0.2 all-reduce.3.cloned.1.call-start
  195.2 0.1 broadcast_bitcast_fusion
  195.3 9.0 %copy.21 = f32[256,8192]{0,1:T(8,128)} copy(f32[256,8192]{1,0:T(8,128)} %param.6) | data formatting | bytes 16777216 | tf_op args[0]
  204.3 9.0 %copy.22 = f32[256,32,256]{2,0,1:T(8,128)} copy(f32[256,32,256]{0,2,1:T(8,128)} %bitcast.42) | data formatting | bytes 16777216 | tf_op jit(solution)/shard_map/reshape | solution.py:29
  213.3 7.8 %gather_fusion = f32[32,256,256]{2,1,0:T(8,128)} fusion(f32[256,32,256]{2,0,1:T(8,128)} %copy.22, s32[1024]{0:T(1024)S(1)} %pad_clamp_fusion), kind=kCustom, calls=%fused_computation | custom fusion | bytes 16777344 | tf_op jit(solution)/shard_map/jit(_take)/gather | solution.py:30
  221.1 0.0 copy-start.2
  221.1 9.0 %copy.23 = f32[256,32,256]{0,2,1:T(8,128)} copy(f32[256,32,256]{2,0,1:T(8,128)} %bitcast.41) | data formatting | bytes 16777216 | tf_op jit(solution)/shard_map/jit(_take)/gather | solution.py:30
  230.1 0.0 copy-done.2
  230.1 0.1 compare_convert_fusion.1
  230.2 6.9 %fusion = f32[256,2,4096]{0,2,1:T(8,128)S(1)} fusion(f32[2,4096]{1,0:T(2,128)S(1)} %compare_convert_fusion.1, pred[2,4096]{1,0:T(4,128)(4,1)S(1)} %bitcast.44, f32[256,2,4096]{0,2,1:T(8,128)} %bitcast.40), kind=kLoop, calls=%fused_computation.3 | loop fusion | flops 4194304 | bytes 16818176 | tf_op jit(solution)/shard_map/mul | solution.py:31
  237.1 16.7 %fusion.3 = f32[2,256,256]{2,1,0:T(8,128)S(1)} fusion(f32[256,2,4096]{0,2,1:T(8,128)S(1)} %fusion, f32[2,4096,256]{2,0,1:T(2,128)} %all-gather.3.cloned.1.call-done), kind=kOutput, calls=%fused_computation.6 | convolution fusion | flops 6442450944 | bytes 17301504 | tf_op jit(solution)/shard_map/rfk,fkc->frc/dot_general | solution.py:34
  253.8 0.0 copy-start.1
  253.8 2.0 fusion.5
  255.8 0.0 copy-start.5
  255.8 0.0 copy-start.3
  255.9 0.0 copy-start.4
  255.9 0.0 all-gather.5.cloned.1.call-done
  255.9 5.2 fusion.7
  261.1 3.3 broadcast_multiply_fusion
  264.4 0.0 all-reduce.3.cloned.1.call-update
  264.4 1.0 constant_dynamic-slice_fusion
  265.4 2.3 gather_fusion.1
  267.8 0.0 copy-done.5
  267.8 0.6 dynamic-slice
  269.0 0.0 copy-done.3
  269.0 0.0 copy-done.4
  269.1 0.2 fusion.20
  269.2 0.1 compare_convert_fusion
  269.3 320.9 %all-reduce.3.cloned.1.call-done = f32[2048,2,256]{2,1,0:T(2,128)} async-done(((f32[2048,2,256]{2,1,0:T(2,128)}), f32[2048,2,256]{2,1,0:T(2,128)}) %all-reduce.3.cloned.1.call-update) | async-done | bytes 4194320
  590.2 1.6 multiply_reduce_fusion
  591.8 77.4 %psum.7 = f32[2,256]{1,0:T(2,128)S(1)} all-reduce(f32[2,256]{1,0:T(2,128)S(1)} %get-tuple-element.3), channel_id=1, replica_groups=mesh['cube'=32,'col'=8] {'cube'}, use_global_device_ids=true, to_apply=%region_4.5 | all-reduce | flops 512 | bytes 4096 | tf_op jit(solution)/shard_map/psum | solution.py:52
  669.2 1.1 add_multiply_fusion
  670.3 0.0 copy-done.1
  (11 shorter events, 0.1 us)
Async XLA Ops:
  7.2 1.0 copy-start
  7.2 176.2 %all-gather.3.cloned.1.call-start = ((), (), s32[]{:S(2)}) async-start(), calls=%async_computation | async-start | bytes 8650752 | tf_op jit(solution)/shard_map/all_gather | solution.py:33
  10.2 245.7 %all-gather.5.cloned.1.call-start = ((), (), s32[]{:S(2)}) async-start(), calls=%async_computation.1 | async-start | bytes 2359296 | tf_op jit(solution)/shard_map/all_gather | solution.py:39
  195.0 395.2 %all-reduce.3.cloned.1.call-start = ((), (), s32[]{:S(2)}) async-start(), calls=%async_computation.2 | async-start | bytes 8388608
  221.1 9.0 %copy-start.2 = (s32[2]{0:T(128)S(1)}, s32[2]{0:T(128)}, u32[]{:S(2)}) copy-start(s32[2]{0:T(128)} %param.10) | copy-start | bytes 28
  253.8 416.5 %copy-start.1 = (f32[2,128,256]{2,1,0:T(8,128)S(1)}, f32[2,128,256]{2,1,0:T(8,128)}, u32[]{:S(2)}) copy-start(f32[2,128,256]{2,1,0:T(8,128)} %param.7) | copy-start | bytes 786436
  255.8 11.9 %copy-start.5 = (u32[256]{0:T(256)S(1)}, u32[256]{0:T(256)}, u32[]{:S(2)}) copy-start(u32[256]{0:T(256)} %constant.58) | copy-start | bytes 3076
  255.8 13.2 %copy-start.3 = (f32[2,256]{1,0:T(2,128)S(1)}, f32[2,256]{1,0:T(2,128)}, u32[]{:S(2)}) copy-start(f32[2,256]{1,0:T(2,128)} %param.8) | copy-start | bytes 6148
  255.9 13.2 %copy-start.4 = (s32[2]{0:T(128)S(1)}, s32[2]{0:T(128)}, u32[]{:S(2)}) copy-start(s32[2]{0:T(128)} %param.11) | copy-start | bytes 28
Sparse Core Ops, SparseCore 0:
  10.4 172.9 all-gather.2
  195.1 36.6 all-gather.4
  264.5 325.6 all-reduce.2
where the time goes:
time: 682 us; the launch traced here: 677 us
  waiting for transfers between devices  491 us (72%)
  blocking collectives  77.4 us (11%)
  local copies, waits for them, and re-layouts  40.5 us (6%)
  matrix products  37.7 us (6%)
  other arithmetic  15.4 us (2%)
  between operations  14.6 us (2%)
    unnamed x4, waiting for transfers between devices  321 us
    all_gather x1, waiting for transfers between devices, body(): gathered = lax.all_gather(u_local, 'cube', axis=1, tiled=True)  170 us
    psum x1, blocking collectives, body(): ff_diag = lax.psum(diag_piece, 'cube')  77.4 us
    gather x2, local copies, waits for them, and re-layouts, body(): gsel = jnp.take(gtiles, tile_map.reshape(-1), axis=1)  16.8 us
    dot_general x1, matrix products, body(): v_all = jnp.einsum('rfk,fkc->frc', gsel, gathered, precision=highest)  16.7 us
  transfers between devices with their start and end apart: 3, of which 2 were waited for; matrix products, arithmetic and copies ran while one was open for 10% of the time, Pallas kernels for 0%

commit v1 on v0

v1 whole, which is shorter than its diff:
```python
import functools

import jax
import jax.numpy as jnp
from jax import lax
from jax.experimental import pallas as pl
from jax.experimental.pallas import tpu as pltpu
from jax.sharding import PartitionSpec as P

AXES = ("cube", "col")
F32 = jnp.float32
VMEM = pltpu.VMEM
SMEM = pltpu.SMEM


def index_of(x, y, zl, zh, core):
    return ((y * 2 + zl) * 4 + x) * 8 + zh * 2 + core


def table(move):
    pairs = []
    for y in range(4):
        for zl in range(2):
            for x in range(4):
                for zh in range(4):
                    for core in range(2):
                        pairs.append(
                            (index_of(x, y, zl, zh, core), index_of(*move(x, y, zl, zh, core)))
                        )
    return pairs


def send_pq(v, dp, dq):
    def move(x, y, zl, zh, core):
        dx, dy = (dp, dq) if core == 0 else (dq, dp)
        return (x + dx) % 4, (y + dy) % 4, zl, zh, core

    return lax.ppermute(v, AXES, table(move))


def send_pair(v):
    return lax.ppermute(v, AXES, table(lambda x, y, zl, zh, core: (x, y, 1 - zl, zh, core)))


def send_core(v):
    return lax.ppermute(v, AXES, table(lambda x, y, zl, zh, core: (x, y, zl, zh, 1 - core)))


def send_zh(v, d):
    return lax.ppermute(v, AXES, table(lambda x, y, zl, zh, core: (x, y, zl, (zh + d) % 4, core)))


def split(a):
    hi = a.astype(jnp.bfloat16)
    lo = (a - hi.astype(F32)).astype(jnp.bfloat16)
    return hi, lo


def dot3(a, b, dims):
    ah, al = split(a)
    bh, bl = split(b)
    dg = functools.partial(lax.dot_general, dimension_numbers=(dims, ((), ())),
                           preferred_element_type=F32)
    return dg(ah, bh) + (dg(ah, bl) + dg(al, bh))


def v_kernel(first, cb, meta, g00, g01, g10, g11, u0, u1, *refs):
    if first:
        v_out, own_out = refs
    else:
        v_in, own_in, v_out, own_out = refs
    k = pl.program_id(0)

    @pl.when(k == 0)
    def _():
        if first:
            v_out[...] = jnp.zeros_like(v_out)
            own_out[...] = jnp.zeros_like(own_out)
        else:
            v_out[...] = v_in[...]
            own_out[...] = own_in[...]

    rows = lax.broadcasted_iota(jnp.int32, (128, 256), 0)
    gs = ((g00, g01), (g10, g11))
    us = (u0, u1)
    for s in range(2):
        parts = []
        for g in range(2):
            base = ((g * 4 + k) * 2 + s) * 2
            live = meta[base]
            half = meta[base + 1]
            u = jnp.where(rows < live, us[g][0, s], 0.0)
            parts.append(u)

            @pl.when(half >= 0)
            def _():
                own_out[pl.ds(pl.multiple_of(half * 128, 128), 128), :] = u

        uu = jnp.concatenate(parts, axis=0)
        gg = jnp.concatenate([gs[0][s][...], gs[1][s][...]], axis=1)
        v_out[s] += dot3(gg, uu, ((1,), (0,)))


def v_call(ginv, ua, ub, cb, meta, carry):
    def gspec(g, s):
        return pl.BlockSpec((256, 128), lambda k, cb, meta: (0, cb[(g * 4 + k) * 2 + s]))

    uspec = pl.BlockSpec((1, 2, 128, 256), lambda k, cb, meta: (k, 0, 0, 0))
    vspec = pl.BlockSpec((2, 256, 256), lambda k, cb, meta: (0, 0, 0))
    ospec = pl.BlockSpec((256, 256), lambda k, cb, meta: (0, 0))
    first = carry is None
    extra = [] if first else [vspec, ospec]
    aliases = {} if first else {8: 0, 9: 1}
    return pl.pallas_call(
        functools.partial(v_kernel, first),
        grid_spec=pltpu.PrefetchScalarGridSpec(
            num_scalar_prefetch=2,
            grid=(4,),
            in_specs=[gspec(0, 0), gspec(0, 1), gspec(1, 0), gspec(1, 1), uspec, uspec] + extra,
            out_specs=[vspec, ospec],
        ),
        out_shape=[jax.ShapeDtypeStruct((2, 256, 256), F32), jax.ShapeDtypeStruct((256, 256), F32)],
        input_output_aliases=aliases,
        compiler_params=pltpu.CompilerParams(vmem_limit_bytes=24 * 2**20),
        cost_estimate=pl.CostEstimate(flops=3 * 2 * 256 * 2048 * 256, bytes_accessed=6 * 2**20,
                                      transcendentals=0),
        name="v_part",
    )(cb, meta, ginv, ginv, ginv, ginv, ua, ub, *(() if first else carry))


def prod_kernel(pos, v, own, c1, c2a, c2b, c3, o_own, o1, o2a, o2b, o3, m0, m1, m2, m3, whole):
    x, y, zh, core = pos[0], pos[1], pos[2], pos[3]
    vv = v[0]
    vh, vl = split(vv)

    def dg(a, b):
        return lax.dot_general(a, b, (((0,), (0,)), ((), ())), preferred_element_type=F32)

    mine = own[...]
    for k in range(4):
        for side in range(2):
            if k == 2:
                u = jnp.concatenate([(c2a, o2a)[side][...], (c2b, o2b)[side][...]], axis=0)
            else:
                u = ((own, o_own), (c1, o1), None, (c3, o3))[k][side][...]
            uh, ul = split(u)
            block = lax.rem(zh + 4 - k, 4) * 2 + (core if side == 0 else 1 - core)
            whole[block] = dg(uh, vh) + (dg(uh, vl) + dg(ul, vh))
    diag = jnp.sum(mine * vv, axis=0, keepdims=True)
    for k, m in enumerate((m0, m1, m2, m3)):
        for i in range(8):
            b = jnp.where(core == 0, i, 2 * lax.rem(y + k, 4) + i // 4)
            sub = jnp.where(core == 0, lax.rem(x + k, 4), i % 4)
            m[i * 64:(i + 1) * 64, :] = whole[b, pl.ds(pl.multiple_of(sub * 64, 64), 64), :]
        m[512:520, :] = jnp.broadcast_to(diag, (8, 256))


def prod_call(pos, v, pieces):
    full = lambda shape: pl.BlockSpec(shape, lambda i, pos: (0,) * len(shape))
    vspec = pl.BlockSpec((1, 256, 256), lambda i, pos: (pos[4], 0, 0))
    big, small, msg = full((256, 256)), full((128, 256)), full((520, 256))
    ins = [big, big, small, small, big]
    return pl.pallas_call(
        prod_kernel,
        grid_spec=pltpu.PrefetchScalarGridSpec(
            num_scalar_prefetch=1, grid=(1,),
            in_specs=[vspec] + ins + ins, out_specs=[msg] * 4,
            scratch_shapes=[VMEM((8, 256, 256), F32)],
        ),
        out_shape=[jax.ShapeDtypeStruct((520, 256), F32)] * 4,
        compiler_params=pltpu.CompilerParams(vmem_limit_bytes=24 * 2**20),
        name="product",
    )(pos, v, *pieces)


def sum1_kernel(pos, r0, r1, r2, r3, m0, m1, m2, m3):
    x, y, zl, core = pos[0], pos[1], pos[2], pos[3]
    rs = (r0, r1, r2, r3)

    def both(rows):
        vals = [r[rows, :] for r in rs]
        out = []
        for s in range(2):
            total = None
            for k in range(4):
                term = jnp.where(pos[4 + k] == s, vals[k], 0.0)
                total = term if total is None else total + term
            out.append(total)
        return out

    d = both(pl.ds(512, 8))
    for k, m in enumerate((m0, m1, m2, m3)):
        for zrel in range(2):
            zb = lax.rem(zl + zrel, 2)
            at = jnp.where(core == 0, 2 * lax.rem(y + k, 4) + zb, zb * 4 + lax.rem(x + k, 4))
            pair = both(pl.ds(pl.multiple_of(at * 64, 64), 64))
            for s in range(2):
                m[(zrel * 2 + s) * 64:(zrel * 2 + s + 1) * 64, :] = pair[s]
        m[256:264, :] = d[0]
        m[264:272, :] = d[1]


def sum1_call(pos, rs):
    spec = pl.BlockSpec(memory_space=VMEM)
    return pl.pallas_call(
        sum1_kernel,
        in_specs=[pl.BlockSpec(memory_space=SMEM)] + [spec] * 4,
        out_specs=[spec] * 4,
        out_shape=[jax.ShapeDtypeStruct((272, 256), F32)] * 4,
        compiler_params=pltpu.CompilerParams(vmem_limit_bytes=16 * 2**20),
        name="sum_first",
    )(pos, *rs)


def sum2_kernel(r0, r1, r2, r3, keep, away):
    for rows, o, to in ((0, keep, 0), (128, away, 0)):
        o[to:to + 128, :] = (r0[rows:rows + 128, :] + r1[rows:rows + 128, :]) + (
            r2[rows:rows + 128, :] + r3[rows:rows + 128, :])
    d = (r0[256:272, :] + r1[256:272, :]) + (r2[256:272, :] + r3[256:272, :])
    keep[128:144, :] = d
    away[128:144, :] = d


def sum2_call(rs):
    spec = pl.BlockSpec(memory_space=VMEM)
    return pl.pallas_call(
        sum2_kernel,
        in_specs=[spec] * 4,
        out_specs=[spec] * 2,
        out_shape=[jax.ShapeDtypeStruct((144, 256), F32)] * 2,
        compiler_params=pltpu.CompilerParams(vmem_limit_bytes=16 * 2**20),
        name="sum_second",
    )(*rs)


def body(ginv, ufactor, dinv, tile_map, counts, assign):
    me = lax.axis_index("cube")
    col = lax.axis_index("col")
    x, zl, y = lax.rem(me, 4), lax.rem(me // 4, 2), me // 8
    zh, core = col // 2, lax.rem(col, 2)

    flip = assign[0] != 0
    tile_s = jnp.where(flip, tile_map[::-1], tile_map)
    counts_s = jnp.where(flip, counts[::-1], counts)

    step = jnp.arange(4, dtype=jnp.int32)
    plane = jnp.arange(2, dtype=jnp.int32)
    dp, dq = step[None, None, :], step[None, :, None]
    dx = jnp.where(core == 0, dp, dq)
    dy = jnp.where(core == 0, dq, dp)
    src = (((y + 4 - dy) % 4) * 2 + (zl + plane[:, None, None]) % 2) * 4 + (x + 4 - dx) % 4
    src = src[..., None]
    s_ids = plane[None, None, None, :]
    slot_tile = tile_s.reshape(-1)[s_ids * 16 + src // 2]
    cb = (slot_tile * 2 + src % 2).astype(jnp.int32)
    live = jnp.clip(counts_s[s_ids] - src * 128, 0, 128).astype(jnp.int32)
    half = jnp.where(slot_tile == me, src % 2, -1).astype(jnp.int32)
    meta = jnp.stack([live, half], axis=-1)

    in_one = jnp.any(tile_s[1][:, None] == jnp.arange(32, dtype=jnp.int32)[None, :], axis=0)
    front_of = in_one.astype(jnp.int32)
    s_own = front_of[me]

    a0 = ufactor
    b0 = send_pair(a0)
    a = [a0, send_pq(a0, 1, 0), send_pq(a0, 2, 0), send_pq(a0, -1, 0)]
    ga = jnp.stack(a)
    ga1 = send_pq(ga, 0, 1)
    ga3 = send_pq(ga, 0, -1)
    b = [b0, send_pq(b0, 1, 0), send_pq(b0, 2, 0), send_pq(b0, -1, 0)]
    gb = jnp.stack(b)
    gb1 = send_pq(gb, 0, 1)
    gb3 = send_pq(gb, 0, -1)
    ga2 = send_pq(ga1, 0, 1)
    gb2 = send_pq(gb3, 0, -1)

    def args(first, second):
        pick = lambda t: jnp.concatenate([t[first].reshape(-1), t[second].reshape(-1)])
        return pick(cb), pick(meta)

    carry = v_call(ginv, ga, gb, *args((0, 0), (1, 0)), None)
    carry = v_call(ginv, ga1, ga3, *args((0, 1), (0, 3)), carry)
    carry = v_call(ginv, gb1, gb3, *args((1, 1), (1, 3)), carry)
    v, own = v_call(ginv, ga2, gb2, *args((0, 2), (1, 2)), carry)

    c1 = send_zh(own, 1)
    c3 = send_zh(own, -1)
    c2a = send_zh(c1[:128], 1)
    c2b = send_zh(c3[128:], -1)
    near = [own, c1, c2a, c2b, c3]
    far = [send_core(t) for t in near]

    pos = jnp.stack([x, y, zh, core, s_own]).astype(jnp.int32)
    m = prod_call(pos, v, near + far)
    r = [m[0], send_pq(m[1], 1, 0), send_pq(m[2], 2, 0), send_pq(m[3], -1, 0)]
    from_p = jnp.where(core == 0, (y * 2 + zl) * 4 + (x + 4 - step) % 4,
                       (((y + 4 - step) % 4) * 2 + zl) * 4 + x)
    pos1 = jnp.concatenate([jnp.stack([x, y, zl, core]), front_of[from_p]]).astype(jnp.int32)
    m = sum1_call(pos1, r)
    r = [m[0], send_pq(m[1], 0, 1), send_pq(m[2], 0, 2), send_pq(m[3], 0, -1)]
    keep, away = sum2_call(r)
    total = keep + send_pair(away)

    front_order = lambda t: jnp.where(flip, t[::-1], t)
    d_local = front_order(dinv)
    sigma = front_order(total[:128].reshape(2, 64, 256)).transpose(1, 0, 2)
    rows = me * 64 + jnp.arange(64, dtype=jnp.int32)
    cols = col * 256 + jnp.arange(256, dtype=jnp.int32)
    on_diag = rows[:, None] == cols[None, :]
    sigma = sigma + jnp.where(on_diag[:, None, :], d_local[None], 0.0)
    diag = front_order(jnp.stack([total[128], total[136]])) + d_local

    block = lax.dynamic_slice_in_dim(ginv, me * 256, 256, 1)
    eye = jnp.arange(256)[:, None] == jnp.arange(256)[None, :]
    g_diag = jnp.sum(jnp.where(eye, block, 0.0), axis=1)
    slots = jnp.arange(16, dtype=jnp.int32)
    at = jnp.sum(jnp.where(tile_map == me, slots[None, :] + 1, 0), axis=1)
    row = (at[:, None] - 1) * 256 + jnp.arange(256, dtype=jnp.int32)[None, :]
    live_row = (at[:, None] > 0) & (row < counts[:, None])
    vf = front_order(v)
    cross = -vf
    resist = jnp.where(live_row[:, :, None], diag[:, None, :] + g_diag[None, :, None] + 2.0 * vf, 0.0)
    return cross, resist, sigma


def solution(mesh):
    in_specs = (P("cube", None), P(None, "cube", "col"), P(None, "col"), P(), P(), P())
    out_specs = (P(None, "cube", "col"), P(None, "cube", "col"), P("cube", None, "col"))
    return jax.shard_map(body, mesh=mesh, in_specs=in_specs, out_specs=out_specs, check_vma=False)
```

time: 682 us -> 144 us (0.21)
  waiting for transfers between devices: 491 us -> 61.5 us
  blocking collectives: 77.4 us -> 0 us
  starting transfers between devices: 0.3 us -> 40.1 us
  matrix products: 37.7 us -> 0 us
  local copies, waits for them, and re-layouts: 40.5 us -> 11.7 us
  Pallas kernels: 0 us -> 23 us
  between operations: 14.6 us -> 1.65 us
  other arithmetic: 15.4 us -> 5.99 us
    unnamed x4 -> x0, waiting for transfers between devices: 321 us -> none
    all_gather x2 -> x0, waiting for transfers between devices: 170 us -> none  [the longest x1 170 us: body(): gathered = lax.all_gather(u_local, 'cube', axis=1, tiled=True)]
    psum x1 -> x0, blocking collectives: 77.4 us -> none  [body(): ff_diag = lax.psum(diag_piece, 'cube')]
    ppermute x0 -> x29, waiting for transfers between devices: none -> 61.5 us  [the longest x18 39.5 us: send_pq(): return lax.ppermute(v, AXES, table(move))]
    ppermute x0 -> x29, starting transfers between devices: none -> 40.1 us  [the longest x18 27.9 us: send_pq(): return lax.ppermute(v, AXES, table(move))]
    dot_general x7 -> x0, matrix products: 37.7 us -> none  [the longest x1 16.7 us: body(): v_all = jnp.einsum('rfk,fkc->frc', gsel, gathered, precision=highest)]
    pallas_call x0 -> x7, Pallas kernels: none -> 23 us  [the longest x4 20.4 us: v_call(): pl.pallas_call(functools.partial(v_kernel, first), grid_spec=pltpu.Prefet...]
    gather x3, local copies, waits for them, and re-layouts: 19.1 us -> 2.06 us  [the longest x1 0.78 us: body(): slot_tile = tile_s.reshape(-1)[s_ids * 16 + src // 2]]
  transfers between devices with their start and end apart: 3 -> 29, of which waited for: 2 -> 14; matrix products, arithmetic and copies ran while one was open for 10% -> 8% of each run, Pallas kernels for 0% -> 10%
where the time goes in v1:
time: 144 us
  waiting for transfers between devices  61.5 us (43%)
  starting transfers between devices  40.1 us (28%)
  Pallas kernels  23 us (16%)
  local copies, waits for them, and re-layouts  11.7 us (8%)
  other arithmetic  5.99 us (4%)
  between operations  1.65 us (1%)
    ppermute x18, waiting for transfers between devices, send_pq(): return lax.ppermute(v, AXES, table(move))  39.5 us
    ppermute x18, starting transfers between devices, send_pq(): return lax.ppermute(v, AXES, table(move))  27.9 us
    pallas_call x4, Pallas kernels, v_call(): pl.pallas_call(functools.partial(v_kernel, first), grid_spec=pltpu.Prefet...  20.4 us
    ppermute x4, waiting for transfers between devices, send_zh(): lax.ppermute(v, AXES, table(lambda x, y, zl, zh, core: (x, y, zl, (zh + d...  16.3 us
    ppermute x4, starting transfers between devices, send_zh(): lax.ppermute(v, AXES, table(lambda x, y, zl, zh, core: (x, y, zl, (zh + d...  10.8 us
    ppermute x2, waiting for transfers between devices, send_pair(): lax.ppermute(v, AXES, table(lambda x, y, zl, zh, core: (x, y, 1 - zl, zh,...  5.74 us
    unnamed x8, local copies, waits for them, and re-layouts  3.41 us
  transfers between devices with their start and end apart: 29, of which 14 were waited for; matrix products, arithmetic and copies ran while one was open for 8% of the time, Pallas kernels for 10%

profile of v1, /device:TPU:2, one launch (start us, length us, event | category | flops | bytes accessed | tf_op | source)
XLA Modules:
  0.0 144.0 jit_solution(705936269803179449)
XLA Ops:
  0.6 2.2 %collective-permute-start.1 = (f32[2,128,256]{2,1,0:T(8,128)}, f32[2,128,256]{2,1,0:T(8,128)S(1)}, u32[]{:S(2)}, u32[]{:S(2)}) collective-permute-start(f32[2,128,256]{2,1,0:T(8,128)} %param.7), channel_id=1, source_target_pairs={{0,16},{1,129},{2,18},{3,131},{4,20},{5,133},{6,22},{7,135},{8,24}... | collective-permute-start | bytes 786440 | tf_op jit(solution)/shard_map/ppermute | solution.py:38
  2.8 1.6 %collective-permute-start = (f32[2,128,256]{2,1,0:T(8,128)}, f32[2,128,256]{2,1,0:T(8,128)S(1)}, u32[]{:S(2)}, u32[]{:S(2)}) collective-permute-start(f32[2,128,256]{2,1,0:T(8,128)} %param.7), channel_id=1, source_target_pairs={{0,8},{1,65},{2,10},{3,67},{4,12},{5,69},{6,14},{7,71},{8,16},{9,7... | collective-permute-start | bytes 786440 | tf_op jit(solution)/shard_map/ppermute | solution.py:38
  4.5 0.3 collective-permute-start.5
  4.8 2.0 %collective-permute-start.2 = (f32[2,128,256]{2,1,0:T(8,128)}, f32[2,128,256]{2,1,0:T(8,128)S(1)}, u32[]{:S(2)}, u32[]{:S(2)}) collective-permute-start(f32[2,128,256]{2,1,0:T(8,128)} %param.7), channel_id=1, source_target_pairs={{0,24},{1,193},{2,26},{3,195},{4,28},{5,197},{6,30},{7,199},{8,0},... | collective-permute-start | bytes 786440 | tf_op jit(solution)/shard_map/ppermute | solution.py:38
  6.8 0.7 rev.19
  7.5 0.7 rev.18
  8.4 0.1 reshape.407
  9.2 0.7 broadcast_select_fusion.3
  9.9 0.8 fusion.15
  10.8 0.8 gather_fusion
  11.5 1.0 collective-permute-done.5
  12.5 1.8 %collective-permute-start.8 = (f32[2,128,256]{2,1,0:T(8,128)S(1)}, f32[2,128,256]{2,1,0:T(8,128)S(1)}, u32[]{:S(2)}, u32[]{:S(2)}) collective-permute-start(f32[2,128,256]{2,1,0:T(8,128)S(1)} %collective-permute-done.5), channel_id=1, source_target_pairs={{0,24},{1,193},{2,26},{3,195},{4,28},{5,197},{6,30},{7,199},{8,0},... | collective-permute-start | bytes 786440 | tf_op jit(solution)/shard_map/ppermute | solution.py:38
  14.3 1.2 collective-permute-start.7
  15.4 1.8 %collective-permute-start.6 = (f32[2,128,256]{2,1,0:T(8,128)S(1)}, f32[2,128,256]{2,1,0:T(8,128)S(1)}, u32[]{:S(2)}, u32[]{:S(2)}) collective-permute-start(f32[2,128,256]{2,1,0:T(8,128)S(1)} %collective-permute-done.5), channel_id=1, source_target_pairs={{0,8},{1,65},{2,10},{3,67},{4,12},{5,69},{6,14},{7,71},{8,16},{9,7... | collective-permute-start | bytes 786440 | tf_op jit(solution)/shard_map/ppermute | solution.py:38
  17.4 0.4 collective-permute-start.3
  17.7 1.1 collective-permute-done.8
  18.9 3.7 %collective-permute-done.7 = f32[2,128,256]{2,1,0:T(8,128)S(1)} collective-permute-done((f32[2,128,256]{2,1,0:T(8,128)S(1)}, f32[2,128,256]{2,1,0:T(8,128)S(1)}, u32[]{:S(2)}, u32[]{:S(2)}) %collective-permute-start.7) | collective-permute-done | bytes 262176 | tf_op jit(solution)/shard_map/ppermute | solution.py:38
  22.6 6.8 %collective-permute-done.6 = f32[2,128,256]{2,1,0:T(8,128)S(1)} collective-permute-done((f32[2,128,256]{2,1,0:T(8,128)S(1)}, f32[2,128,256]{2,1,0:T(8,128)S(1)}, u32[]{:S(2)}, u32[]{:S(2)}) %collective-permute-start.6) | collective-permute-done | bytes 262176 | tf_op jit(solution)/shard_map/ppermute | solution.py:38
  29.5 2.6 %collective-permute-start.9 = (f32[4,2,128,256]{3,2,1,0:T(8,128)S(1)}, f32[4,2,128,256]{3,2,1,0:T(8,128)}, u32[]{:S(2)}, u32[]{:S(2)}) collective-permute-start(f32[4,2,128,256]{3,2,1,0:T(8,128)S(1)} %pad_maximum_fusion.1.u1), channel_id=1, source_target_pairs={{0,192},{1,25},{2,194},{3,27},{4,196},{5,29},{6,198},{7,31},{8,200... | collective-permute-start | bytes 3145736 | tf_op jit(solution)/shard_map/ppermute | solution.py:38
  32.2 0.1 reshape.432
  32.3 0.6 gather_fusion.1
  33.3 0.1 copy.35
  33.5 0.1 copy.36
  33.7 2.0 %collective-permute-start.11 = (f32[4,2,128,256]{3,2,1,0:T(8,128)S(1)}, f32[4,2,128,256]{3,2,1,0:T(8,128)}, u32[]{:S(2)}, u32[]{:S(2)}) collective-permute-start(f32[4,2,128,256]{3,2,1,0:T(8,128)S(1)} %pad_maximum_fusion.1.u1), channel_id=1, source_target_pairs={{0,64},{1,9},{2,66},{3,11},{4,68},{5,13},{6,70},{7,15},{8,72},{9,1... | collective-permute-start | bytes 3145736 | tf_op jit(solution)/shard_map/ppermute | solution.py:38
  35.8 8.6 %collective-permute-done.9.u1 = f32[4,2,128,256]{3,2,1,0:T(8,128)} collective-permute-done((f32[4,2,128,256]{3,2,1,0:T(8,128)S(1)}, f32[4,2,128,256]{3,2,1,0:T(8,128)}, u32[]{:S(2)}, u32[]{:S(2)}) %collective-permute-start.9) | collective-permute-done | bytes 1048608 | tf_op jit(solution)/shard_map/ppermute | solution.py:38
  44.4 3.8 %collective-permute-start.10 = (f32[4,2,128,256]{3,2,1,0:T(8,128)}, f32[4,2,128,256]{3,2,1,0:T(8,128)}, u32[]{:S(2)}, u32[]{:S(2)}) collective-permute-start(f32[4,2,128,256]{3,2,1,0:T(8,128)} %collective-permute-done.9.u1), channel_id=1, source_target_pairs={{0,192},{1,25},{2,194},{3,27},{4,196},{5,29},{6,198},{7,31},{8,200... | collective-permute-start | bytes 3145736 | tf_op jit(solution)/shard_map/ppermute | solution.py:38
  48.3 0.1 copy.41
  48.5 0.1 copy.37
  48.7 0.1 copy.38
  48.9 0.1 copy.39
  49.1 0.1 copy.40
  49.3 0.1 copy.42
  50.7 3.4 %copy-done = f32[256,8192]{1,0:T(8,128)S(1)} copy-done((f32[256,8192]{1,0:T(8,128)S(1)}, f32[256,8192]{1,0:T(8,128)}, u32[]{:S(2)}) %copy-start) | copy-done | bytes 8388632
  54.1 4.2 %v_part.4 = (f32[2,256,256]{2,1,0:T(8,128)S(1)}, f32[256,256]{1,0:T(8,128)S(1)}) custom-call(s32[16]{0:T(128)S(1)} %pad_add_fusion.7.cb, s32[32]{0:T(128)S(1)} %pad_add_fusion.8.meta, f32[256,8192]{1,0:T(8,128)S(1)} %copy-done, f32[256,8192]{1,0:T(8,128)S(1)} %copy-done, f32[256,8192]{1,0:T(8,128)S(1)} %copy-done, f32[256,8192]{1,0:T(8,128)S(1)} %copy-done, ...), custom_call_target="tpu_custom_call" | custom-call | flops 805306368 | bytes 6291456 | tf_op jit(solution)/shard_map/v_part/pallas_call | solution.py:114
  58.3 5.4 %v_part.5 = (f32[2,256,256]{2,1,0:T(8,128)S(1)}, f32[256,256]{1,0:T(8,128)S(1)}) custom-call(s32[16]{0:T(128)S(1)} %pad_add_fusion.5.cb, s32[32]{0:T(128)S(1)} %pad_add_fusion.6.meta, f32[256,8192]{1,0:T(8,128)S(1)} %copy-done, f32[256,8192]{1,0:T(8,128)S(1)} %copy-done, f32[256,8192]{1,0:T(8,128)S(1)} %copy-done, ...), custom_call_target="tpu_custom_call", output_to_operand_aliasing={{0}: (8, {}), {1}: (9, {})} | custom-call | flops 805306368 | bytes 6291456 | tf_op jit(solution)/shard_map/v_part/pallas_call | solution.py:114
  63.7 5.4 %v_part.6 = (f32[2,256,256]{2,1,0:T(8,128)S(1)}, f32[256,256]{1,0:T(8,128)S(1)}) custom-call(s32[16]{0:T(128)S(1)} %pad_add_fusion.3.cb, s32[32]{0:T(128)S(1)} %pad_add_fusion.4.meta, f32[256,8192]{1,0:T(8,128)S(1)} %copy-done, f32[256,8192]{1,0:T(8,128)S(1)} %copy-done, f32[256,8192]{1,0:T(8,128)S(1)} %copy-done, ...), custom_call_target="tpu_custom_call", output_to_operand_aliasing={{0}: (8, {}), {1}: (9, {})} | custom-call | flops 805306368 | bytes 6291456 | tf_op jit(solution)/shard_map/v_part/pallas_call | solution.py:114
  69.1 5.4 %v_part.7 = (f32[2,256,256]{2,1,0:T(8,128)S(1)}, f32[256,256]{1,0:T(8,128)S(1)}) custom-call(s32[16]{0:T(128)S(1)} %pad_add_fusion.1.cb, s32[32]{0:T(128)S(1)} %pad_add_fusion.2.meta, f32[256,8192]{1,0:T(8,128)S(1)} %copy-done, f32[256,8192]{1,0:T(8,128)S(1)} %copy-done, f32[256,8192]{1,0:T(8,128)S(1)} %copy-done, ...), custom_call_target="tpu_custom_call", output_to_operand_aliasing={{0}: (8, {}), {1}: (9, {})} | custom-call | flops 805306368 | bytes 6291456 | tf_op jit(solution)/shard_map/v_part/pallas_call | solution.py:114
  74.5 6.1 %collective-permute-start.15 = (f32[256,256]{1,0:T(8,128)S(1)}, f32[256,256]{1,0:T(8,128)S(1)}, u32[]{:S(2)}, u32[]{:S(2)}) collective-permute-start(f32[256,256]{1,0:T(8,128)S(1)} %get-tuple-element.28.own), channel_id=1, source_target_pairs={{0,6},{1,7},{2,0},{3,1},{4,2},{5,3},{6,4},{7,5},{8,14},{9,15},{10,... | collective-permute-start | bytes 786440 | tf_op jit(solution)/shard_map/ppermute | solution.py:50
  80.6 9.2 %collective-permute-done.15.c3 = f32[256,256]{1,0:T(8,128)S(1)} collective-permute-done((f32[256,256]{1,0:T(8,128)S(1)}, f32[256,256]{1,0:T(8,128)S(1)}, u32[]{:S(2)}, u32[]{:S(2)}) %collective-permute-start.15) | collective-permute-done | bytes 262176 | tf_op jit(solution)/shard_map/ppermute | solution.py:50
  89.9 4.7 %collective-permute-start.16 = (f32[128,256]{1,0:T(8,128)S(1)}, f32[128,256]{1,0:T(8,128)S(1)}, u32[]{:S(2)}, u32[]{:S(2)}) collective-permute-start(f32[128,256]{1,0:T(8,128)S(1)} %slice.121), channel_id=1, source_target_pairs={{0,6},{1,7},{2,0},{3,1},{4,2},{5,3},{6,4},{7,5},{8,14},{9,15},{10,... | collective-permute-start | bytes 393224 | tf_op jit(solution)/shard_map/ppermute | solution.py:50
  94.8 0.5 collective-permute-start.21
  95.5 1.9 %collective-permute-done.16.c2b = f32[128,256]{1,0:T(8,128)S(1)} collective-permute-done((f32[128,256]{1,0:T(8,128)S(1)}, f32[128,256]{1,0:T(8,128)S(1)}, u32[]{:S(2)}, u32[]{:S(2)}) %collective-permute-start.16) | collective-permute-done | bytes 131104 | tf_op jit(solution)/shard_map/ppermute | solution.py:50
  97.4 5.1 %collective-permute-done.14.c2a = f32[128,256]{1,0:T(8,128)S(1)} collective-permute-done((f32[128,256]{1,0:T(8,128)S(1)}, f32[128,256]{1,0:T(8,128)S(1)}, u32[]{:S(2)}, u32[]{:S(2)}) %collective-permute-start.14) | collective-permute-done | bytes 131104 | tf_op jit(solution)/shard_map/ppermute | solution.py:50
  102.5 0.6 dynamic_slice.6
  103.2 0.6 gather_fusion.2
  103.8 0.7 stack.75.pos
  104.6 1.8 %product.1 = (f32[520,256]{1,0:T(8,128)S(1)}, f32[520,256]{1,0:T(8,128)S(1)}, f32[520,256]{1,0:T(8,128)S(1)}, f32[520,256]{1,0:T(8,128)S(1)}) custom-call(s32[5]{0:T(128)S(1)} %stack.75.pos, f32[2,256,256]{2,1,0:T(8,128)S(1)} %get-tuple-element.27.v, f32[256,256]{1,0:T(8,128)S(1)} %get-tuple-element.28.own, f32[256,256]{1,0:T(8,128)S(1)} %collective-permute-done.13.c1, ...), custom_call_target="tpu_custom_call" | custom-call | tf_op jit(solution)/shard_map/product/pallas_call | solution.py:163
  106.4 0.7 collective-permute-start.22
  107.1 1.8 %collective-permute-start.23 = (f32[520,256]{1,0:T(8,128)S(1)}, f32[520,256]{1,0:T(8,128)S(1)}, u32[]{:S(2)}, u32[]{:S(2)}) collective-permute-start(f32[520,256]{1,0:T(8,128)S(1)} %get-tuple-element.31), channel_id=1, source_target_pairs={{0,16},{1,129},{2,18},{3,131},{4,20},{5,133},{6,22},{7,135},{8,24}... | collective-permute-start | bytes 1597448 | tf_op jit(solution)/shard_map/ppermute | solution.py:38
  108.9 2.5 %collective-permute-start.24 = (f32[520,256]{1,0:T(8,128)S(1)}, f32[520,256]{1,0:T(8,128)S(1)}, u32[]{:S(2)}, u32[]{:S(2)}) collective-permute-start(f32[520,256]{1,0:T(8,128)S(1)} %get-tuple-element.32), channel_id=1, source_target_pairs={{0,24},{1,193},{2,26},{3,195},{4,28},{5,197},{6,30},{7,199},{8,0},... | collective-permute-start | bytes 1597448 | tf_op jit(solution)/shard_map/ppermute | solution.py:38
  111.4 4.3 %collective-permute-done.22.r1 = f32[520,256]{1,0:T(8,128)S(1)} collective-permute-done((f32[520,256]{1,0:T(8,128)S(1)}, f32[520,256]{1,0:T(8,128)S(1)}, u32[]{:S(2)}, u32[]{:S(2)}) %collective-permute-start.22) | collective-permute-done | bytes 532512 | tf_op jit(solution)/shard_map/ppermute | solution.py:38
  115.7 2.2 %collective-permute-done.23.r2 = f32[520,256]{1,0:T(8,128)S(1)} collective-permute-done((f32[520,256]{1,0:T(8,128)S(1)}, f32[520,256]{1,0:T(8,128)S(1)}, u32[]{:S(2)}, u32[]{:S(2)}) %collective-permute-start.23) | collective-permute-done | bytes 532512 | tf_op jit(solution)/shard_map/ppermute | solution.py:38
  117.9 5.6 %collective-permute-done.24.r3 = f32[520,256]{1,0:T(8,128)S(1)} collective-permute-done((f32[520,256]{1,0:T(8,128)S(1)}, f32[520,256]{1,0:T(8,128)S(1)}, u32[]{:S(2)}, u32[]{:S(2)}) %collective-permute-start.24) | collective-permute-done | bytes 532512 | tf_op jit(solution)/shard_map/ppermute | solution.py:38
  123.5 0.8 sum_first.1
  124.4 2.9 %collective-permute-start.26 = (f32[272,256]{1,0:T(8,128)S(1)}, f32[272,256]{1,0:T(8,128)S(1)}, u32[]{:S(2)}, u32[]{:S(2)}) collective-permute-start(f32[272,256]{1,0:T(8,128)S(1)} %get-tuple-element.35), channel_id=1, source_target_pairs={{0,128},{1,17},{2,130},{3,19},{4,132},{5,21},{6,134},{7,23},{8,136... | collective-permute-start | bytes 835592 | tf_op jit(solution)/shard_map/ppermute | solution.py:38
  127.3 0.4 collective-permute-start.27
  127.7 1.1 select_reduce_fusion
  128.9 6.3 %collective-permute-done.25.r1 = f32[272,256]{1,0:T(8,128)S(1)} collective-permute-done((f32[272,256]{1,0:T(8,128)S(1)}, f32[272,256]{1,0:T(8,128)S(1)}, u32[]{:S(2)}, u32[]{:S(2)}) %collective-permute-start.25) | collective-permute-done | bytes 278560 | tf_op jit(solution)/shard_map/ppermute | solution.py:38
  135.2 0.9 collective-permute-done.27.r3
  136.1 0.4 collective-permute-start.28
  136.6 4.8 %collective-permute-done.28 = f32[144,256]{1,0:T(8,128)S(1)} collective-permute-done((f32[144,256]{1,0:T(8,128)S(1)}, f32[144,256]{1,0:T(8,128)S(1)}, u32[]{:S(2)}, u32[]{:S(2)}) %collective-permute-start.28) | collective-permute-done | bytes 147488 | tf_op jit(solution)/shard_map/ppermute | solution.py:42
  141.6 0.4 rev.23
  142.0 0.8 bitcast_add_fusion
  142.9 1.1 add_select_fusion
  (98 shorter events, 4.1 us)
Async XLA Ops:
  0.6 14.8 %collective-permute-start.1 = (f32[2,128,256]{2,1,0:T(8,128)}, f32[2,128,256]{2,1,0:T(8,128)S(1)}, u32[]{:S(2)}, u32[]{:S(2)}) collective-permute-start(f32[2,128,256]{2,1,0:T(8,128)} %param.7), channel_id=1, source_target_pairs={{0,16},{1,129},{2,18},{3,131},{4,20},{5,133},{6,22},{7,135},{8,24}... | collective-permute-start | bytes 786440 | tf_op jit(solution)/shard_map/ppermute | solution.py:38
  2.8 14.4 %collective-permute-start = (f32[2,128,256]{2,1,0:T(8,128)}, f32[2,128,256]{2,1,0:T(8,128)S(1)}, u32[]{:S(2)}, u32[]{:S(2)}) collective-permute-start(f32[2,128,256]{2,1,0:T(8,128)} %param.7), channel_id=1, source_target_pairs={{0,8},{1,65},{2,10},{3,67},{4,12},{5,69},{6,14},{7,71},{8,16},{9,7... | collective-permute-start | bytes 786440 | tf_op jit(solution)/shard_map/ppermute | solution.py:38
  4.5 8.0 %collective-permute-start.5 = (f32[2,128,256]{2,1,0:T(8,128)}, f32[2,128,256]{2,1,0:T(8,128)S(1)}, u32[]{:S(2)}, u32[]{:S(2)}) collective-permute-start(f32[2,128,256]{2,1,0:T(8,128)} %param.7), channel_id=1, source_target_pairs={{0,32},{1,33},{2,34},{3,35},{4,36},{5,37},{6,38},{7,39},{8,40},{9,... | collective-permute-start | bytes 786440 | tf_op jit(solution)/shard_map/ppermute | solution.py:42
  4.8 12.5 %collective-permute-start.2 = (f32[2,128,256]{2,1,0:T(8,128)}, f32[2,128,256]{2,1,0:T(8,128)S(1)}, u32[]{:S(2)}, u32[]{:S(2)}) collective-permute-start(f32[2,128,256]{2,1,0:T(8,128)} %param.7), channel_id=1, source_target_pairs={{0,24},{1,193},{2,26},{3,195},{4,28},{5,197},{6,30},{7,199},{8,0},... | collective-permute-start | bytes 786440 | tf_op jit(solution)/shard_map/ppermute | solution.py:38
  10.8 6.5 %copy-start.1 = (f32[2,128,256]{2,1,0:T(8,128)S(1)}, f32[2,128,256]{2,1,0:T(8,128)}, u32[]{:S(2)}) copy-start(f32[2,128,256]{2,1,0:T(8,128)} %param.7) | copy-start | bytes 786436
  12.5 6.4 %collective-permute-start.8 = (f32[2,128,256]{2,1,0:T(8,128)S(1)}, f32[2,128,256]{2,1,0:T(8,128)S(1)}, u32[]{:S(2)}, u32[]{:S(2)}) collective-permute-start(f32[2,128,256]{2,1,0:T(8,128)S(1)} %collective-permute-done.5), channel_id=1, source_target_pairs={{0,24},{1,193},{2,26},{3,195},{4,28},{5,197},{6,30},{7,199},{8,0},... | collective-permute-start | bytes 786440 | tf_op jit(solution)/shard_map/ppermute | solution.py:38
  14.3 8.3 %collective-permute-start.7 = (f32[2,128,256]{2,1,0:T(8,128)S(1)}, f32[2,128,256]{2,1,0:T(8,128)S(1)}, u32[]{:S(2)}, u32[]{:S(2)}) collective-permute-start(f32[2,128,256]{2,1,0:T(8,128)S(1)} %collective-permute-done.5), channel_id=1, source_target_pairs={{0,16},{1,129},{2,18},{3,131},{4,20},{5,133},{6,22},{7,135},{8,24}... | collective-permute-start | bytes 786440 | tf_op jit(solution)/shard_map/ppermute | solution.py:38
  15.4 13.9 %collective-permute-start.6 = (f32[2,128,256]{2,1,0:T(8,128)S(1)}, f32[2,128,256]{2,1,0:T(8,128)S(1)}, u32[]{:S(2)}, u32[]{:S(2)}) collective-permute-start(f32[2,128,256]{2,1,0:T(8,128)S(1)} %collective-permute-done.5), channel_id=1, source_target_pairs={{0,8},{1,65},{2,10},{3,67},{4,12},{5,69},{6,14},{7,71},{8,16},{9,7... | collective-permute-start | bytes 786440 | tf_op jit(solution)/shard_map/ppermute | solution.py:38
  17.4 18.4 %collective-permute-start.3 = (f32[4,2,128,256]{3,2,1,0:T(8,128)S(1)}, f32[4,2,128,256]{3,2,1,0:T(8,128)}, u32[]{:S(2)}, u32[]{:S(2)}) collective-permute-start(f32[4,2,128,256]{3,2,1,0:T(8,128)S(1)} %pad_maximum_fusion.u0), channel_id=1, source_target_pairs={{0,64},{1,9},{2,66},{3,11},{4,68},{5,13},{6,70},{7,15},{8,72},{9,1... | collective-permute-start | bytes 3145736 | tf_op jit(solution)/shard_map/ppermute | solution.py:38
  29.5 15.0 %collective-permute-start.9 = (f32[4,2,128,256]{3,2,1,0:T(8,128)S(1)}, f32[4,2,128,256]{3,2,1,0:T(8,128)}, u32[]{:S(2)}, u32[]{:S(2)}) collective-permute-start(f32[4,2,128,256]{3,2,1,0:T(8,128)S(1)} %pad_maximum_fusion.1.u1), channel_id=1, source_target_pairs={{0,192},{1,25},{2,194},{3,27},{4,196},{5,29},{6,198},{7,31},{8,200... | collective-permute-start | bytes 3145736 | tf_op jit(solution)/shard_map/ppermute | solution.py:38
  33.2 25.0 %collective-permute-start.12 = (f32[4,2,128,256]{3,2,1,0:T(8,128)S(1)}, f32[4,2,128,256]{3,2,1,0:T(8,128)}, u32[]{:S(2)}, u32[]{:S(2)}) collective-permute-start(f32[4,2,128,256]{3,2,1,0:T(8,128)S(1)} %pad_maximum_fusion.u0), channel_id=1, source_target_pairs={{0,192},{1,25},{2,194},{3,27},{4,196},{5,29},{6,198},{7,31},{8,200... | collective-permute-start | bytes 3145736 | tf_op jit(solution)/shard_map/ppermute | solution.py:38
  33.7 30.0 %collective-permute-start.11 = (f32[4,2,128,256]{3,2,1,0:T(8,128)S(1)}, f32[4,2,128,256]{3,2,1,0:T(8,128)}, u32[]{:S(2)}, u32[]{:S(2)}) collective-permute-start(f32[4,2,128,256]{3,2,1,0:T(8,128)S(1)} %pad_maximum_fusion.1.u1), channel_id=1, source_target_pairs={{0,64},{1,9},{2,66},{3,11},{4,68},{5,13},{6,70},{7,15},{8,72},{9,1... | collective-permute-start | bytes 3145736 | tf_op jit(solution)/shard_map/ppermute | solution.py:38
  35.7 33.4 %collective-permute-start.4 = (f32[4,2,128,256]{3,2,1,0:T(8,128)}, f32[4,2,128,256]{3,2,1,0:T(8,128)}, u32[]{:S(2)}, u32[]{:S(2)}) collective-permute-start(f32[4,2,128,256]{3,2,1,0:T(8,128)} %collective-permute-done.3.u0), channel_id=1, source_target_pairs={{0,64},{1,9},{2,66},{3,11},{4,68},{5,13},{6,70},{7,15},{8,72},{9,1... | collective-permute-start | bytes 3145736 | tf_op jit(solution)/shard_map/ppermute | solution.py:38
  44.4 24.7 %collective-permute-start.10 = (f32[4,2,128,256]{3,2,1,0:T(8,128)}, f32[4,2,128,256]{3,2,1,0:T(8,128)}, u32[]{:S(2)}, u32[]{:S(2)}) collective-permute-start(f32[4,2,128,256]{3,2,1,0:T(8,128)} %collective-permute-done.9.u1), channel_id=1, source_target_pairs={{0,192},{1,25},{2,194},{3,27},{4,196},{5,29},{6,198},{7,31},{8,200... | collective-permute-start | bytes 3145736 | tf_op jit(solution)/shard_map/ppermute | solution.py:38
  50.7 3.4 %copy-start = (f32[256,8192]{1,0:T(8,128)S(1)}, f32[256,8192]{1,0:T(8,128)}, u32[]{:S(2)}) copy-start(f32[256,8192]{1,0:T(8,128)} %g11.7) | copy-start | bytes 25165828
  69.1 58.6 %copy-start.2 = (f32[2,256]{1,0:T(2,128)S(1)}, f32[2,256]{1,0:T(2,128)}, u32[]{:S(2)}) copy-start(f32[2,256]{1,0:T(2,128)} %param.8) | copy-start | bytes 6148
  69.1 67.4 %copy-start.3 = (s32[2]{0:T(128)S(1)}, s32[2]{0:T(128)}, u32[]{:S(2)}) copy-start(s32[2]{0:T(128)} %param.10) | copy-start | bytes 28
  74.5 15.3 %collective-permute-start.15 = (f32[256,256]{1,0:T(8,128)S(1)}, f32[256,256]{1,0:T(8,128)S(1)}, u32[]{:S(2)}, u32[]{:S(2)}) collective-permute-start(f32[256,256]{1,0:T(8,128)S(1)} %get-tuple-element.28.own), channel_id=1, source_target_pairs={{0,6},{1,7},{2,0},{3,1},{4,2},{5,3},{6,4},{7,5},{8,14},{9,15},{10,... | collective-permute-start | bytes 786440 | tf_op jit(solution)/shard_map/ppermute | solution.py:50
  80.6 13.9 %collective-permute-start.13 = (f32[256,256]{1,0:T(8,128)S(1)}, f32[256,256]{1,0:T(8,128)S(1)}, u32[]{:S(2)}, u32[]{:S(2)}) collective-permute-start(f32[256,256]{1,0:T(8,128)S(1)} %get-tuple-element.28.own), channel_id=1, source_target_pairs={{0,2},{1,3},{2,4},{3,5},{4,6},{5,7},{6,0},{7,1},{8,10},{9,11},{10,... | collective-permute-start | bytes 786440 | tf_op jit(solution)/shard_map/ppermute | solution.py:50
  89.9 7.5 %collective-permute-start.16 = (f32[128,256]{1,0:T(8,128)S(1)}, f32[128,256]{1,0:T(8,128)S(1)}, u32[]{:S(2)}, u32[]{:S(2)}) collective-permute-start(f32[128,256]{1,0:T(8,128)S(1)} %slice.121), channel_id=1, source_target_pairs={{0,6},{1,7},{2,0},{3,1},{4,2},{5,3},{6,4},{7,5},{8,14},{9,15},{10,... | collective-permute-start | bytes 393224 | tf_op jit(solution)/shard_map/ppermute | solution.py:50
  94.6 7.9 %collective-permute-start.14 = (f32[128,256]{1,0:T(8,128)S(1)}, f32[128,256]{1,0:T(8,128)S(1)}, u32[]{:S(2)}, u32[]{:S(2)}) collective-permute-start(f32[128,256]{1,0:T(8,128)S(1)} %slice.120), channel_id=1, source_target_pairs={{0,2},{1,3},{2,4},{3,5},{4,6},{5,7},{6,0},{7,1},{8,10},{9,11},{10,... | collective-permute-start | bytes 393224 | tf_op jit(solution)/shard_map/ppermute | solution.py:50
  94.7 9.9 %collective-permute-start.17 = (f32[256,256]{1,0:T(8,128)S(1)}, f32[256,256]{1,0:T(8,128)S(1)}, u32[]{:S(2)}, u32[]{:S(2)}) collective-permute-start(f32[256,256]{1,0:T(8,128)S(1)} %get-tuple-element.28.own), channel_id=1, source_target_pairs={{0,1},{1,0},{2,3},{3,2},{4,5},{5,4},{6,7},{7,6},{8,9},{9,8},{10,11... | collective-permute-start | bytes 786440 | tf_op jit(solution)/shard_map/ppermute | solution.py:46
  94.8 9.8 %collective-permute-start.21 = (f32[256,256]{1,0:T(8,128)S(1)}, f32[256,256]{1,0:T(8,128)S(1)}, u32[]{:S(2)}, u32[]{:S(2)}) collective-permute-start(f32[256,256]{1,0:T(8,128)S(1)} %collective-permute-done.15.c3), channel_id=1, source_target_pairs={{0,1},{1,0},{2,3},{3,2},{4,5},{5,4},{6,7},{7,6},{8,9},{9,8},{10,11... | collective-permute-start | bytes 786440 | tf_op jit(solution)/shard_map/ppermute | solution.py:46
  95.3 9.3 %collective-permute-start.18 = (f32[256,256]{1,0:T(8,128)S(1)}, f32[256,256]{1,0:T(8,128)S(1)}, u32[]{:S(2)}, u32[]{:S(2)}) collective-permute-start(f32[256,256]{1,0:T(8,128)S(1)} %collective-permute-done.13.c1), channel_id=1, source_target_pairs={{0,1},{1,0},{2,3},{3,2},{4,5},{5,4},{6,7},{7,6},{8,9},{9,8},{10,11... | collective-permute-start | bytes 786440 | tf_op jit(solution)/shard_map/ppermute | solution.py:46
  97.4 7.2 %collective-permute-start.20 = (f32[128,256]{1,0:T(8,128)S(1)}, f32[128,256]{1,0:T(8,128)S(1)}, u32[]{:S(2)}, u32[]{:S(2)}) collective-permute-start(f32[128,256]{1,0:T(8,128)S(1)} %collective-permute-done.16.c2b), channel_id=1, source_target_pairs={{0,1},{1,0},{2,3},{3,2},{4,5},{5,4},{6,7},{7,6},{8,9},{9,8},{10,11... | collective-permute-start | bytes 393224 | tf_op jit(solution)/shard_map/ppermute | solution.py:46
  102.5 2.1 %collective-permute-start.19 = (f32[128,256]{1,0:T(8,128)S(1)}, f32[128,256]{1,0:T(8,128)S(1)}, u32[]{:S(2)}, u32[]{:S(2)}) collective-permute-start(f32[128,256]{1,0:T(8,128)S(1)} %collective-permute-done.14.c2a), channel_id=1, source_target_pairs={{0,1},{1,0},{2,3},{3,2},{4,5},{5,4},{6,7},{7,6},{8,9},{9,8},{10,11... | collective-permute-start | bytes 393224 | tf_op jit(solution)/shard_map/ppermute | solution.py:46
  106.4 9.3 %collective-permute-start.22 = (f32[520,256]{1,0:T(8,128)S(1)}, f32[520,256]{1,0:T(8,128)S(1)}, u32[]{:S(2)}, u32[]{:S(2)}) collective-permute-start(f32[520,256]{1,0:T(8,128)S(1)} %get-tuple-element.30), channel_id=1, source_target_pairs={{0,8},{1,65},{2,10},{3,67},{4,12},{5,69},{6,14},{7,71},{8,16},{9,7... | collective-permute-start | bytes 1597448 | tf_op jit(solution)/shard_map/ppermute | solution.py:38
  107.1 10.9 %collective-permute-start.23 = (f32[520,256]{1,0:T(8,128)S(1)}, f32[520,256]{1,0:T(8,128)S(1)}, u32[]{:S(2)}, u32[]{:S(2)}) collective-permute-start(f32[520,256]{1,0:T(8,128)S(1)} %get-tuple-element.31), channel_id=1, source_target_pairs={{0,16},{1,129},{2,18},{3,131},{4,20},{5,133},{6,22},{7,135},{8,24}... | collective-permute-start | bytes 1597448 | tf_op jit(solution)/shard_map/ppermute | solution.py:38
  108.9 14.6 %collective-permute-start.24 = (f32[520,256]{1,0:T(8,128)S(1)}, f32[520,256]{1,0:T(8,128)S(1)}, u32[]{:S(2)}, u32[]{:S(2)}) collective-permute-start(f32[520,256]{1,0:T(8,128)S(1)} %get-tuple-element.32), channel_id=1, source_target_pairs={{0,24},{1,193},{2,26},{3,195},{4,28},{5,197},{6,30},{7,199},{8,0},... | collective-permute-start | bytes 1597448 | tf_op jit(solution)/shard_map/ppermute | solution.py:38
  124.4 10.8 %collective-permute-start.25 = (f32[272,256]{1,0:T(8,128)S(1)}, f32[272,256]{1,0:T(8,128)S(1)}, u32[]{:S(2)}, u32[]{:S(2)}) collective-permute-start(f32[272,256]{1,0:T(8,128)S(1)} %get-tuple-element.34), channel_id=1, source_target_pairs={{0,64},{1,9},{2,66},{3,11},{4,68},{5,13},{6,70},{7,15},{8,72},{9,1... | collective-permute-start | bytes 835592 | tf_op jit(solution)/shard_map/ppermute | solution.py:38
  124.4 10.7 %collective-permute-start.26 = (f32[272,256]{1,0:T(8,128)S(1)}, f32[272,256]{1,0:T(8,128)S(1)}, u32[]{:S(2)}, u32[]{:S(2)}) collective-permute-start(f32[272,256]{1,0:T(8,128)S(1)} %get-tuple-element.35), channel_id=1, source_target_pairs={{0,128},{1,17},{2,130},{3,19},{4,132},{5,21},{6,134},{7,23},{8,136... | collective-permute-start | bytes 835592 | tf_op jit(solution)/shard_map/ppermute | solution.py:38
  127.3 8.8 %collective-permute-start.27 = (f32[272,256]{1,0:T(8,128)S(1)}, f32[272,256]{1,0:T(8,128)S(1)}, u32[]{:S(2)}, u32[]{:S(2)}) collective-permute-start(f32[272,256]{1,0:T(8,128)S(1)} %get-tuple-element.36), channel_id=1, source_target_pairs={{0,192},{1,25},{2,194},{3,27},{4,196},{5,29},{6,198},{7,31},{8,200... | collective-permute-start | bytes 835592 | tf_op jit(solution)/shard_map/ppermute | solution.py:38
  136.1 5.2 %collective-permute-start.28 = (f32[144,256]{1,0:T(8,128)S(1)}, f32[144,256]{1,0:T(8,128)S(1)}, u32[]{:S(2)}, u32[]{:S(2)}) collective-permute-start(f32[144,256]{1,0:T(8,128)S(1)} %get-tuple-element.38), channel_id=1, source_target_pairs={{0,32},{1,33},{2,34},{3,35},{4,36},{5,37},{6,38},{7,39},{8,40},{9,... | collective-permute-start | bytes 442376 | tf_op jit(solution)/shard_map/ppermute | solution.py:42

commit v2 on v1

v2 whole, which is shorter than its diff:
```python
import functools

import jax
import jax.numpy as jnp
from jax import lax
from jax.experimental import pallas as pl
from jax.experimental.pallas import tpu as pltpu
from jax.sharding import PartitionSpec as P

AXES = ("cube", "col")
F32 = jnp.float32
VMEM = pltpu.VMEM
SMEM = pltpu.SMEM


def index_of(x, y, zl, zh, core):
    return ((y * 2 + zl) * 4 + x) * 8 + zh * 2 + core


def table(move):
    pairs = []
    for y in range(4):
        for zl in range(2):
            for x in range(4):
                for zh in range(4):
                    for core in range(2):
                        pairs.append(
                            (index_of(x, y, zl, zh, core), index_of(*move(x, y, zl, zh, core)))
                        )
    return pairs


def send_pq(v, dp, dq):
    def move(x, y, zl, zh, core):
        dx, dy = (dp, dq) if core == 0 else (dq, dp)
        return (x + dx) % 4, (y + dy) % 4, zl, zh, core

    return lax.ppermute(v, AXES, table(move))


def send_x(v, d):
    return lax.ppermute(v, AXES, table(lambda x, y, zl, zh, core: ((x + d) % 4, y, zl, zh, core)))


def send_y(v, d):
    return lax.ppermute(v, AXES, table(lambda x, y, zl, zh, core: (x, (y + d) % 4, zl, zh, core)))


def send_pair(v):
    return lax.ppermute(v, AXES, table(lambda x, y, zl, zh, core: (x, y, 1 - zl, zh, core)))


def send_core(v):
    return lax.ppermute(v, AXES, table(lambda x, y, zl, zh, core: (x, y, zl, zh, 1 - core)))


def send_zh(v, d):
    return lax.ppermute(v, AXES, table(lambda x, y, zl, zh, core: (x, y, zl, (zh + d) % 4, core)))


def split(a):
    hi = a.astype(jnp.bfloat16)
    lo = (a - hi.astype(F32)).astype(jnp.bfloat16)
    return hi, lo


def dot3(a, b, dims):
    ah, al = split(a)
    bh, bl = split(b)
    dg = functools.partial(lax.dot_general, dimension_numbers=(dims, ((), ())),
                           preferred_element_type=F32)
    return dg(ah, bh) + (dg(ah, bl) + dg(al, bh))


def v_kernel(first, last, n, sizes, cb, meta, *refs):
    gs, refs = refs[:2 * n], refs[2 * n:]
    us, refs = refs[:len(sizes)], refs[len(sizes):]
    if not first:
        (v_in, own_in, ut_in), refs = refs[:3], refs[3:]
    v_out, own_out, ut_out = refs[:3]
    turned = refs[-1]
    if first:
        v_out[...] = jnp.zeros_like(v_out)
        own_out[...] = jnp.zeros_like(own_out)
        ut_out[...] = jnp.zeros_like(ut_out)
    else:
        v_out[...] = v_in[...]
        own_out[...] = own_in[...]
        ut_out[...] = ut_in[...]
    sub = meta[8 * n]
    rows = lax.broadcasted_iota(jnp.int32, (128, 256), 0)
    where = [(u, k) for u, size in zip(us, sizes) for k in range(size)]
    for s in range(2):
        parts = []
        for b, (u, k) in enumerate(where):
            base = (b * 2 + s) * 4
            part = jnp.where(rows < meta[base], u[k, s], 0.0)
            parts.append(part)

            @pl.when(meta[base + 1] >= 0)
            def _():
                at = pl.multiple_of(meta[base + 1] * 128, 128)
                own_out[pl.ds(at, 128), :] = part

            @pl.when(meta[base + 2] >= 0)
            def _():
                turned[...] = part.T
                ut_out[meta[base + 2]] = turned[pl.ds(pl.multiple_of(sub * 64, 64), 64), :]

        uu = jnp.concatenate(parts, axis=0)
        gg = jnp.concatenate([gs[b * 2 + s][...] for b in range(n)], axis=1)
        v_out[s] += dot3(gg, uu, ((1,), (0,)))
    if last:
        msg = refs[3]
        v_own = v_out[meta[8 * n + 1]]
        msg[:256, :] = v_own
        diag = jnp.sum(own_out[...] * v_own, axis=0, keepdims=True)
        msg[256:264, :] = jnp.broadcast_to(diag, (8, 256))


def v_call(ginv, us, cb, meta, carry, last=False):
    sizes = tuple(u.shape[0] for u in us)
    n = sum(sizes)

    def gspec(i):
        return pl.BlockSpec((256, 128), lambda _, cb, meta: (0, cb[i]))

    def full(*shape):
        return pl.BlockSpec(shape, lambda _, cb, meta: (0,) * len(shape))

    first = carry is None
    shapes = [(2, 256, 256), (256, 256), (8, 64, 128)]
    extra = [] if first else [full(*shape) for shape in shapes]
    at = 2 + 2 * n + len(us)
    aliases = {} if first else {at + i: i for i in range(3)}
    if last:
        shapes.append((264, 256))
    return pl.pallas_call(
        functools.partial(v_kernel, first, last, n, sizes),
        grid_spec=pltpu.PrefetchScalarGridSpec(
            num_scalar_prefetch=2,
            grid=(1,),
            in_specs=[gspec(i) for i in range(2 * n)] + [full(z, 2, 128, 256) for z in sizes] + extra,
            out_specs=[full(*shape) for shape in shapes],
            scratch_shapes=[VMEM((256, 128), F32)],
        ),
        out_shape=[jax.ShapeDtypeStruct(shape, F32) for shape in shapes],
        input_output_aliases=aliases,
        compiler_params=pltpu.CompilerParams(vmem_limit_bytes=57 * 2**20),
        cost_estimate=pl.CostEstimate(flops=3 * 4 * 256 * 128 * n * 256,
                                      bytes_accessed=(n + 3) * 2**19, transcendentals=0),
        name="v_part",
    )(cb, meta, *([ginv] * (2 * n)), *us, *(() if first else carry))


def prod_kernel(pos, v0, v1, v2, v3, n0, n1, n2a, n2b, n3, f0, f1, f2a, f2b, f3,
                m0, m1, m2, m3, acc):
    x, y, zl, zh, core = pos[0], pos[1], pos[2], pos[3], pos[4]
    acc[...] = jnp.zeros_like(acc)
    vs = (v0, v1, v2, v3)
    us = ((n0, f0), (n1, f1), ((n2a, n2b), (f2a, f2b)), (n3, f3))
    order = [(k, side) for k in range(4) for side in range(2)]
    for t in range(4):
        tile = lax.rem(x + 4 - t, 4)
        left = []
        for k, side in order:
            if k == 2:
                lo, hi = us[k][side]
                at = lax.rem(tile, 2) * 2
                pair = [jnp.where(tile < 2, lo[at + h], hi[at + h]) for h in range(2)]
            else:
                pair = [us[k][side][tile * 2 + h] for h in range(2)]
            left.append(jnp.concatenate(pair, axis=1))
        part = dot3(jnp.concatenate(left, axis=0), vs[t][:256, :], ((1,), (0,)))
        s = pos[5 + t]
        for i, (k, side) in enumerate(order):
            block = lax.rem(zh + 4 - k, 4) * 2 + (core if side == 0 else 1 - core)
            acc[s, block] += part[i * 64:(i + 1) * 64, :]
    diag = []
    for s in range(2):
        total = None
        for t in range(4):
            term = jnp.where(pos[5 + t] == s, vs[t][256:264, :], 0.0)
            total = term if total is None else total + term
        diag.append(total)
    for k, m in enumerate((m0, m1, m2, m3)):
        for zrel in range(2):
            for s in range(2):
                block = 2 * lax.rem(y + k, 4) + lax.rem(zl + zrel, 2)
                at = (zrel * 2 + s) * 64
                m[at:at + 64, :] = acc[s, block]
        m[256:264, :] = diag[0]
        m[264:272, :] = diag[1]


def prod_call(pos, vs, pieces):
    spec = pl.BlockSpec(memory_space=VMEM)
    return pl.pallas_call(
        prod_kernel,
        in_specs=[pl.BlockSpec(memory_space=SMEM)] + [spec] * 14,
        out_specs=[spec] * 4,
        out_shape=[jax.ShapeDtypeStruct((272, 256), F32)] * 4,
        scratch_shapes=[VMEM((2, 8, 64, 256), F32)],
        compiler_params=pltpu.CompilerParams(vmem_limit_bytes=24 * 2**20),
        cost_estimate=pl.CostEstimate(flops=3 * 2 * 512 * 1024 * 256, bytes_accessed=5 * 2**20,
                                      transcendentals=0),
        name="product",
    )(pos, *vs, *pieces)


def sum2_kernel(r0, r1, r2, r3, keep, away):
    for rows, o, to in ((0, keep, 0), (128, away, 0)):
        o[to:to + 128, :] = (r0[rows:rows + 128, :] + r1[rows:rows + 128, :]) + (
            r2[rows:rows + 128, :] + r3[rows:rows + 128, :])
    d = (r0[256:272, :] + r1[256:272, :]) + (r2[256:272, :] + r3[256:272, :])
    keep[128:144, :] = d
    away[128:144, :] = d


def sum2_call(rs):
    spec = pl.BlockSpec(memory_space=VMEM)
    return pl.pallas_call(
        sum2_kernel,
        in_specs=[spec] * 4,
        out_specs=[spec] * 2,
        out_shape=[jax.ShapeDtypeStruct((144, 256), F32)] * 2,
        compiler_params=pltpu.CompilerParams(vmem_limit_bytes=16 * 2**20),
        name="sum_second",
    )(*rs)


def body(ginv, ufactor, dinv, tile_map, counts, assign):
    me = lax.axis_index("cube")
    col = lax.axis_index("col")
    x, zl, y = lax.rem(me, 4), lax.rem(me // 4, 2), me // 8
    zh, core = col // 2, lax.rem(col, 2)

    flip = assign[0] != 0
    tile_s = jnp.where(flip, tile_map[::-1], tile_map)
    counts_s = jnp.where(flip, counts[::-1], counts)

    step = jnp.arange(4, dtype=jnp.int32)
    plane = jnp.arange(2, dtype=jnp.int32)
    dp, dq = step[None, None, :], step[None, :, None]
    dx = jnp.where(core == 0, dp, dq)
    dy = jnp.where(core == 0, dq, dp)
    src = (((y + 4 - dy) % 4) * 2 + (zl + plane[:, None, None]) % 2) * 4 + (x + 4 - dx) % 4
    src = src[..., None]
    s_ids = plane[None, None, None, :]
    slot_tile = tile_s.reshape(-1)[s_ids * 16 + src // 2]
    cb = (slot_tile * 2 + src % 2).astype(jnp.int32)
    live = jnp.clip(counts_s[s_ids] - src * 128, 0, 128).astype(jnp.int32)
    half = jnp.where(slot_tile == me, src % 2, -1).astype(jnp.int32)
    spot = slot_tile - (y * 2 + zl) * 4
    spot = jnp.where((spot >= 0) & (spot < 4), spot * 2 + src % 2, -1).astype(jnp.int32)
    meta = jnp.stack([live, half, spot, jnp.zeros_like(live)], axis=-1)

    in_one = jnp.any(tile_s[1][:, None] == jnp.arange(32, dtype=jnp.int32)[None, :], axis=0)
    front_of = in_one.astype(jnp.int32)
    s_own = front_of[me]

    pin = lax.optimization_barrier

    def part(*which):
        pick = lambda t: jnp.concatenate([t[g, q, lo:hi].reshape(-1) for g, q, lo, hi in which])
        return pick(cb), jnp.concatenate([pick(meta), jnp.stack([x, s_own]).astype(jnp.int32)])

    a0 = ufactor
    ga = jnp.stack([a0, send_pq(a0, 1, 0), send_pq(a0, 2, 0), send_pq(a0, -1, 0)])
    ga1 = send_pq(ga, 0, 1)
    ga3 = send_pq(ga, 0, -1)
    b1 = send_pair(ga[:2])
    b2 = send_pair(ga[2:])
    carry = v_call(ginv, [ga], *part((0, 0, 0, 4)), None)
    ga1, ga3, b1, carry = pin((ga1, ga3, b1, carry))
    ga2a = send_pq(ga1[:2], 0, 1)
    ga2b = send_pq(ga3[2:], 0, -1)
    b11 = send_pq(b1, 0, 1)
    b13 = send_pq(b1, 0, -1)
    carry = v_call(ginv, [ga1, ga3], *part((0, 1, 0, 4), (0, 3, 0, 4)), carry)
    b2, carry, ga2a, ga2b = pin((b2, carry, ga2a, ga2b))
    b21 = send_pq(b2, 0, 1)
    b23 = send_pq(b2, 0, -1)
    b11, b13, b2 = pin((b11, b13, b2))
    b12 = send_pq(b11, 0, 1)
    carry = v_call(ginv, [ga2a, ga2b, b1, b2],
                   *part((0, 2, 0, 2), (0, 2, 2, 4), (1, 0, 0, 2), (1, 0, 2, 4)), carry)
    b21, b23, carry = pin((b21, b23, carry))
    b22 = send_pq(b23, 0, -1)
    carry = v_call(ginv, [b11, b13, b21, b23],
                   *part((1, 1, 0, 2), (1, 3, 0, 2), (1, 1, 2, 4), (1, 3, 2, 4)), carry)
    b12, b22, carry = pin((b12, b22, carry))
    v, _, ut, msg = v_call(ginv, [b12, b22], *part((1, 2, 0, 2), (1, 2, 2, 4)), carry, True)

    c1 = send_zh(ut, 1)
    c3 = send_zh(ut, -1)
    vs = [msg, send_x(msg, 1), send_x(msg, 2), send_x(msg, -1)]
    c2a = send_zh(c1[:4], 1)
    c2b = send_zh(c3[4:], -1)
    near = [ut, c1, c2a, c2b, c3]
    far = [send_core(t) for t in near]

    fronts = front_of[(y * 2 + zl) * 4 + (x + 4 - step) % 4]
    pos = jnp.concatenate([jnp.stack([x, y, zl, zh, core]), fronts]).astype(jnp.int32)
    m = prod_call(pos, vs, near + far)
    r = [m[0], send_y(m[1], 1), send_y(m[2], 2), send_y(m[3], -1)]
    keep, away = sum2_call(r)
    total = keep + send_pair(away)

    front_order = lambda t: jnp.where(flip, t[::-1], t)
    d_local = front_order(dinv)
    sigma = front_order(total[:128].reshape(2, 64, 256)).transpose(1, 0, 2)
    rows = me * 64 + jnp.arange(64, dtype=jnp.int32)
    cols = col * 256 + jnp.arange(256, dtype=jnp.int32)
    on_diag = rows[:, None] == cols[None, :]
    sigma = sigma + jnp.where(on_diag[:, None, :], d_local[None], 0.0)
    diag = front_order(jnp.stack([total[128], total[136]])) + d_local

    block = lax.dynamic_slice_in_dim(ginv, me * 256, 256, 1)
    eye = jnp.arange(256)[:, None] == jnp.arange(256)[None, :]
    g_diag = jnp.sum(jnp.where(eye, block, 0.0), axis=1)
    slots = jnp.arange(16, dtype=jnp.int32)
    at = jnp.sum(jnp.where(tile_map == me, slots[None, :] + 1, 0), axis=1)
    row = (at[:, None] - 1) * 256 + jnp.arange(256, dtype=jnp.int32)[None, :]
    live_row = (at[:, None] > 0) & (row < counts[:, None])
    vf = front_order(v)
    cross = -vf
    resist = jnp.where(live_row[:, :, None], diag[:, None, :] + g_diag[None, :, None] + 2.0 * vf, 0.0)
    return cross, resist, sigma


def solution(mesh):
    in_specs = (P("cube", None), P(None, "cube", "col"), P(None, "col"), P(), P(), P())
    out_specs = (P(None, "cube", "col"), P(None, "cube", "col"), P("cube", None, "col"))
    return jax.shard_map(body, mesh=mesh, in_specs=in_specs, out_specs=out_specs, check_vma=False)
```

time: 144 us -> 144 us (level); the launches traced: 144 us -> 142 us
  waiting for transfers between devices: 61.5 us -> 32.8 us
  other arithmetic: 5.99 us -> 16.3 us
  Pallas kernels: 23 us -> 32.7 us
  local copies, waits for them, and re-layouts: 11.7 us -> 16.7 us
    ppermute x18 -> x13, waiting for transfers between devices: 39.5 us -> 2.4 us  [send_pq(): return lax.ppermute(v, AXES, table(move))]
    ppermute x0 -> x6, waiting for transfers between devices: none -> 12.1 us  [the longest x3 12 us: send_y(): lax.ppermute(v, AXES, table(lambda x, y, zl, zh, core: (x, (y + d) % 4, z...]
    pallas_call x6, Pallas kernels: 22.9 us -> 32.7 us  [the longest x5 30.1 us: v_call(): pl.pallas_call(functools.partial(v_kernel, first, last, n, sizes), grid_s...]
    ppermute x18 -> x13, starting transfers between devices: 27.9 us -> 20.1 us  [send_pq(): return lax.ppermute(v, AXES, table(move))]
    ppermute x4, waiting for transfers between devices: 16.3 us -> 8.73 us  [send_zh(): lax.ppermute(v, AXES, table(lambda x, y, zl, zh, core: (x, y, zl, (zh + d...]
    ppermute x0 -> x6, starting transfers between devices: none -> 5.63 us  [the longest x3 3.24 us: send_y(): lax.ppermute(v, AXES, table(lambda x, y, zl, zh, core: (x, (y + d) % 4, z...]
    concatenate x8 -> x7, other arithmetic: 0.61 us -> 6.22 us  [the longest x3 3.79 us: part(): jnp.concatenate([pick(meta), jnp.stack([x, s_own]).astype(jnp.int32)])]
    another operation x3 -> x4, other arithmetic: 0.18 us -> 3.74 us  [the longest x3 3.72 us: body(): jnp.stack([a0, send_pq(a0, 1, 0), send_pq(a0, 2, 0), send_pq(a0, -1, 0)])]
  transfers between devices with their start and end apart: 29 -> 31, of which waited for: 14 -> 9; matrix products, arithmetic and copies ran while one was open for 8% -> 18% of each run, Pallas kernels for 10% -> 18%
where the time goes in v2:
time: 144 us; the launch traced here: 142 us
  starting transfers between devices  41.3 us (29%)
  waiting for transfers between devices  32.8 us (23%)
  Pallas kernels  32.7 us (23%)
  local copies, waits for them, and re-layouts  16.7 us (12%)
  other arithmetic  16.3 us (11%)
  between operations  1.8 us (1%)
    pallas_call x5, Pallas kernels, v_call(): pl.pallas_call(functools.partial(v_kernel, first, last, n, sizes), grid_s...  30.1 us
    ppermute x13, starting transfers between devices, send_pq(): return lax.ppermute(v, AXES, table(move))  20.1 us
    ppermute x4, starting transfers between devices, send_zh(): lax.ppermute(v, AXES, table(lambda x, y, zl, zh, core: (x, y, zl, (zh + d...  13 us
    ppermute x3, waiting for transfers between devices, send_y(): lax.ppermute(v, AXES, table(lambda x, y, zl, zh, core: (x, (y + d) % 4, z...  12 us
    ppermute x3, waiting for transfers between devices, send_pair(): lax.ppermute(v, AXES, table(lambda x, y, zl, zh, core: (x, y, 1 - zl, zh,...  9.04 us
    ppermute x4, waiting for transfers between devices, send_zh(): lax.ppermute(v, AXES, table(lambda x, y, zl, zh, core: (x, y, zl, (zh + d...  8.73 us
    concatenate x3, other arithmetic, part(): jnp.concatenate([pick(meta), jnp.stack([x, s_own]).astype(jnp.int32)])  3.79 us
    another operation x3, other arithmetic, body(): jnp.stack([a0, send_pq(a0, 1, 0), send_pq(a0, 2, 0), send_pq(a0, -1, 0)])  3.72 us
  transfers between devices with their start and end apart: 31, of which 9 were waited for; matrix products, arithmetic and copies ran while one was open for 18% of the time, Pallas kernels for 18%

profile of v2, /device:TPU:2, one launch (start us, length us, event | category | flops | bytes accessed | tf_op | source)
XLA Modules:
  0.0 141.7 jit_solution(1788421321441224425)
XLA Ops:
  0.6 1.6 %collective-permute-start = (f32[2,128,256]{2,1,0:T(8,128)}, f32[2,128,256]{2,1,0:T(8,128)S(1)}, u32[]{:S(2)}, u32[]{:S(2)}) collective-permute-start(f32[2,128,256]{2,1,0:T(8,128)} %param.7), channel_id=1, source_target_pairs={{0,8},{1,65},{2,10},{3,67},{4,12},{5,69},{6,14},{7,71},{8,16},{9,7... | collective-permute-start | bytes 786440 | tf_op jit(solution)/shard_map/ppermute | solution.py:38
  2.2 2.8 %collective-permute-start.1 = (f32[2,128,256]{2,1,0:T(8,128)}, f32[2,128,256]{2,1,0:T(8,128)S(1)}, u32[]{:S(2)}, u32[]{:S(2)}) collective-permute-start(f32[2,128,256]{2,1,0:T(8,128)} %param.7), channel_id=1, source_target_pairs={{0,16},{1,129},{2,18},{3,131},{4,20},{5,133},{6,22},{7,135},{8,24}... | collective-permute-start | bytes 786440 | tf_op jit(solution)/shard_map/ppermute | solution.py:38
  5.0 0.4 collective-permute-start.2
  5.8 0.7 rev.18
  7.2 1.3 fusion.8
  8.6 0.8 gather_fusion
  9.8 0.6 gather_fusion.1
  10.7 2.4 %collective-permute-done.2 = f32[2,128,256]{2,1,0:T(8,128)S(1)} collective-permute-done((f32[2,128,256]{2,1,0:T(8,128)}, f32[2,128,256]{2,1,0:T(8,128)S(1)}, u32[]{:S(2)}, u32[]{:S(2)}) %collective-permute-start.2) | collective-permute-done | bytes 262176 | tf_op jit(solution)/shard_map/ppermute | solution.py:38
  13.1 0.7 copy-done.9
  13.9 1.3 collective-permute-start.3
  15.2 2.1 %collective-permute-start.4 = (f32[4,2,128,256]{3,2,1,0:T(8,128)S(1)}, f32[4,2,128,256]{3,2,1,0:T(8,128)S(1)}, u32[]{:S(2)}, u32[]{:S(2)}) collective-permute-start(f32[4,2,128,256]{3,2,1,0:T(8,128)S(1)} %pad_maximum_fusion.refs_8_), channel_id=1, source_target_pairs={{0,192},{1,25},{2,194},{3,27},{4,196},{5,29},{6,198},{7,31},{8,200... | collective-permute-start | bytes 3145736 | tf_op jit(solution)/shard_map/ppermute | solution.py:38
  17.4 1.8 %pad_maximum_fusion.1 = f32[2,2,128,256]{3,2,1,0:T(8,128)} fusion(f32[1,2,128,256]{3,2,1,0:T(8,128)} %bitcast.29, f32[1,2,128,256]{3,2,1,0:T(8,128)S(1)} %bitcast.23), kind=kLoop, calls=%fused_computation.5 | loop fusion | flops 131072 | bytes 1048576 | tf_op jit(solution)/shard_map/stack | solution.py:269
  19.2 1.5 %collective-permute-start.5 = (f32[2,2,128,256]{3,2,1,0:T(8,128)}, f32[2,2,128,256]{3,2,1,0:T(8,128)}, u32[]{:S(2)}, u32[]{:S(2)}) collective-permute-start(f32[2,2,128,256]{3,2,1,0:T(8,128)} %pad_maximum_fusion.1), channel_id=1, source_target_pairs={{0,32},{1,33},{2,34},{3,35},{4,36},{5,37},{6,38},{7,39},{8,40},{9,... | collective-permute-start | bytes 1572872 | tf_op jit(solution)/shard_map/ppermute | solution.py:50
  21.1 0.6 reshape_squeeze.82.cb
  21.6 0.6 dynamic_slice.6
  22.2 1.3 add_add_fusion.1.meta
  23.5 1.9 %pad_maximum_fusion.2 = f32[2,2,128,256]{3,2,1,0:T(8,128)} fusion(f32[1,2,128,256]{3,2,1,0:T(8,128)} %bitcast.27, f32[1,2,128,256]{3,2,1,0:T(8,128)} %bitcast.25), kind=kLoop, calls=%fused_computation.6 | loop fusion | flops 131072 | bytes 1048576 | tf_op jit(solution)/shard_map/stack | solution.py:269
  25.4 0.5 collective-permute-start.8
  25.9 4.5 %v_part.5 = (f32[2,256,256]{2,1,0:T(8,128)}, f32[256,256]{1,0:T(8,128)}, f32[8,64,128]{2,1,0:T(8,128)}) custom-call(s32[8]{0:T(128)} %reshape_squeeze.82.cb, s32[34]{0:T(128)} %add_add_fusion.1.meta, f32[256,8192]{1,0:T(8,128)} %refs_7_.9, f32[256,8192]{1,0:T(8,128)} %refs_7_.9, f32[256,8192]{1,0:T(8,128)} %refs_7_.9, f32[256,8192]{1,0:T(8,128)} %refs_7_.9, ...), custom_call_target="tpu_custom_call" | custom-call | flops 402653184 | bytes 3670016 | tf_op jit(solution)/shard_map/v_part/pallas_call | solution.py:138
  30.4 4.0 %collective-permute-done.5.refs_18_ = f32[2,2,128,256]{3,2,1,0:T(8,128)} collective-permute-done((f32[2,2,128,256]{3,2,1,0:T(8,128)}, f32[2,2,128,256]{3,2,1,0:T(8,128)}, u32[]{:S(2)}, u32[]{:S(2)}) %collective-permute-start.5) | collective-permute-done | bytes 524320 | tf_op jit(solution)/shard_map/ppermute | solution.py:50
  34.4 0.9 slice.122
  35.3 1.4 collective-permute-start.10
  36.7 0.8 slice.121
  37.6 0.6 collective-permute-start.9
  39.3 1.2 pad_add_fusion.13.meta
  40.6 0.6 pad_add_fusion.12.cb
  41.2 3.2 %collective-permute-start.7 = (f32[2,2,128,256]{3,2,1,0:T(8,128)}, f32[2,2,128,256]{3,2,1,0:T(8,128)S(1)}, u32[]{:S(2)}, u32[]{:S(2)}) collective-permute-start(f32[2,2,128,256]{3,2,1,0:T(8,128)} %collective-permute-done.5.refs_18_), channel_id=1, source_target_pairs={{0,192},{1,25},{2,194},{3,27},{4,196},{5,29},{6,198},{7,31},{8,200... | collective-permute-start | bytes 1572872 | tf_op jit(solution)/shard_map/ppermute | solution.py:38
  44.4 6.9 %v_part.6 = (f32[2,256,256]{2,1,0:T(8,128)}, f32[256,256]{1,0:T(8,128)}, f32[8,64,128]{2,1,0:T(8,128)}) custom-call(s32[16]{0:T(128)} %pad_add_fusion.12.cb, s32[66]{0:T(128)} %pad_add_fusion.13.meta, f32[256,8192]{1,0:T(8,128)} %refs_7_.9, f32[256,8192]{1,0:T(8,128)} %refs_7_.9, ...), custom_call_target="tpu_custom_call", output_to_operand_aliasing={{0}: (20, {}), {1}: (21, {}), {2}: (22, {})} | custom-call | flops 805306368 | bytes 5767168 | tf_op jit(solution)/shard_map/v_part/pallas_call | solution.py:138
  51.4 3.2 %collective-permute-start.13 = (f32[2,2,128,256]{3,2,1,0:T(8,128)}, f32[2,2,128,256]{3,2,1,0:T(8,128)S(1)}, u32[]{:S(2)}, u32[]{:S(2)}) collective-permute-start(f32[2,2,128,256]{3,2,1,0:T(8,128)} %collective-permute-done.8.refs_19_), channel_id=1, source_target_pairs={{0,192},{1,25},{2,194},{3,27},{4,196},{5,29},{6,198},{7,31},{8,200... | collective-permute-start | bytes 1572872 | tf_op jit(solution)/shard_map/ppermute | solution.py:38
  56.3 1.2 concatenate.38.meta
  57.5 0.6 pad_add_fusion.14.cb
  58.2 7.0 %v_part.7 = (f32[2,256,256]{2,1,0:T(8,128)}, f32[256,256]{1,0:T(8,128)}, f32[8,64,128]{2,1,0:T(8,128)}) custom-call(s32[16]{0:T(128)} %pad_add_fusion.14.cb, s32[66]{0:T(128)} %concatenate.38.meta, f32[256,8192]{1,0:T(8,128)} %refs_7_.9, f32[256,8192]{1,0:T(8,128)} %refs_7_.9, ...), custom_call_target="tpu_custom_call", output_to_operand_aliasing={{0}: (22, {}), {1}: (23, {}), {2}: (24, {})} | custom-call | flops 805306368 | bytes 5767168 | tf_op jit(solution)/shard_map/v_part/pallas_call | solution.py:138
  65.3 3.3 %collective-permute-start.14 = (f32[2,2,128,256]{3,2,1,0:T(8,128)S(1)}, f32[2,2,128,256]{3,2,1,0:T(8,128)S(1)}, u32[]{:S(2)}, u32[]{:S(2)}) collective-permute-start(f32[2,2,128,256]{3,2,1,0:T(8,128)S(1)} %collective-permute-done.13.refs_19_), channel_id=1, source_target_pairs={{0,192},{1,25},{2,194},{3,27},{4,196},{5,29},{6,198},{7,31},{8,200... | collective-permute-start | bytes 1572872 | tf_op jit(solution)/shard_map/ppermute | solution.py:38
  69.1 1.3 concatenate.40.meta
  70.3 1.3 add_add_fusion.meta
  71.6 0.6 pad_add_fusion.11.cb
  72.2 0.6 pad_add_fusion.15.cb
  72.8 6.5 %v_part.8 = (f32[2,256,256]{2,1,0:T(8,128)}, f32[256,256]{1,0:T(8,128)}, f32[8,64,128]{2,1,0:T(8,128)}) custom-call(s32[16]{0:T(128)} %pad_add_fusion.15.cb, s32[66]{0:T(128)} %concatenate.40.meta, f32[256,8192]{1,0:T(8,128)} %refs_7_.9, f32[256,8192]{1,0:T(8,128)} %refs_7_.9, ...), custom_call_target="tpu_custom_call", output_to_operand_aliasing={{0}: (22, {}), {1}: (23, {}), {2}: (24, {})} | custom-call | flops 805306368 | bytes 5767168 | tf_op jit(solution)/shard_map/v_part/pallas_call | solution.py:138
  79.4 0.8 copy-done.15
  80.3 5.2 %v_part.9 = (f32[2,256,256]{2,1,0:T(8,128)}, f32[256,256]{1,0:T(8,128)}, f32[8,64,128]{2,1,0:T(8,128)}, f32[264,256]{1,0:T(8,128)}) custom-call(s32[8]{0:T(128)} %pad_add_fusion.11.cb, s32[34]{0:T(128)} %add_add_fusion.meta, f32[256,8192]{1,0:T(8,128)} %refs_7_.9, ...), custom_call_target="tpu_custom_call", output_to_operand_aliasing={{0}: (12, {}), {1}: (13, {}), {2}: (14, {})} | custom-call | flops 402653184 | bytes 3670016 | tf_op jit(solution)/shard_map/v_part/pallas_call | solution.py:138
  85.5 2.9 %collective-permute-start.18 = (f32[8,64,128]{2,1,0:T(8,128)}, f32[8,64,128]{2,1,0:T(8,128)S(1)}, u32[]{:S(2)}, u32[]{:S(2)}) collective-permute-start(f32[8,64,128]{2,1,0:T(8,128)} %get-tuple-element.88.n0), channel_id=1, source_target_pairs={{0,2},{1,3},{2,4},{3,5},{4,6},{5,7},{6,0},{7,1},{8,10},{9,11},{10,... | collective-permute-start | bytes 786440 | tf_op jit(solution)/shard_map/ppermute | solution.py:58
  88.4 3.3 %collective-permute-start.20 = (f32[8,64,128]{2,1,0:T(8,128)}, f32[8,64,128]{2,1,0:T(8,128)S(1)}, u32[]{:S(2)}, u32[]{:S(2)}) collective-permute-start(f32[8,64,128]{2,1,0:T(8,128)} %get-tuple-element.88.n0), channel_id=1, source_target_pairs={{0,6},{1,7},{2,0},{3,1},{4,2},{5,3},{6,4},{7,5},{8,14},{9,15},{10,... | collective-permute-start | bytes 786440 | tf_op jit(solution)/shard_map/ppermute | solution.py:58
  91.7 1.0 collective-permute-start.15
  92.7 1.3 collective-permute-start.16
  94.0 2.6 %collective-permute-done.18.n1 = f32[8,64,128]{2,1,0:T(8,128)S(1)} collective-permute-done((f32[8,64,128]{2,1,0:T(8,128)}, f32[8,64,128]{2,1,0:T(8,128)S(1)}, u32[]{:S(2)}, u32[]{:S(2)}) %collective-permute-start.18) | collective-permute-done | bytes 262176 | tf_op jit(solution)/shard_map/ppermute | solution.py:58
  96.6 5.8 %collective-permute-start.19 = (f32[4,64,128]{2,1,0:T(8,128)S(1)}, f32[4,64,128]{2,1,0:T(8,128)S(1)}, u32[]{:S(2)}, u32[]{:S(2)}) collective-permute-start(f32[4,64,128]{2,1,0:T(8,128)S(1)} %slice.166), channel_id=1, source_target_pairs={{0,2},{1,3},{2,4},{3,5},{4,6},{5,7},{6,0},{7,1},{8,10},{9,11},{10,... | collective-permute-start | bytes 393224 | tf_op jit(solution)/shard_map/ppermute | solution.py:58
  102.4 1.0 collective-permute-start.21
  103.7 0.5 collective-permute-start.26
  104.2 2.1 %collective-permute-done.19.n2a = f32[4,64,128]{2,1,0:T(8,128)S(1)} collective-permute-done((f32[4,64,128]{2,1,0:T(8,128)S(1)}, f32[4,64,128]{2,1,0:T(8,128)S(1)}, u32[]{:S(2)}, u32[]{:S(2)}) %collective-permute-start.19) | collective-permute-done | bytes 131104 | tf_op jit(solution)/shard_map/ppermute | solution.py:58
  106.3 4.0 %collective-permute-done.21.n2b = f32[4,64,128]{2,1,0:T(8,128)S(1)} collective-permute-done((f32[4,64,128]{2,1,0:T(8,128)S(1)}, f32[4,64,128]{2,1,0:T(8,128)S(1)}, u32[]{:S(2)}, u32[]{:S(2)}) %collective-permute-start.21) | collective-permute-done | bytes 131104 | tf_op jit(solution)/shard_map/ppermute | solution.py:58
  110.3 0.6 gather_fusion.2
  111.0 0.6 collective-permute-done.25.f2b
  111.6 0.9 copy-done
  112.6 1.0 copy-done.1
  113.5 2.5 %product.1 = (f32[272,256]{1,0:T(8,128)S(1)}, f32[272,256]{1,0:T(8,128)}, f32[272,256]{1,0:T(8,128)S(1)}, f32[272,256]{1,0:T(8,128)S(1)}) custom-call(s32[9]{0:T(128)S(1)} %concatenate.41.pos, f32[264,256]{1,0:T(8,128)S(1)} %copy-done.1, f32[264,256]{1,0:T(8,128)S(1)} %collective-permute-done.15.v1, f32[264,256]{1,0:T(8,128)S(1)} %collective-permute-done.16.v2, ...), custom_call_target="tpu_custom_call" | custom-call | flops 805306368 | bytes 5242880 | tf_op jit(solution)/shard_map/product/pallas_call | solution.py:198
  116.1 1.3 collective-permute-start.28
  117.3 2.0 %collective-permute-start.29 = (f32[272,256]{1,0:T(8,128)S(1)}, f32[272,256]{1,0:T(8,128)S(1)}, u32[]{:S(2)}, u32[]{:S(2)}) collective-permute-start(f32[272,256]{1,0:T(8,128)S(1)} %get-tuple-element.92), channel_id=1, source_target_pairs={{0,192},{1,193},{2,194},{3,195},{4,196},{5,197},{6,198},{7,199},{8... | collective-permute-start | bytes 835592 | tf_op jit(solution)/shard_map/ppermute | solution.py:46
  119.4 1.1 select_reduce_fusion
  120.5 11.6 %collective-permute-done.27.r1 = f32[272,256]{1,0:T(8,128)S(1)} collective-permute-done((f32[272,256]{1,0:T(8,128)}, f32[272,256]{1,0:T(8,128)S(1)}, u32[]{:S(2)}, u32[]{:S(2)}) %collective-permute-start.27) | collective-permute-done | bytes 278560 | tf_op jit(solution)/shard_map/ppermute | solution.py:46
  132.2 0.4 collective-permute-done.29.r3
  132.8 5.0 %collective-permute-done.30 = f32[144,256]{1,0:T(8,128)S(1)} collective-permute-done((f32[144,256]{1,0:T(8,128)S(1)}, f32[144,256]{1,0:T(8,128)S(1)}, u32[]{:S(2)}, u32[]{:S(2)}) %collective-permute-start.30) | collective-permute-done | bytes 147488 | tf_op jit(solution)/shard_map/ppermute | solution.py:50
  138.0 0.4 rev.23
  138.6 0.8 bitcast_add_fusion
  139.4 2.3 %add_select_fusion = (f32[2,256,256]{2,1,0:T(8,128)}, f32[2,256,256]{2,1,0:T(8,128)}) fusion(f32[2,256,256]{2,1,0:T(8,128)} %get-tuple-element.86, f32[256]{0:T(256)S(1)} %select_reduce_fusion, f32[2,256]{1,0:T(2,128)S(1)} %get-tuple-element.95, pred[2,256]{1,0:T(4,128)(4,1)S(1)} %compare_and_fusion, pred[]{:T(512)} %bitcast), kind=kLoop, calls=%fused_computation.7 | loop fusion | flops 786432 | bytes 1576449 | tf_op jit(solution)/shard_map/jit(_where)/select_n | solution.py:328
  (162 shorter events, 6.3 us)
Async XLA Ops:
  0.6 10.1 %collective-permute-start = (f32[2,128,256]{2,1,0:T(8,128)}, f32[2,128,256]{2,1,0:T(8,128)S(1)}, u32[]{:S(2)}, u32[]{:S(2)}) collective-permute-start(f32[2,128,256]{2,1,0:T(8,128)} %param.7), channel_id=1, source_target_pairs={{0,8},{1,65},{2,10},{3,67},{4,12},{5,69},{6,14},{7,71},{8,16},{9,7... | collective-permute-start | bytes 786440 | tf_op jit(solution)/shard_map/ppermute | solution.py:38
  2.2 8.5 %collective-permute-start.1 = (f32[2,128,256]{2,1,0:T(8,128)}, f32[2,128,256]{2,1,0:T(8,128)S(1)}, u32[]{:S(2)}, u32[]{:S(2)}) collective-permute-start(f32[2,128,256]{2,1,0:T(8,128)} %param.7), channel_id=1, source_target_pairs={{0,16},{1,129},{2,18},{3,131},{4,20},{5,133},{6,22},{7,135},{8,24}... | collective-permute-start | bytes 786440 | tf_op jit(solution)/shard_map/ppermute | solution.py:38
  5.0 8.0 %collective-permute-start.2 = (f32[2,128,256]{2,1,0:T(8,128)}, f32[2,128,256]{2,1,0:T(8,128)S(1)}, u32[]{:S(2)}, u32[]{:S(2)}) collective-permute-start(f32[2,128,256]{2,1,0:T(8,128)} %param.7), channel_id=1, source_target_pairs={{0,24},{1,193},{2,26},{3,195},{4,28},{5,197},{6,30},{7,199},{8,0},... | collective-permute-start | bytes 786440 | tf_op jit(solution)/shard_map/ppermute | solution.py:38
  8.5 1.2 copy-start.18
  8.5 5.3 %copy-start.7 = (f32[2,128,256]{2,1,0:T(8,128)S(1)}, f32[2,128,256]{2,1,0:T(8,128)}, u32[]{:S(2)}) copy-start(f32[2,128,256]{2,1,0:T(8,128)} %param.7) | copy-start | bytes 786436
  10.7 2.4 %copy-start.10 = (f32[2,128,256]{2,1,0:T(8,128)}, f32[2,128,256]{2,1,0:T(8,128)S(1)}, u32[]{:S(2)}) copy-start(f32[2,128,256]{2,1,0:T(8,128)S(1)} %collective-permute-done) | copy-start | bytes 786436
  10.7 2.4 %copy-start.8 = (f32[2,128,256]{2,1,0:T(8,128)}, f32[2,128,256]{2,1,0:T(8,128)S(1)}, u32[]{:S(2)}) copy-start(f32[2,128,256]{2,1,0:T(8,128)S(1)} %collective-permute-done.1) | copy-start | bytes 786436
  13.1 0.7 copy-start.9
  13.9 12.0 %copy-start.4 = (f32[4,2,128,256]{3,2,1,0:T(8,128)}, f32[4,2,128,256]{3,2,1,0:T(8,128)S(1)}, u32[]{:S(2)}) copy-start(f32[4,2,128,256]{3,2,1,0:T(8,128)S(1)} %pad_maximum_fusion.refs_8_) | copy-start | bytes 3145732
  13.9 20.5 %collective-permute-start.3 = (f32[4,2,128,256]{3,2,1,0:T(8,128)S(1)}, f32[4,2,128,256]{3,2,1,0:T(8,128)S(1)}, u32[]{:S(2)}, u32[]{:S(2)}) collective-permute-start(f32[4,2,128,256]{3,2,1,0:T(8,128)S(1)} %pad_maximum_fusion.refs_8_), channel_id=1, source_target_pairs={{0,64},{1,9},{2,66},{3,11},{4,68},{5,13},{6,70},{7,15},{8,72},{9,1... | collective-permute-start | bytes 3145736 | tf_op jit(solution)/shard_map/ppermute | solution.py:38
  15.2 19.2 %collective-permute-start.4 = (f32[4,2,128,256]{3,2,1,0:T(8,128)S(1)}, f32[4,2,128,256]{3,2,1,0:T(8,128)S(1)}, u32[]{:S(2)}, u32[]{:S(2)}) collective-permute-start(f32[4,2,128,256]{3,2,1,0:T(8,128)S(1)} %pad_maximum_fusion.refs_8_), channel_id=1, source_target_pairs={{0,192},{1,25},{2,194},{3,27},{4,196},{5,29},{6,198},{7,31},{8,200... | collective-permute-start | bytes 3145736 | tf_op jit(solution)/shard_map/ppermute | solution.py:38
  19.2 15.2 %collective-permute-start.5 = (f32[2,2,128,256]{3,2,1,0:T(8,128)}, f32[2,2,128,256]{3,2,1,0:T(8,128)}, u32[]{:S(2)}, u32[]{:S(2)}) collective-permute-start(f32[2,2,128,256]{3,2,1,0:T(8,128)} %pad_maximum_fusion.1), channel_id=1, source_target_pairs={{0,32},{1,33},{2,34},{3,35},{4,36},{5,37},{6,38},{7,39},{8,40},{9,... | collective-permute-start | bytes 1572872 | tf_op jit(solution)/shard_map/ppermute | solution.py:50
  21.0 9.4 %copy-start.2 = (s32[32]{0:T(128)}, s32[32]{0:T(128)S(1)}, u32[]{:S(2)}) copy-start(s32[32]{0:T(128)S(1)} %convert_element_type.3) | copy-start | bytes 388
  25.4 26.0 %collective-permute-start.8 = (f32[2,2,128,256]{3,2,1,0:T(8,128)}, f32[2,2,128,256]{3,2,1,0:T(8,128)}, u32[]{:S(2)}, u32[]{:S(2)}) collective-permute-start(f32[2,2,128,256]{3,2,1,0:T(8,128)} %pad_maximum_fusion.2), channel_id=1, source_target_pairs={{0,32},{1,33},{2,34},{3,35},{4,36},{5,37},{6,38},{7,39},{8,40},{9,... | collective-permute-start | bytes 1572872 | tf_op jit(solution)/shard_map/ppermute | solution.py:50
  34.4 10.0 %copy-start.5 = (f32[4,2,128,256]{3,2,1,0:T(8,128)}, f32[4,2,128,256]{3,2,1,0:T(8,128)S(1)}, u32[]{:S(2)}) copy-start(f32[4,2,128,256]{3,2,1,0:T(8,128)S(1)} %collective-permute-done.3.refs_16_) | copy-start | bytes 3145732
  34.4 10.0 %copy-start.6 = (f32[4,2,128,256]{3,2,1,0:T(8,128)}, f32[4,2,128,256]{3,2,1,0:T(8,128)S(1)}, u32[]{:S(2)}) copy-start(f32[4,2,128,256]{3,2,1,0:T(8,128)S(1)} %collective-permute-done.4.refs_17_) | copy-start | bytes 3145732
  35.3 16.0 %collective-permute-start.10 = (f32[2,2,128,256]{3,2,1,0:T(8,128)}, f32[2,2,128,256]{3,2,1,0:T(8,128)}, u32[]{:S(2)}, u32[]{:S(2)}) collective-permute-start(f32[2,2,128,256]{3,2,1,0:T(8,128)} %slice.122), channel_id=1, source_target_pairs={{0,192},{1,25},{2,194},{3,27},{4,196},{5,29},{6,198},{7,31},{8,200... | collective-permute-start | bytes 1572872 | tf_op jit(solution)/shard_map/ppermute | solution.py:38
  37.6 13.8 %collective-permute-start.9 = (f32[2,2,128,256]{3,2,1,0:T(8,128)}, f32[2,2,128,256]{3,2,1,0:T(8,128)}, u32[]{:S(2)}, u32[]{:S(2)}) collective-permute-start(f32[2,2,128,256]{3,2,1,0:T(8,128)} %slice.121), channel_id=1, source_target_pairs={{0,64},{1,9},{2,66},{3,11},{4,68},{5,13},{6,70},{7,15},{8,72},{9,1... | collective-permute-start | bytes 1572872 | tf_op jit(solution)/shard_map/ppermute | solution.py:38
  41.2 16.9 %collective-permute-start.6 = (f32[2,2,128,256]{3,2,1,0:T(8,128)}, f32[2,2,128,256]{3,2,1,0:T(8,128)S(1)}, u32[]{:S(2)}, u32[]{:S(2)}) collective-permute-start(f32[2,2,128,256]{3,2,1,0:T(8,128)} %collective-permute-done.5.refs_18_), channel_id=1, source_target_pairs={{0,64},{1,9},{2,66},{3,11},{4,68},{5,13},{6,70},{7,15},{8,72},{9,1... | collective-permute-start | bytes 1572872 | tf_op jit(solution)/shard_map/ppermute | solution.py:38
  41.2 16.9 %collective-permute-start.7 = (f32[2,2,128,256]{3,2,1,0:T(8,128)}, f32[2,2,128,256]{3,2,1,0:T(8,128)S(1)}, u32[]{:S(2)}, u32[]{:S(2)}) collective-permute-start(f32[2,2,128,256]{3,2,1,0:T(8,128)} %collective-permute-done.5.refs_18_), channel_id=1, source_target_pairs={{0,192},{1,25},{2,194},{3,27},{4,196},{5,29},{6,198},{7,31},{8,200... | collective-permute-start | bytes 1572872 | tf_op jit(solution)/shard_map/ppermute | solution.py:38
  51.4 13.9 %collective-permute-start.12 = (f32[2,2,128,256]{3,2,1,0:T(8,128)}, f32[2,2,128,256]{3,2,1,0:T(8,128)S(1)}, u32[]{:S(2)}, u32[]{:S(2)}) collective-permute-start(f32[2,2,128,256]{3,2,1,0:T(8,128)} %collective-permute-done.8.refs_19_), channel_id=1, source_target_pairs={{0,64},{1,9},{2,66},{3,11},{4,68},{5,13},{6,70},{7,15},{8,72},{9,1... | collective-permute-start | bytes 1572872 | tf_op jit(solution)/shard_map/ppermute | solution.py:38
  51.4 13.8 %collective-permute-start.13 = (f32[2,2,128,256]{3,2,1,0:T(8,128)}, f32[2,2,128,256]{3,2,1,0:T(8,128)S(1)}, u32[]{:S(2)}, u32[]{:S(2)}) collective-permute-start(f32[2,2,128,256]{3,2,1,0:T(8,128)} %collective-permute-done.8.refs_19_), channel_id=1, source_target_pairs={{0,192},{1,25},{2,194},{3,27},{4,196},{5,29},{6,198},{7,31},{8,200... | collective-permute-start | bytes 1572872 | tf_op jit(solution)/shard_map/ppermute | solution.py:38
  58.1 7.1 %copy-start.11 = (f32[2,2,128,256]{3,2,1,0:T(8,128)}, f32[2,2,128,256]{3,2,1,0:T(8,128)S(1)}, u32[]{:S(2)}) copy-start(f32[2,2,128,256]{3,2,1,0:T(8,128)S(1)} %collective-permute-done.6.refs_16_) | copy-start | bytes 1572868
  58.1 7.1 %copy-start.12 = (f32[2,2,128,256]{3,2,1,0:T(8,128)}, f32[2,2,128,256]{3,2,1,0:T(8,128)S(1)}, u32[]{:S(2)}) copy-start(f32[2,2,128,256]{3,2,1,0:T(8,128)S(1)} %collective-permute-done.7.refs_17_) | copy-start | bytes 1572868
  58.1 21.2 %collective-permute-start.11 = (f32[2,2,128,256]{3,2,1,0:T(8,128)S(1)}, f32[2,2,128,256]{3,2,1,0:T(8,128)S(1)}, u32[]{:S(2)}, u32[]{:S(2)}) collective-permute-start(f32[2,2,128,256]{3,2,1,0:T(8,128)S(1)} %collective-permute-done.6.refs_16_), channel_id=1, source_target_pairs={{0,64},{1,9},{2,66},{3,11},{4,68},{5,13},{6,70},{7,15},{8,72},{9,1... | collective-permute-start | bytes 1572872 | tf_op jit(solution)/shard_map/ppermute | solution.py:38
  65.2 7.6 %copy-start.14 = (f32[2,2,128,256]{3,2,1,0:T(8,128)}, f32[2,2,128,256]{3,2,1,0:T(8,128)S(1)}, u32[]{:S(2)}) copy-start(f32[2,2,128,256]{3,2,1,0:T(8,128)S(1)} %collective-permute-done.12.refs_18_) | copy-start | bytes 1572868
  65.2 7.6 %copy-start.13 = (f32[2,2,128,256]{3,2,1,0:T(8,128)}, f32[2,2,128,256]{3,2,1,0:T(8,128)S(1)}, u32[]{:S(2)}) copy-start(f32[2,2,128,256]{3,2,1,0:T(8,128)S(1)} %collective-permute-done.13.refs_19_) | copy-start | bytes 1572868
  65.3 14.1 %collective-permute-start.14 = (f32[2,2,128,256]{3,2,1,0:T(8,128)S(1)}, f32[2,2,128,256]{3,2,1,0:T(8,128)S(1)}, u32[]{:S(2)}, u32[]{:S(2)}) collective-permute-start(f32[2,2,128,256]{3,2,1,0:T(8,128)S(1)} %collective-permute-done.13.refs_19_), channel_id=1, source_target_pairs={{0,192},{1,25},{2,194},{3,27},{4,196},{5,29},{6,198},{7,31},{8,200... | collective-permute-start | bytes 1572872 | tf_op jit(solution)/shard_map/ppermute | solution.py:38
  79.3 0.8 copy-start.15
  79.3 0.9 copy-start.16
  80.3 13.7 %copy-start.20 = (s32[2]{0:T(128)S(1)}, s32[2]{0:T(128)}, u32[]{:S(2)}) copy-start(s32[2]{0:T(128)} %get-tuple-element.132) | copy-start | bytes 28
  80.3 30.0 %copy-start.3 = (s32[32]{0:T(128)S(1)}, s32[32]{0:T(128)}, u32[]{:S(2)}) copy-start(s32[32]{0:T(128)} %copy-done.2) | copy-start | bytes 388
  80.3 39.0 %copy-start.17 = (f32[2,256]{1,0:T(2,128)S(1)}, f32[2,256]{1,0:T(2,128)}, u32[]{:S(2)}) copy-start(f32[2,256]{1,0:T(2,128)} %param.8) | copy-start | bytes 6148
  80.3 52.4 %copy-start.19 = (s32[2]{0:T(128)S(1)}, s32[2]{0:T(128)}, u32[]{:S(2)}) copy-start(s32[2]{0:T(128)} %param.10) | copy-start | bytes 28
  85.5 11.1 %collective-permute-start.18 = (f32[8,64,128]{2,1,0:T(8,128)}, f32[8,64,128]{2,1,0:T(8,128)S(1)}, u32[]{:S(2)}, u32[]{:S(2)}) collective-permute-start(f32[8,64,128]{2,1,0:T(8,128)} %get-tuple-element.88.n0), channel_id=1, source_target_pairs={{0,2},{1,3},{2,4},{3,5},{4,6},{5,7},{6,0},{7,1},{8,10},{9,11},{10,... | collective-permute-start | bytes 786440 | tf_op jit(solution)/shard_map/ppermute | solution.py:58
  88.4 14.0 %collective-permute-start.20 = (f32[8,64,128]{2,1,0:T(8,128)}, f32[8,64,128]{2,1,0:T(8,128)S(1)}, u32[]{:S(2)}, u32[]{:S(2)}) collective-permute-start(f32[8,64,128]{2,1,0:T(8,128)} %get-tuple-element.88.n0), channel_id=1, source_target_pairs={{0,6},{1,7},{2,0},{3,1},{4,2},{5,3},{6,4},{7,5},{8,14},{9,15},{10,... | collective-permute-start | bytes 786440 | tf_op jit(solution)/shard_map/ppermute | solution.py:58
  91.7 11.9 %collective-permute-start.15 = (f32[264,256]{1,0:T(8,128)}, f32[264,256]{1,0:T(8,128)S(1)}, u32[]{:S(2)}, u32[]{:S(2)}) collective-permute-start(f32[264,256]{1,0:T(8,128)} %get-tuple-element.87.v0), channel_id=1, source_target_pairs={{0,8},{1,9},{2,10},{3,11},{4,12},{5,13},{6,14},{7,15},{8,16},{9,17... | collective-permute-start | bytes 811016 | tf_op jit(solution)/shard_map/ppermute | solution.py:42
  92.7 10.9 %collective-permute-start.16 = (f32[264,256]{1,0:T(8,128)}, f32[264,256]{1,0:T(8,128)S(1)}, u32[]{:S(2)}, u32[]{:S(2)}) collective-permute-start(f32[264,256]{1,0:T(8,128)} %get-tuple-element.87.v0), channel_id=1, source_target_pairs={{0,16},{1,17},{2,18},{3,19},{4,20},{5,21},{6,22},{7,23},{8,24},{9,... | collective-permute-start | bytes 811016 | tf_op jit(solution)/shard_map/ppermute | solution.py:42
  94.0 9.5 %collective-permute-start.22 = (f32[8,64,128]{2,1,0:T(8,128)}, f32[8,64,128]{2,1,0:T(8,128)S(1)}, u32[]{:S(2)}, u32[]{:S(2)}) collective-permute-start(f32[8,64,128]{2,1,0:T(8,128)} %get-tuple-element.88.n0), channel_id=1, source_target_pairs={{0,1},{1,0},{2,3},{3,2},{4,5},{5,4},{6,7},{7,6},{8,9},{9,8},{10,11... | collective-permute-start | bytes 786440 | tf_op jit(solution)/shard_map/ppermute | solution.py:54
  96.6 9.7 %collective-permute-start.19 = (f32[4,64,128]{2,1,0:T(8,128)S(1)}, f32[4,64,128]{2,1,0:T(8,128)S(1)}, u32[]{:S(2)}, u32[]{:S(2)}) collective-permute-start(f32[4,64,128]{2,1,0:T(8,128)S(1)} %slice.166), channel_id=1, source_target_pairs={{0,2},{1,3},{2,4},{3,5},{4,6},{5,7},{6,0},{7,1},{8,10},{9,11},{10,... | collective-permute-start | bytes 393224 | tf_op jit(solution)/shard_map/ppermute | solution.py:58
  102.4 7.9 %collective-permute-start.21 = (f32[4,64,128]{2,1,0:T(8,128)S(1)}, f32[4,64,128]{2,1,0:T(8,128)S(1)}, u32[]{:S(2)}, u32[]{:S(2)}) collective-permute-start(f32[4,64,128]{2,1,0:T(8,128)S(1)} %slice.167), channel_id=1, source_target_pairs={{0,6},{1,7},{2,0},{3,1},{4,2},{5,3},{6,4},{7,5},{8,14},{9,15},{10,... | collective-permute-start | bytes 393224 | tf_op jit(solution)/shard_map/ppermute | solution.py:58
  103.4 7.6 %collective-permute-start.17 = (f32[264,256]{1,0:T(8,128)}, f32[264,256]{1,0:T(8,128)S(1)}, u32[]{:S(2)}, u32[]{:S(2)}) collective-permute-start(f32[264,256]{1,0:T(8,128)} %get-tuple-element.87.v0), channel_id=1, source_target_pairs={{0,24},{1,25},{2,26},{3,27},{4,28},{5,29},{6,30},{7,31},{8,0},{9,1... | collective-permute-start | bytes 811016 | tf_op jit(solution)/shard_map/ppermute | solution.py:42
  103.6 8.0 %collective-permute-start.23 = (f32[8,64,128]{2,1,0:T(8,128)S(1)}, f32[8,64,128]{2,1,0:T(8,128)S(1)}, u32[]{:S(2)}, u32[]{:S(2)}) collective-permute-start(f32[8,64,128]{2,1,0:T(8,128)S(1)} %collective-permute-done.18.n1), channel_id=1, source_target_pairs={{0,1},{1,0},{2,3},{3,2},{4,5},{5,4},{6,7},{7,6},{8,9},{9,8},{10,11... | collective-permute-start | bytes 786440 | tf_op jit(solution)/shard_map/ppermute | solution.py:54
  103.7 8.0 %collective-permute-start.26 = (f32[8,64,128]{2,1,0:T(8,128)S(1)}, f32[8,64,128]{2,1,0:T(8,128)S(1)}, u32[]{:S(2)}, u32[]{:S(2)}) collective-permute-start(f32[8,64,128]{2,1,0:T(8,128)S(1)} %collective-permute-done.20.n3), channel_id=1, source_target_pairs={{0,1},{1,0},{2,3},{3,2},{4,5},{5,4},{6,7},{7,6},{8,9},{9,8},{10,11... | collective-permute-start | bytes 786440 | tf_op jit(solution)/shard_map/ppermute | solution.py:54
  106.3 4.7 %collective-permute-start.24 = (f32[4,64,128]{2,1,0:T(8,128)S(1)}, f32[4,64,128]{2,1,0:T(8,128)S(1)}, u32[]{:S(2)}, u32[]{:S(2)}) collective-permute-start(f32[4,64,128]{2,1,0:T(8,128)S(1)} %collective-permute-done.19.n2a), channel_id=1, source_target_pairs={{0,1},{1,0},{2,3},{3,2},{4,5},{5,4},{6,7},{7,6},{8,9},{9,8},{10,11... | collective-permute-start | bytes 393224 | tf_op jit(solution)/shard_map/ppermute | solution.py:54
  110.3 1.3 collective-permute-start.25
  111.6 1.0 copy-start
  112.6 1.0 copy-start.1
  116.1 16.1 %collective-permute-start.27 = (f32[272,256]{1,0:T(8,128)}, f32[272,256]{1,0:T(8,128)S(1)}, u32[]{:S(2)}, u32[]{:S(2)}) collective-permute-start(f32[272,256]{1,0:T(8,128)} %get-tuple-element.90), channel_id=1, source_target_pairs={{0,64},{1,65},{2,66},{3,67},{4,68},{5,69},{6,70},{7,71},{8,72},{9,... | collective-permute-start | bytes 835592 | tf_op jit(solution)/shard_map/ppermute | solution.py:46
  116.1 16.1 %collective-permute-start.28 = (f32[272,256]{1,0:T(8,128)S(1)}, f32[272,256]{1,0:T(8,128)S(1)}, u32[]{:S(2)}, u32[]{:S(2)}) collective-permute-start(f32[272,256]{1,0:T(8,128)S(1)} %get-tuple-element.91), channel_id=1, source_target_pairs={{0,128},{1,129},{2,130},{3,131},{4,132},{5,133},{6,134},{7,135},{8... | collective-permute-start | bytes 835592 | tf_op jit(solution)/shard_map/ppermute | solution.py:46
  117.3 15.2 %collective-permute-start.29 = (f32[272,256]{1,0:T(8,128)S(1)}, f32[272,256]{1,0:T(8,128)S(1)}, u32[]{:S(2)}, u32[]{:S(2)}) collective-permute-start(f32[272,256]{1,0:T(8,128)S(1)} %get-tuple-element.92), channel_id=1, source_target_pairs={{0,192},{1,193},{2,194},{3,195},{4,196},{5,197},{6,198},{7,199},{8... | collective-permute-start | bytes 835592 | tf_op jit(solution)/shard_map/ppermute | solution.py:46
  132.6 5.2 %collective-permute-start.30 = (f32[144,256]{1,0:T(8,128)S(1)}, f32[144,256]{1,0:T(8,128)S(1)}, u32[]{:S(2)}, u32[]{:S(2)}) collective-permute-start(f32[144,256]{1,0:T(8,128)S(1)} %get-tuple-element.94), channel_id=1, source_target_pairs={{0,32},{1,33},{2,34},{3,35},{4,36},{5,37},{6,38},{7,39},{8,40},{9,... | collective-permute-start | bytes 442376 | tf_op jit(solution)/shard_map/ppermute | solution.py:50

commit v3 on v2

v3 whole, which is shorter than its diff:
```python
import functools

import jax
import jax.numpy as jnp
from jax import lax
from jax.experimental import pallas as pl
from jax.experimental.pallas import tpu as pltpu
from jax.sharding import PartitionSpec as P

AXES = ("cube", "col")
F32 = jnp.float32
VMEM = pltpu.VMEM
SMEM = pltpu.SMEM
VLIM = 24
COST = 4


def index_of(x, y, zl, zh, core):
    return ((y * 2 + zl) * 4 + x) * 8 + zh * 2 + core


def table(move):
    pairs = []
    for y in range(4):
        for zl in range(2):
            for x in range(4):
                for zh in range(4):
                    for core in range(2):
                        pairs.append(
                            (index_of(x, y, zl, zh, core), index_of(*move(x, y, zl, zh, core)))
                        )
    return pairs


def send_pq(v, dp, dq):
    def move(x, y, zl, zh, core):
        dx, dy = (dp, dq) if core == 0 else (dq, dp)
        return (x + dx) % 4, (y + dy) % 4, zl, zh, core

    return lax.ppermute(v, AXES, table(move))


def send_x(v, d):
    return lax.ppermute(v, AXES, table(lambda x, y, zl, zh, core: ((x + d) % 4, y, zl, zh, core)))


def send_x_flip(v, bit):
    return lax.ppermute(v, AXES, table(lambda x, y, zl, zh, core: (x ^ bit, y, zl, zh, core)))


def send_y(v, d):
    return lax.ppermute(v, AXES, table(lambda x, y, zl, zh, core: (x, (y + d) % 4, zl, zh, core)))


def send_pair(v):
    return lax.ppermute(v, AXES, table(lambda x, y, zl, zh, core: (x, y, 1 - zl, zh, core)))


def send_core(v):
    return lax.ppermute(v, AXES, table(lambda x, y, zl, zh, core: (x, y, zl, zh, 1 - core)))


def send_zh(v, d):
    return lax.ppermute(v, AXES, table(lambda x, y, zl, zh, core: (x, y, zl, (zh + d) % 4, core)))


def split(a):
    hi = a.astype(jnp.bfloat16)
    lo = (a - hi.astype(F32)).astype(jnp.bfloat16)
    return hi, lo


def dot3(a, b, dims):
    ah, al = split(a)
    bh, bl = split(b)
    dg = functools.partial(lax.dot_general, dimension_numbers=(dims, ((), ())),
                           preferred_element_type=F32)
    return dg(ah, bh) + (dg(ah, bl) + dg(al, bh))


def plan_kernel(tile_map, counts, assign, cb, meta, info):
    me, col = lax.axis_index("cube"), lax.axis_index("col")
    x, zl, y = lax.rem(me, 4), lax.rem(lax.div(me, 4), 2), lax.div(me, 8)
    zh, core = lax.div(col, 2), lax.rem(col, 2)
    group = (y * 2 + zl) * 4
    flip = jnp.where(assign[0] != 0, 1, 0)
    for i, value in enumerate((x, y, zl, zh, core)):
        info[i] = value

    def fill(i, _):
        s, dp, dq, plane = i & 1, (i >> 1) & 3, (i >> 3) & 3, i >> 5
        dx = jnp.where(core == 0, dp, dq)
        dy = jnp.where(core == 0, dq, dp)
        src = (((y - dy) & 3) * 2 + ((zl + plane) & 1)) * 4 + ((x - dx) & 3)
        front = s ^ flip
        tile = tile_map[front, src >> 1]
        cb[i] = tile * 2 + (src & 1)
        live = jnp.clip(counts[front] - src * 128, 0, 128)
        meta[i] = live

        @pl.when((tile >= group) & (tile < group + 4))
        def _():
            piece = (tile - group) * 2 + (src & 1)
            meta[64 + piece] = i
            meta[72 + piece] = live

        return 0

    lax.fori_loop(0, 64, fill, 0)

    def look(i, _):
        front, j = i >> 4, i & 15
        tile = tile_map[front, j]

        @pl.when((tile >= group) & (tile < group + 4))
        def _():
            info[5 + ((x ^ tile) & 3)] = front ^ flip

        @pl.when(tile == me)
        def _():
            info[9] = front
            info[10] = jnp.clip(counts[front] - j * 256, 0, 256)

        return 0

    lax.fori_loop(0, 32, look, 0)
    info[11] = flip
    info[12] = me


def plan_call(tile_map, counts, assign):
    spec = pl.BlockSpec(memory_space=SMEM)
    return pl.pallas_call(
        plan_kernel,
        in_specs=[spec] * 3,
        out_specs=[spec] * 3,
        out_shape=[jax.ShapeDtypeStruct((size,), jnp.int32) for size in (64, 80, 16)],
        name="plan",
    )(tile_map, counts, assign)


def u_kernel(first, groups, meta, info, *refs):
    us, refs = refs[:len(groups)], refs[len(groups):]
    if not first:
        (own_in, ut_in), refs = refs[:2], refs[2:]
    own, ut, buf, turned, sem = refs

    def each(do):
        for piece in range(8):
            place = meta[64 + piece]
            for u, (base, size) in zip(us, groups):
                @pl.when((place >= base * 2) & (place < (base + size) * 2))
                def _():
                    at = place - base * 2
                    do(piece, pltpu.make_async_copy(u.at[at >> 1, at & 1], buf.at[piece],
                                                    sem.at[piece]))

    each(lambda piece, copy: copy.start())
    if first:
        own[...] = jnp.zeros_like(own)
        ut[...] = jnp.zeros_like(ut)
    else:
        own[...] = own_in[...]
        ut[...] = ut_in[...]
    x = info[0]
    rows = lax.broadcasted_iota(jnp.int32, (128, 256), 0)

    def take(piece, copy):
        copy.wait()
        part = jnp.where(rows < meta[72 + piece], buf[piece], 0.0)
        turned[...] = part.T
        ut[piece] = turned[pl.ds(pl.multiple_of(x * 64, 64), 64), :]

        @pl.when(x == piece // 2)
        def _():
            half = piece % 2
            own[half * 128:(half + 1) * 128, :] = part

    each(take)


def u_call(plan, us, starts, carry):
    groups = tuple((start, u.shape[0]) for start, u in zip(starts, us))
    first = carry is None
    smem, vmem, anywhere = (pl.BlockSpec(memory_space=m) for m in (SMEM, VMEM, pl.ANY))
    at = 2 + len(us)
    return pl.pallas_call(
        functools.partial(u_kernel, first, groups),
        in_specs=[smem] * 2 + [anywhere] * len(us) + ([] if first else [vmem] * 2),
        out_specs=[vmem] * 2,
        out_shape=[jax.ShapeDtypeStruct((256, 256), F32), jax.ShapeDtypeStruct((8, 64, 128), F32)],
        scratch_shapes=[VMEM((8, 128, 256), F32), VMEM((256, 128), F32),
                        pltpu.SemaphoreType.DMA((8,))],
        input_output_aliases={} if first else {at: 0, at + 1: 1},
        compiler_params=pltpu.CompilerParams(vmem_limit_bytes=16 * 2**20),
        name="u_rows",
    )(*plan[1:], *us, *(() if first else carry))


def v_kernel(first, last, groups, cb, meta, info, *refs):
    ginv, refs = refs[0], refs[1:]
    us, refs = refs[:len(groups)], refs[len(groups):]
    if not first:
        v_in, refs = refs[0], refs[1:]
    if last:
        own, refs = refs[0], refs[1:]
    v_out = refs[0]
    gbuf, ubuf, gsem, usem = refs[-4:]
    copies = []
    at = 0
    for i, (base, size) in enumerate(groups):
        mine = [pltpu.make_async_copy(us[i], ubuf.at[pl.ds(at, size)], usem.at[i])]
        for b in range(size):
            for s in range(2):
                column = pl.multiple_of(cb[(base + b) * 2 + s] * 128, 128)
                mine.append(pltpu.make_async_copy(
                    ginv.at[:, pl.ds(column, 128)],
                    gbuf.at[s, :, pl.ds((at + b) * 128, 128)],
                    gsem.at[(at + b) * 2 + s]))
        for c in mine:
            c.start()
        copies.append(mine)
        at += size
    rows = lax.broadcasted_iota(jnp.int32, (128, 256), 0)
    at = 0
    for i, (base, size) in enumerate(groups):
        for c in copies[i]:
            c.wait()
        for s in range(2):
            uu = jnp.concatenate(
                [jnp.where(rows < meta[(base + b) * 2 + s], ubuf[at + b, s], 0.0)
                 for b in range(size)], axis=0)
            gg = gbuf[s, :, at * 128:(at + size) * 128]
            part = dot3(gg, uu, ((1,), (0,)))
            if i > 0:
                part += v_out[s]
            elif not first:
                part += v_in[s]
            v_out[s] = part
        at += size
    if last:
        msg = refs[1]
        v_own = v_out[info[9] ^ info[11]]
        msg[:256, :] = v_own
        diag = jnp.sum(own[...] * v_own, axis=0, keepdims=True)
        msg[256:264, :] = jnp.broadcast_to(diag, (8, 256))


def v_call(ginv, plan, us, starts, carry, own=None):
    groups = tuple((start, u.shape[0]) for start, u in zip(starts, us))
    n = sum(size for _, size in groups)
    first, last = carry is None, own is not None
    shapes = [(2, 256, 256)]
    smem, vmem, anywhere = (pl.BlockSpec(memory_space=m) for m in (SMEM, VMEM, pl.ANY))
    extra = [t for t in (carry, own) if t is not None]
    if last:
        shapes.append((264, 256))
    out = pl.pallas_call(
        functools.partial(v_kernel, first, last, groups),
        in_specs=[smem] * 3 + [pl.BlockSpec(memory_space=pltpu.HBM)] + [anywhere] * len(us)
        + [vmem] * len(extra),
        out_specs=[vmem] * len(shapes),
        out_shape=[jax.ShapeDtypeStruct(shape, F32) for shape in shapes],
        scratch_shapes=[VMEM((2, 256, n * 128), F32), VMEM((n, 2, 128, 256), F32),
                        pltpu.SemaphoreType.DMA((2 * n,)), pltpu.SemaphoreType.DMA((len(us),))],
        compiler_params=pltpu.CompilerParams(vmem_limit_bytes=VLIM * 2**20),
        cost_estimate=pl.CostEstimate(flops=3 * 4 * 256 * 128 * n * 256,
                                      bytes_accessed=n * COST * 2**20, transcendentals=0),
        name="v_part",
    )(*plan, ginv, *us, *extra)
    return out if last else out[0]


def prod_kernel(pos, v0, v1, v2, v3, near, near2, far, far2, m0, m1, m2, m3, acc):
    x, y, zl, zh, core = pos[0], pos[1], pos[2], pos[3], pos[4]
    acc[...] = jnp.zeros_like(acc)
    vs = (v0, v1, v2, v3)
    order = [(k, side) for k in range(4) for side in range(2)]
    for t in range(4):
        tile = x ^ t
        left = []
        for k, side in order:
            u = (near2, far2)[side] if k == 2 else (near, far)[side].at[(0, 1, None, 2)[k]]
            left.append(jnp.concatenate([u[tile * 2 + h] for h in range(2)], axis=1))
        part = dot3(jnp.concatenate(left, axis=0), vs[t][:256, :], ((1,), (0,)))
        s = pos[5 + t]
        for i, (k, side) in enumerate(order):
            block = lax.rem(zh + 4 - k, 4) * 2 + (core if side == 0 else 1 - core)
            acc[s, block] += part[i * 64:(i + 1) * 64, :]
    diag = []
    for s in range(2):
        total = None
        for t in range(4):
            term = jnp.where(pos[5 + t] == s, vs[t][256:264, :], 0.0)
            total = term if total is None else total + term
        diag.append(total)
    for k, m in enumerate((m0, m1, m2, m3)):
        for zrel in range(2):
            for s in range(2):
                block = 2 * lax.rem(y + k, 4) + lax.rem(zl + zrel, 2)
                at = (zrel * 2 + s) * 64
                m[at:at + 64, :] = acc[s, block]
        m[256:264, :] = diag[0]
        m[264:272, :] = diag[1]


def prod_call(pos, vs, pieces):
    spec = pl.BlockSpec(memory_space=VMEM)
    return pl.pallas_call(
        prod_kernel,
        in_specs=[pl.BlockSpec(memory_space=SMEM)] + [spec] * 8,
        out_specs=[spec] * 4,
        out_shape=[jax.ShapeDtypeStruct((272, 256), F32)] * 4,
        scratch_shapes=[VMEM((2, 8, 64, 256), F32)],
        compiler_params=pltpu.CompilerParams(vmem_limit_bytes=24 * 2**20),
        cost_estimate=pl.CostEstimate(flops=3 * 2 * 512 * 1024 * 256, bytes_accessed=5 * 2**20,
                                      transcendentals=0),
        name="product",
    )(pos, *vs, *pieces)


def sum2_kernel(r0, r1, r2, r3, keep, away):
    for rows, o, to in ((0, keep, 0), (128, away, 0)):
        o[to:to + 128, :] = (r0[rows:rows + 128, :] + r1[rows:rows + 128, :]) + (
            r2[rows:rows + 128, :] + r3[rows:rows + 128, :])
    d = (r0[256:272, :] + r1[256:272, :]) + (r2[256:272, :] + r3[256:272, :])
    keep[128:144, :] = d
    away[128:144, :] = d


def sum2_call(rs):
    spec = pl.BlockSpec(memory_space=VMEM)
    return pl.pallas_call(
        sum2_kernel,
        in_specs=[spec] * 4,
        out_specs=[spec] * 2,
        out_shape=[jax.ShapeDtypeStruct((144, 256), F32)] * 2,
        compiler_params=pltpu.CompilerParams(vmem_limit_bytes=16 * 2**20),
        name="sum_second",
    )(*rs)


def cross_kernel(info, v, block, cross, base):
    flip = info[11]
    eye = lax.broadcasted_iota(jnp.int32, (256, 256), 0) == lax.broadcasted_iota(
        jnp.int32, (256, 256), 1)
    g_diag = jnp.sum(jnp.where(eye, block[...], 0.0), axis=1, keepdims=True)
    for f in range(2):
        vf = v[f ^ flip]
        cross[f] = -vf
        base[f] = g_diag + 2.0 * vf


def cross_call(info, v, ginv):
    full = pl.BlockSpec((2, 256, 256), lambda _, info: (0, 0, 0))
    return pl.pallas_call(
        cross_kernel,
        grid_spec=pltpu.PrefetchScalarGridSpec(
            num_scalar_prefetch=1, grid=(1,),
            in_specs=[full, pl.BlockSpec((256, 256), lambda _, info: (0, info[12]))],
            out_specs=[full, full],
        ),
        out_shape=[jax.ShapeDtypeStruct((2, 256, 256), F32)] * 2,
        name="cross",
    )(info, v, ginv)


def last_kernel(info, keep, came, dinv, base, resist, sigma):
    flip = info[11]
    rows = lax.broadcasted_iota(jnp.int32, (256, 256), 0)
    at = lax.broadcasted_iota(jnp.int32, (64, 256), 0) + lax.rem(info[12], 4) * 64
    on_diag = at == lax.broadcasted_iota(jnp.int32, (64, 256), 1)
    on_diag = on_diag & (info[12] // 4 == info[3] * 2 + info[4])
    for f in range(2):
        s = f ^ flip
        d = dinv[pl.ds(s, 1), :]
        total = keep[pl.ds(pl.multiple_of(s * 64, 64), 64), :] + came[
            pl.ds(pl.multiple_of(s * 64, 64), 64), :]
        sigma[:, f, :] = total + jnp.where(on_diag, d, 0.0)
        deep = pl.ds(pl.multiple_of(128 + s * 8, 8), 8)
        diag = (keep[deep, :] + came[deep, :])[0:1, :] + d
        live = jnp.where(info[9] == f, info[10], 0)
        resist[f] = jnp.where(rows < live, diag + base[f], 0.0)


def last_call(info, keep, came, dinv, base):
    spec = pl.BlockSpec(memory_space=VMEM)
    return pl.pallas_call(
        last_kernel,
        in_specs=[pl.BlockSpec(memory_space=SMEM)] + [spec] * 4,
        out_specs=[spec] * 2,
        out_shape=[jax.ShapeDtypeStruct((2, 256, 256), F32), jax.ShapeDtypeStruct((64, 2, 256), F32)],
        name="last",
    )(info, keep, came, dinv, base)


def body(ginv, ufactor, dinv, tile_map, counts, assign):
    pin = lax.optimization_barrier

    a0 = ufactor
    b0 = send_pair(a0)
    ga = jnp.stack([a0, send_pq(a0, 1, 0), send_pq(a0, 2, 0), send_pq(a0, -1, 0)])
    ga, tile_map = pin((ga, tile_map))
    ga1 = send_pq(ga, 0, 1)
    ga3 = send_pq(ga, 0, -1)
    plan = plan_call(tile_map, counts, assign)
    info = plan[2]
    *b, plan = pin([b0, send_pq(b0, 1, 0), send_pq(b0, 2, 0), send_pq(b0, -1, 0), plan])
    gb = jnp.stack(b)
    gb1 = send_pq(gb, 0, 1)
    gb3 = send_pq(gb, 0, -1)
    carry = v_call(ginv, plan, [ga, gb], [0, 16], None)
    ga1, ga3, carry = pin((ga1, ga3, carry))
    ga2a = send_pq(ga1[:2], 0, 1)
    ga2b = send_pq(ga3[2:], 0, -1)
    carry = v_call(ginv, plan, [ga1, ga3], [4, 12], carry)
    gb1, gb3, carry = pin((gb1, gb3, carry))
    gb2a = send_pq(gb1[:2], 0, 1)
    gb2b = send_pq(gb3[2:], 0, -1)
    carry = v_call(ginv, plan, [gb1, gb3, ga2a, ga2b], [20, 28, 8, 10], carry)
    rows = u_call(plan, [ga, gb, ga1, ga3, gb1, gb3, ga2a, ga2b],
                  [0, 16, 4, 12, 20, 28, 8, 10], None)
    gb2a, gb2b, carry, rows = pin((gb2a, gb2b, carry, rows))
    own, ut = u_call(plan, [gb2a, gb2b], [24, 26], rows)

    c1, c3 = send_zh(ut, 1), send_zh(ut, -1)
    v, msg = v_call(ginv, plan, [gb2a, gb2b], [24, 26], carry, own)
    v1, v2 = send_x_flip(msg, 1), send_x_flip(msg, 2)
    c1, c3, ut, v1, v2 = pin((c1, c3, ut, v1, v2))
    vs = [msg, v1, v2, send_x_flip(v1, 2)]
    c2 = jnp.concatenate([send_zh(c1[:4], 1), send_zh(c3[4:], -1)])
    near = [jnp.stack([ut, c1, c3]), c2]
    far = [send_core(t) for t in near]
    cross, base = cross_call(info, v, ginv)

    m = prod_call(info, vs, near + far)
    r = [m[0], send_y(m[1], 1), send_y(m[2], 2), send_y(m[3], -1)]
    keep, away = sum2_call(r)
    came = send_pair(away)
    resist, sigma = last_call(info, keep, came, dinv, base)
    return cross, resist, sigma


def solution(mesh):
    in_specs = (P("cube", None), P(None, "cube", "col"), P(None, "col"), P(), P(), P())
    out_specs = (P(None, "cube", "col"), P(None, "cube", "col"), P("cube", None, "col"))
    return jax.shard_map(body, mesh=mesh, in_specs=in_specs, out_specs=out_specs, check_vma=False)
```

time: 144 us -> 125 us (0.87)
  other arithmetic: 16.3 us -> 2.26 us
  local copies, waits for them, and re-layouts: 16.7 us -> 6.79 us
  waiting for transfers between devices: 32.8 us -> 42.4 us
  Pallas kernels: 32.7 us -> 24.9 us
  starting transfers between devices: 41.3 us -> 45.6 us
    ppermute x4, waiting for transfers between devices: 8.73 us -> 18.2 us  [send_zh(): lax.ppermute(v, AXES, table(lambda x, y, zl, zh, core: (x, y, zl, (zh + d...]
    pallas_call x5 -> x9, Pallas kernels: 30.1 us -> 23 us  [the longest x4 10.4 us: v_call(): pl.pallas_call(functools.partial(v_kernel, first, last, groups), in_specs...]
    concatenate x7 -> x0, other arithmetic: 6.22 us -> none  [the longest x3 3.79 us: part(): jnp.concatenate([pick(meta), jnp.stack([x, s_own]).astype(jnp.int32)])]
    ppermute x13 -> x14, waiting for transfers between devices: 2.4 us -> 8.23 us  [send_pq(): return lax.ppermute(v, AXES, table(move))]
    ppermute x3 -> x2, waiting for transfers between devices: 9.04 us -> 3.22 us  [send_pair(): lax.ppermute(v, AXES, table(lambda x, y, zl, zh, core: (x, y, 1 - zl, zh,...]
    ppermute x4, starting transfers between devices: 13 us -> 9.69 us  [send_zh(): lax.ppermute(v, AXES, table(lambda x, y, zl, zh, core: (x, y, zl, (zh + d...]
    unnamed x42 -> x17, local copies, waits for them, and re-layouts: 3.64 us -> 6.62 us
    ppermute x13 -> x14, starting transfers between devices: 20.1 us -> 22.9 us  [send_pq(): return lax.ppermute(v, AXES, table(move))]
  transfers between devices with their start and end apart: 31 -> 28, of which waited for: 9 -> 14; matrix products, arithmetic and copies ran while one was open for 18% -> 2% of each run, Pallas kernels for 18% -> 15%
where the time goes in v3:
time: 125 us; the launch traced here: 123 us
  starting transfers between devices  45.6 us (36%)
  waiting for transfers between devices  42.4 us (34%)
  Pallas kernels  24.9 us (20%)
  local copies, waits for them, and re-layouts  6.79 us (5%)
  other arithmetic  2.26 us (2%)
    ppermute x14, starting transfers between devices, send_pq(): return lax.ppermute(v, AXES, table(move))  22.9 us
    ppermute x4, waiting for transfers between devices, send_zh(): lax.ppermute(v, AXES, table(lambda x, y, zl, zh, core: (x, y, zl, (zh + d...  18.2 us
    ppermute x3, waiting for transfers between devices, send_y(): lax.ppermute(v, AXES, table(lambda x, y, zl, zh, core: (x, (y + d) % 4, z...  11.3 us
    pallas_call x4, Pallas kernels, v_call(): pl.pallas_call(functools.partial(v_kernel, first, last, groups), in_specs...  10.4 us
    ppermute x4, starting transfers between devices, send_zh(): lax.ppermute(v, AXES, table(lambda x, y, zl, zh, core: (x, y, zl, (zh + d...  9.69 us
    ppermute x14, waiting for transfers between devices, send_pq(): return lax.ppermute(v, AXES, table(move))  8.23 us
    unnamed x17, local copies, waits for them, and re-layouts  6.62 us
    ppermute x3, starting transfers between devices, send_y(): lax.ppermute(v, AXES, table(lambda x, y, zl, zh, core: (x, (y + d) % 4, z...  5.79 us
  transfers between devices with their start and end apart: 28, of which 14 were waited for; matrix products, arithmetic and copies ran while one was open for 2% of the time, Pallas kernels for 15%

profile of v3, /device:TPU:2, one launch (start us, length us, event | category | flops | bytes accessed | tf_op | source)
XLA Modules:
  0.0 122.9 jit_solution(15655210937240134866)
XLA Ops:
  0.6 2.0 %collective-permute-start.3 = (f32[2,128,256]{2,1,0:T(8,128)}, f32[2,128,256]{2,1,0:T(8,128)S(1)}, u32[]{:S(2)}, u32[]{:S(2)}) collective-permute-start(f32[2,128,256]{2,1,0:T(8,128)} %param.7), channel_id=1, source_target_pairs={{0,32},{1,33},{2,34},{3,35},{4,36},{5,37},{6,38},{7,39},{8,40},{9,... | collective-permute-start | bytes 786440 | tf_op jit(solution)/shard_map/ppermute | solution.py:56
  2.6 1.5 %collective-permute-start = (f32[2,128,256]{2,1,0:T(8,128)}, f32[2,128,256]{2,1,0:T(8,128)S(1)}, u32[]{:S(2)}, u32[]{:S(2)}) collective-permute-start(f32[2,128,256]{2,1,0:T(8,128)} %param.7), channel_id=1, source_target_pairs={{0,8},{1,65},{2,10},{3,67},{4,12},{5,69},{6,14},{7,71},{8,16},{9,7... | collective-permute-start | bytes 786440 | tf_op jit(solution)/shard_map/ppermute | solution.py:40
  4.1 1.1 collective-permute-start.1
  5.2 2.2 %collective-permute-start.2 = (f32[2,128,256]{2,1,0:T(8,128)}, f32[2,128,256]{2,1,0:T(8,128)S(1)}, u32[]{:S(2)}, u32[]{:S(2)}) collective-permute-start(f32[2,128,256]{2,1,0:T(8,128)} %param.7), channel_id=1, source_target_pairs={{0,24},{1,193},{2,26},{3,195},{4,28},{5,197},{6,30},{7,199},{8,0},... | collective-permute-start | bytes 786440 | tf_op jit(solution)/shard_map/ppermute | solution.py:40
  7.4 1.8 %collective-permute-done.3 = f32[2,128,256]{2,1,0:T(8,128)S(1)} collective-permute-done((f32[2,128,256]{2,1,0:T(8,128)}, f32[2,128,256]{2,1,0:T(8,128)S(1)}, u32[]{:S(2)}, u32[]{:S(2)}) %collective-permute-start.3) | collective-permute-done | bytes 262176 | tf_op jit(solution)/shard_map/ppermute | solution.py:56
  9.2 1.5 %collective-permute-start.4 = (f32[2,128,256]{2,1,0:T(8,128)S(1)}, f32[2,128,256]{2,1,0:T(8,128)}, u32[]{:S(2)}, u32[]{:S(2)}) collective-permute-start(f32[2,128,256]{2,1,0:T(8,128)S(1)} %collective-permute-done.3), channel_id=1, source_target_pairs={{0,8},{1,65},{2,10},{3,67},{4,12},{5,69},{6,14},{7,71},{8,16},{9,7... | collective-permute-start | bytes 786440 | tf_op jit(solution)/shard_map/ppermute | solution.py:40
  10.6 1.1 collective-permute-start.5
  11.8 0.0 collective-permute-done
  11.8 2.2 %collective-permute-start.6 = (f32[2,128,256]{2,1,0:T(8,128)S(1)}, f32[2,128,256]{2,1,0:T(8,128)}, u32[]{:S(2)}, u32[]{:S(2)}) collective-permute-start(f32[2,128,256]{2,1,0:T(8,128)S(1)} %collective-permute-done.3), channel_id=1, source_target_pairs={{0,24},{1,193},{2,26},{3,195},{4,28},{5,197},{6,30},{7,199},{8,0},... | collective-permute-start | bytes 786440 | tf_op jit(solution)/shard_map/ppermute | solution.py:40
  13.9 0.7 collective-permute-done.2
  14.6 1.0 pad_maximum_fusion.refs_1_.refs_0_
  15.7 3.1 %collective-permute-start.10 = (f32[4,2,128,256]{3,2,1,0:T(8,128)S(1)}, f32[4,2,128,256]{3,2,1,0:T(8,128)S(1)}, u32[]{:S(2)}, u32[]{:S(2)}) collective-permute-start(f32[4,2,128,256]{3,2,1,0:T(8,128)S(1)} %pad_maximum_fusion.refs_1_.refs_0_), channel_id=1, source_target_pairs={{0,192},{1,25},{2,194},{3,27},{4,196},{5,29},{6,198},{7,31},{8,200... | collective-permute-start | bytes 3145736 | tf_op jit(solution)/shard_map/ppermute | solution.py:40
  18.8 0.0 collective-permute-start.9
  18.8 3.3 %plan.1 = (s32[64]{0:T(128)}, s32[80]{0:T(128)}, s32[16]{0:T(128)}) custom-call(s32[2,16]{1,0:T(2,128)} %tile_map, s32[2]{0:T(128)} %counts.1, s32[2]{0:T(128)} %assign.1), custom_call_target="tpu_custom_call" | custom-call | tf_op jit(solution)/shard_map/plan/pallas_call | solution.py:133
  22.1 1.2 %collective-permute-done.6 = f32[2,128,256]{2,1,0:T(8,128)} collective-permute-done((f32[2,128,256]{2,1,0:T(8,128)S(1)}, f32[2,128,256]{2,1,0:T(8,128)}, u32[]{:S(2)}, u32[]{:S(2)}) %collective-permute-start.6) | collective-permute-done | bytes 262176 | tf_op jit(solution)/shard_map/ppermute | solution.py:40
  23.3 1.2 pad_maximum_fusion.1.refs_2_.refs_1_
  24.5 1.7 %collective-permute-start.7 = (f32[4,2,128,256]{3,2,1,0:T(8,128)S(1)}, f32[4,2,128,256]{3,2,1,0:T(8,128)S(1)}, u32[]{:S(2)}, u32[]{:S(2)}) collective-permute-start(f32[4,2,128,256]{3,2,1,0:T(8,128)S(1)} %pad_maximum_fusion.1.refs_2_.refs_1_), channel_id=1, source_target_pairs={{0,64},{1,9},{2,66},{3,11},{4,68},{5,13},{6,70},{7,15},{8,72},{9,1... | collective-permute-start | bytes 3145736 | tf_op jit(solution)/shard_map/ppermute | solution.py:40
  26.2 1.7 %collective-permute-start.8 = (f32[4,2,128,256]{3,2,1,0:T(8,128)S(1)}, f32[4,2,128,256]{3,2,1,0:T(8,128)S(1)}, u32[]{:S(2)}, u32[]{:S(2)}) collective-permute-start(f32[4,2,128,256]{3,2,1,0:T(8,128)S(1)} %pad_maximum_fusion.1.refs_2_.refs_1_), channel_id=1, source_target_pairs={{0,192},{1,25},{2,194},{3,27},{4,196},{5,29},{6,198},{7,31},{8,200... | collective-permute-start | bytes 3145736 | tf_op jit(solution)/shard_map/ppermute | solution.py:40
  27.8 3.4 %copy-done = f32[256,8192]{1,0:T(8,128)S(1)} copy-done((f32[256,8192]{1,0:T(8,128)S(1)}, f32[256,8192]{1,0:T(8,128)}, u32[]{:S(2)}) %copy-start) | copy-done | bytes 8388632
  31.2 0.6 copy-done.3
  31.8 0.7 copy-done.5
  32.5 0.7 copy-done.6
  33.1 2.5 %v_part.4.refs_3_ = f32[2,256,256]{2,1,0:T(8,128)S(1)} custom-call(s32[64]{0:T(128)S(1)} %copy-done.6, s32[80]{0:T(128)S(1)} %copy-done.5, s32[16]{0:T(128)S(1)} %copy-done.3, f32[256,8192]{1,0:T(8,128)S(1)} %copy-done, f32[4,2,128,256]{3,2,1,0:T(8,128)S(1)} %pad_maximum_fusion.refs_1_.refs_0_, f32[4,2,128,256]{3,2,1,0:T(8,128)S(1)} %pad_maximum_fusion.1.refs_2_.refs_1_), custom_call_target="tpu_custom_call" | custom-call | flops 805306368 | bytes 33554432 | tf_op jit(solution)/shard_map/v_part/pallas_call | solution.py:258
  35.7 0.5 collective-permute-start.13
  36.2 3.1 %collective-permute-start.14 = (f32[2,2,128,256]{3,2,1,0:T(8,128)S(1)}, f32[2,2,128,256]{3,2,1,0:T(8,128)S(1)}, u32[]{:S(2)}, u32[]{:S(2)}) collective-permute-start(f32[2,2,128,256]{3,2,1,0:T(8,128)S(1)} %slice.21), channel_id=1, source_target_pairs={{0,192},{1,25},{2,194},{3,27},{4,196},{5,29},{6,198},{7,31},{8,200... | collective-permute-start | bytes 1572872 | tf_op jit(solution)/shard_map/ppermute | solution.py:40
  39.3 2.6 %v_part.5.refs_5_ = f32[2,256,256]{2,1,0:T(8,128)S(1)} custom-call(s32[64]{0:T(128)S(1)} %copy-done.6, s32[80]{0:T(128)S(1)} %copy-done.5, s32[16]{0:T(128)S(1)} %copy-done.3, f32[256,8192]{1,0:T(8,128)S(1)} %copy-done, f32[4,2,128,256]{3,2,1,0:T(8,128)S(1)} %collective-permute-done.9.refs_1_.refs_2_, ...), custom_call_target="tpu_custom_call" | custom-call | flops 805306368 | bytes 33554432 | tf_op jit(solution)/shard_map/v_part/pallas_call | solution.py:258
  41.9 4.1 %collective-permute-done.7.refs_1_.refs_4_ = f32[4,2,128,256]{3,2,1,0:T(8,128)S(1)} collective-permute-done((f32[4,2,128,256]{3,2,1,0:T(8,128)S(1)}, f32[4,2,128,256]{3,2,1,0:T(8,128)S(1)}, u32[]{:S(2)}, u32[]{:S(2)}) %collective-permute-start.7) | collective-permute-done | bytes 1048608 | tf_op jit(solution)/shard_map/ppermute | solution.py:40
  46.0 0.1 collective-permute-start.11
  46.2 3.3 %collective-permute-start.12 = (f32[2,2,128,256]{3,2,1,0:T(8,128)S(1)}, f32[2,2,128,256]{3,2,1,0:T(8,128)S(1)}, u32[]{:S(2)}, u32[]{:S(2)}) collective-permute-start(f32[2,2,128,256]{3,2,1,0:T(8,128)S(1)} %slice.19), channel_id=1, source_target_pairs={{0,192},{1,25},{2,194},{3,27},{4,196},{5,29},{6,198},{7,31},{8,200... | collective-permute-start | bytes 1572872 | tf_op jit(solution)/shard_map/ppermute | solution.py:40
  49.5 2.1 %collective-permute-done.13.refs_3_.refs_6_ = f32[2,2,128,256]{3,2,1,0:T(8,128)S(1)} collective-permute-done((f32[2,2,128,256]{3,2,1,0:T(8,128)S(1)}, f32[2,2,128,256]{3,2,1,0:T(8,128)S(1)}, u32[]{:S(2)}, u32[]{:S(2)}) %collective-permute-start.13) | collective-permute-done | bytes 524320 | tf_op jit(solution)/shard_map/ppermute | solution.py:40
  51.6 3.5 %u_rows.2 = (f32[256,256]{1,0:T(8,128)S(1)}, f32[8,64,128]{2,1,0:T(8,128)S(1)}) custom-call(s32[80]{0:T(128)S(1)} %copy-done.5, s32[16]{0:T(128)S(1)} %copy-done.3, f32[4,2,128,256]{3,2,1,0:T(8,128)S(1)} %pad_maximum_fusion.refs_1_.refs_0_, f32[4,2,128,256]{3,2,1,0:T(8,128)S(1)} %pad_maximum_fusion.1.refs_2_.refs_1_, ...), custom_call_target="tpu_custom_call" | custom-call | tf_op jit(solution)/shard_map/u_rows/pallas_call | solution.py:187
  55.1 3.5 %v_part.6.refs_3_ = f32[2,256,256]{2,1,0:T(8,128)S(1)} custom-call(s32[64]{0:T(128)S(1)} %copy-done.6, s32[80]{0:T(128)S(1)} %copy-done.5, s32[16]{0:T(128)S(1)} %copy-done.3, f32[256,8192]{1,0:T(8,128)S(1)} %copy-done, f32[4,2,128,256]{3,2,1,0:T(8,128)S(1)} %collective-permute-done.7.refs_1_.refs_4_, ...), custom_call_target="tpu_custom_call" | custom-call | flops 1207959552 | bytes 50331648 | tf_op jit(solution)/shard_map/v_part/pallas_call | solution.py:258
  58.7 0.9 u_rows.3
  59.6 1.7 %v_part.7 = (f32[2,256,256]{2,1,0:T(8,128)S(1)}, f32[264,256]{1,0:T(8,128)S(1)}) custom-call(s32[64]{0:T(128)S(1)} %copy-done.6, s32[80]{0:T(128)S(1)} %copy-done.5, s32[16]{0:T(128)S(1)} %copy-done.3, f32[256,8192]{1,0:T(8,128)S(1)} %copy-done, f32[2,2,128,256]{3,2,1,0:T(8,128)S(1)} %collective-permute-done.11.refs_0_.refs_1_, ...), custom_call_target="tpu_custom_call" | custom-call | flops 402653184 | bytes 16777216 | tf_op jit(solution)/shard_map/v_part/pallas_call | solution.py:258
  61.4 0.0 copy-start.1
  61.4 0.8 collective-permute-start.17
  62.2 1.7 %collective-permute-start.18 = (f32[264,256]{1,0:T(8,128)S(1)}, f32[264,256]{1,0:T(8,128)S(1)}, u32[]{:S(2)}, u32[]{:S(2)}) collective-permute-start(f32[264,256]{1,0:T(8,128)S(1)} %get-tuple-element.75.v0), channel_id=1, source_target_pairs={{0,16},{1,17},{2,18},{3,19},{4,20},{5,21},{6,22},{7,23},{8,24},{9,... | collective-permute-start | bytes 811016 | tf_op jit(solution)/shard_map/ppermute | solution.py:48
  63.9 3.3 %collective-permute-start.15 = (f32[8,64,128]{2,1,0:T(8,128)S(1)}, f32[8,64,128]{2,1,0:T(8,128)S(1)}, u32[]{:S(2)}, u32[]{:S(2)}) collective-permute-start(f32[8,64,128]{2,1,0:T(8,128)S(1)} %get-tuple-element.79), channel_id=1, source_target_pairs={{0,2},{1,3},{2,4},{3,5},{4,6},{5,7},{6,0},{7,1},{8,10},{9,11},{10,... | collective-permute-start | bytes 786440 | tf_op jit(solution)/shard_map/ppermute | solution.py:64
  67.2 2.1 %collective-permute-start.16 = (f32[8,64,128]{2,1,0:T(8,128)S(1)}, f32[8,64,128]{2,1,0:T(8,128)S(1)}, u32[]{:S(2)}, u32[]{:S(2)}) collective-permute-start(f32[8,64,128]{2,1,0:T(8,128)S(1)} %get-tuple-element.79), channel_id=1, source_target_pairs={{0,6},{1,7},{2,0},{3,1},{4,2},{5,3},{6,4},{7,5},{8,14},{9,15},{10,... | collective-permute-start | bytes 786440 | tf_op jit(solution)/shard_map/ppermute | solution.py:64
  69.3 6.7 %collective-permute-done.15 = f32[8,64,128]{2,1,0:T(8,128)S(1)} collective-permute-done((f32[8,64,128]{2,1,0:T(8,128)S(1)}, f32[8,64,128]{2,1,0:T(8,128)S(1)}, u32[]{:S(2)}, u32[]{:S(2)}) %collective-permute-start.15) | collective-permute-done | bytes 262176 | tf_op jit(solution)/shard_map/ppermute | solution.py:64
  76.0 4.2 %collective-permute-done.16 = f32[8,64,128]{2,1,0:T(8,128)S(1)} collective-permute-done((f32[8,64,128]{2,1,0:T(8,128)S(1)}, f32[8,64,128]{2,1,0:T(8,128)S(1)}, u32[]{:S(2)}, u32[]{:S(2)}) %collective-permute-start.16) | collective-permute-done | bytes 262176 | tf_op jit(solution)/shard_map/ppermute | solution.py:64
  80.3 0.1 pad_maximum_fusion.2.near
  80.3 0.1 collective-permute-start.22
  80.4 3.8 %collective-permute-start.20 = (f32[4,64,128]{2,1,0:T(8,128)S(1)}, f32[4,64,128]{2,1,0:T(8,128)S(1)}, u32[]{:S(2)}, u32[]{:S(2)}) collective-permute-start(f32[4,64,128]{2,1,0:T(8,128)S(1)} %slice.22), channel_id=1, source_target_pairs={{0,2},{1,3},{2,4},{3,5},{4,6},{5,7},{6,0},{7,1},{8,10},{9,11},{10,... | collective-permute-start | bytes 393224 | tf_op jit(solution)/shard_map/ppermute | solution.py:64
  84.3 0.4 collective-permute-start.21
  84.8 1.7 %collective-permute-start.19 = (f32[264,256]{1,0:T(8,128)S(1)}, f32[264,256]{1,0:T(8,128)S(1)}, u32[]{:S(2)}, u32[]{:S(2)}) collective-permute-start(f32[264,256]{1,0:T(8,128)S(1)} %collective-permute-done.17.v1), channel_id=1, source_target_pairs={{0,16},{1,17},{2,18},{3,19},{4,20},{5,21},{6,22},{7,23},{8,24},{9,... | collective-permute-start | bytes 811016 | tf_op jit(solution)/shard_map/ppermute | solution.py:48
  86.4 4.1 %collective-permute-done.20 = f32[4,64,128]{2,1,0:T(8,128)S(1)} collective-permute-done((f32[4,64,128]{2,1,0:T(8,128)S(1)}, f32[4,64,128]{2,1,0:T(8,128)S(1)}, u32[]{:S(2)}, u32[]{:S(2)}) %collective-permute-start.20) | collective-permute-done | bytes 131104 | tf_op jit(solution)/shard_map/ppermute | solution.py:64
  90.5 3.1 %collective-permute-done.21 = f32[4,64,128]{2,1,0:T(8,128)S(1)} collective-permute-done((f32[4,64,128]{2,1,0:T(8,128)S(1)}, f32[4,64,128]{2,1,0:T(8,128)S(1)}, u32[]{:S(2)}, u32[]{:S(2)}) %collective-permute-start.21) | collective-permute-done | bytes 131104 | tf_op jit(solution)/shard_map/ppermute | solution.py:64
  93.7 0.1 collective-permute-start.23
  93.8 0.8 collective-permute-done.19.v3
  94.6 0.7 collective-permute-done.23.far2
  95.3 1.8 %product.1 = (f32[272,256]{1,0:T(8,128)S(1)}, f32[272,256]{1,0:T(8,128)S(1)}, f32[272,256]{1,0:T(8,128)S(1)}, f32[272,256]{1,0:T(8,128)S(1)}) custom-call(s32[16]{0:T(128)S(1)} %copy-done.4, f32[264,256]{1,0:T(8,128)S(1)} %get-tuple-element.75.v0, f32[264,256]{1,0:T(8,128)S(1)} %collective-permute-done.17.v1, f32[264,256]{1,0:T(8,128)S(1)} %collective-permute-done.18.v2, ...), custom_call_target="tpu_custom_call" | custom-call | flops 805306368 | bytes 5242880 | tf_op jit(solution)/shard_map/product/pallas_call | solution.py:309
  97.1 1.6 %collective-permute-start.24 = (f32[272,256]{1,0:T(8,128)S(1)}, f32[272,256]{1,0:T(8,128)S(1)}, u32[]{:S(2)}, u32[]{:S(2)}) collective-permute-start(f32[272,256]{1,0:T(8,128)S(1)} %get-tuple-element.83), channel_id=1, source_target_pairs={{0,64},{1,65},{2,66},{3,67},{4,68},{5,69},{6,70},{7,71},{8,72},{9,... | collective-permute-start | bytes 835592 | tf_op jit(solution)/shard_map/ppermute | solution.py:52
  98.7 2.9 %collective-permute-start.25 = (f32[272,256]{1,0:T(8,128)S(1)}, f32[272,256]{1,0:T(8,128)S(1)}, u32[]{:S(2)}, u32[]{:S(2)}) collective-permute-start(f32[272,256]{1,0:T(8,128)S(1)} %get-tuple-element.84), channel_id=1, source_target_pairs={{0,128},{1,129},{2,130},{3,131},{4,132},{5,133},{6,134},{7,135},{8... | collective-permute-start | bytes 835592 | tf_op jit(solution)/shard_map/ppermute | solution.py:52
  101.6 1.3 %collective-permute-start.26 = (f32[272,256]{1,0:T(8,128)S(1)}, f32[272,256]{1,0:T(8,128)S(1)}, u32[]{:S(2)}, u32[]{:S(2)}) collective-permute-start(f32[272,256]{1,0:T(8,128)S(1)} %get-tuple-element.85), channel_id=1, source_target_pairs={{0,192},{1,193},{2,194},{3,195},{4,196},{5,197},{6,198},{7,199},{8... | collective-permute-start | bytes 835592 | tf_op jit(solution)/shard_map/ppermute | solution.py:52
  102.9 4.2 %collective-permute-done.24.r1 = f32[272,256]{1,0:T(8,128)S(1)} collective-permute-done((f32[272,256]{1,0:T(8,128)S(1)}, f32[272,256]{1,0:T(8,128)S(1)}, u32[]{:S(2)}, u32[]{:S(2)}) %collective-permute-start.24) | collective-permute-done | bytes 278560 | tf_op jit(solution)/shard_map/ppermute | solution.py:52
  107.1 7.1 %collective-permute-done.25.r2 = f32[272,256]{1,0:T(8,128)S(1)} collective-permute-done((f32[272,256]{1,0:T(8,128)S(1)}, f32[272,256]{1,0:T(8,128)S(1)}, u32[]{:S(2)}, u32[]{:S(2)}) %collective-permute-start.25) | collective-permute-done | bytes 278560 | tf_op jit(solution)/shard_map/ppermute | solution.py:52
  114.2 0.1 sum_second.1
  114.3 0.6 copy-done.2
  114.9 0.9 collective-permute-start.27
  115.8 2.8 %cross.1 = (f32[2,256,256]{2,1,0:T(8,128)}, f32[2,256,256]{2,1,0:T(8,128)}) custom-call(s32[16]{0:T(128)} %get-tuple-element.53.info.pos, f32[2,256,256]{2,1,0:T(8,128)} %copy-done.1, f32[256,8192]{1,0:T(8,128)} %block.1), custom_call_target="tpu_custom_call" | custom-call | tf_op jit(solution)/shard_map/cross/pallas_call | solution.py:356
  118.6 1.5 %collective-permute-done.27.came = f32[144,256]{1,0:T(8,128)S(1)} collective-permute-done((f32[144,256]{1,0:T(8,128)S(1)}, f32[144,256]{1,0:T(8,128)S(1)}, u32[]{:S(2)}, u32[]{:S(2)}) %collective-permute-start.27) | collective-permute-done | bytes 147488 | tf_op jit(solution)/shard_map/ppermute | solution.py:56
  120.1 0.7 copy-done.7
  120.8 2.2 %last.1 = (f32[2,256,256]{2,1,0:T(8,128)}, f32[64,2,256]{2,1,0:T(2,128)}) custom-call(s32[16]{0:T(128)} %get-tuple-element.53.info.pos, f32[144,256]{1,0:T(8,128)} %copy-done.2, f32[144,256]{1,0:T(8,128)} %copy-done.7, f32[2,256]{1,0:T(2,128)} %dinv.1, f32[2,256,256]{2,1,0:T(8,128)} %get-tuple-element.88.base), custom_call_target="tpu_custom_call" | custom-call | tf_op jit(solution)/shard_map/last/pallas_call | solution.py:388
  (30 shorter events, 0.2 us)
Async XLA Ops:
  0.6 8.5 %collective-permute-start.3 = (f32[2,128,256]{2,1,0:T(8,128)}, f32[2,128,256]{2,1,0:T(8,128)S(1)}, u32[]{:S(2)}, u32[]{:S(2)}) collective-permute-start(f32[2,128,256]{2,1,0:T(8,128)} %param.7), channel_id=1, source_target_pairs={{0,32},{1,33},{2,34},{3,35},{4,36},{5,37},{6,38},{7,39},{8,40},{9,... | collective-permute-start | bytes 786440 | tf_op jit(solution)/shard_map/ppermute | solution.py:56
  2.6 9.1 %collective-permute-start = (f32[2,128,256]{2,1,0:T(8,128)}, f32[2,128,256]{2,1,0:T(8,128)S(1)}, u32[]{:S(2)}, u32[]{:S(2)}) collective-permute-start(f32[2,128,256]{2,1,0:T(8,128)} %param.7), channel_id=1, source_target_pairs={{0,8},{1,65},{2,10},{3,67},{4,12},{5,69},{6,14},{7,71},{8,16},{9,7... | collective-permute-start | bytes 786440 | tf_op jit(solution)/shard_map/ppermute | solution.py:40
  4.1 9.8 %collective-permute-start.1 = (f32[2,128,256]{2,1,0:T(8,128)}, f32[2,128,256]{2,1,0:T(8,128)S(1)}, u32[]{:S(2)}, u32[]{:S(2)}) collective-permute-start(f32[2,128,256]{2,1,0:T(8,128)} %param.7), channel_id=1, source_target_pairs={{0,16},{1,129},{2,18},{3,131},{4,20},{5,133},{6,22},{7,135},{8,24}... | collective-permute-start | bytes 786440 | tf_op jit(solution)/shard_map/ppermute | solution.py:40
  5.2 9.4 %collective-permute-start.2 = (f32[2,128,256]{2,1,0:T(8,128)}, f32[2,128,256]{2,1,0:T(8,128)S(1)}, u32[]{:S(2)}, u32[]{:S(2)}) collective-permute-start(f32[2,128,256]{2,1,0:T(8,128)} %param.7), channel_id=1, source_target_pairs={{0,24},{1,193},{2,26},{3,195},{4,28},{5,197},{6,30},{7,199},{8,0},... | collective-permute-start | bytes 786440 | tf_op jit(solution)/shard_map/ppermute | solution.py:40
  9.2 12.9 %collective-permute-start.4 = (f32[2,128,256]{2,1,0:T(8,128)S(1)}, f32[2,128,256]{2,1,0:T(8,128)}, u32[]{:S(2)}, u32[]{:S(2)}) collective-permute-start(f32[2,128,256]{2,1,0:T(8,128)S(1)} %collective-permute-done.3), channel_id=1, source_target_pairs={{0,8},{1,65},{2,10},{3,67},{4,12},{5,69},{6,14},{7,71},{8,16},{9,7... | collective-permute-start | bytes 786440 | tf_op jit(solution)/shard_map/ppermute | solution.py:40
  10.6 11.4 %collective-permute-start.5 = (f32[2,128,256]{2,1,0:T(8,128)S(1)}, f32[2,128,256]{2,1,0:T(8,128)}, u32[]{:S(2)}, u32[]{:S(2)}) collective-permute-start(f32[2,128,256]{2,1,0:T(8,128)S(1)} %collective-permute-done.3), channel_id=1, source_target_pairs={{0,16},{1,129},{2,18},{3,131},{4,20},{5,133},{6,22},{7,135},{8,24}... | collective-permute-start | bytes 786440 | tf_op jit(solution)/shard_map/ppermute | solution.py:40
  11.8 11.5 %collective-permute-start.6 = (f32[2,128,256]{2,1,0:T(8,128)S(1)}, f32[2,128,256]{2,1,0:T(8,128)}, u32[]{:S(2)}, u32[]{:S(2)}) collective-permute-start(f32[2,128,256]{2,1,0:T(8,128)S(1)} %collective-permute-done.3), channel_id=1, source_target_pairs={{0,24},{1,193},{2,26},{3,195},{4,28},{5,197},{6,30},{7,199},{8,0},... | collective-permute-start | bytes 786440 | tf_op jit(solution)/shard_map/ppermute | solution.py:40
  15.7 20.0 %collective-permute-start.10 = (f32[4,2,128,256]{3,2,1,0:T(8,128)S(1)}, f32[4,2,128,256]{3,2,1,0:T(8,128)S(1)}, u32[]{:S(2)}, u32[]{:S(2)}) collective-permute-start(f32[4,2,128,256]{3,2,1,0:T(8,128)S(1)} %pad_maximum_fusion.refs_1_.refs_0_), channel_id=1, source_target_pairs={{0,192},{1,25},{2,194},{3,27},{4,196},{5,29},{6,198},{7,31},{8,200... | collective-permute-start | bytes 3145736 | tf_op jit(solution)/shard_map/ppermute | solution.py:40
  18.8 16.9 %collective-permute-start.9 = (f32[4,2,128,256]{3,2,1,0:T(8,128)S(1)}, f32[4,2,128,256]{3,2,1,0:T(8,128)S(1)}, u32[]{:S(2)}, u32[]{:S(2)}) collective-permute-start(f32[4,2,128,256]{3,2,1,0:T(8,128)S(1)} %pad_maximum_fusion.refs_1_.refs_0_), channel_id=1, source_target_pairs={{0,64},{1,9},{2,66},{3,11},{4,68},{5,13},{6,70},{7,15},{8,72},{9,1... | collective-permute-start | bytes 3145736 | tf_op jit(solution)/shard_map/ppermute | solution.py:40
  24.5 21.5 %collective-permute-start.7 = (f32[4,2,128,256]{3,2,1,0:T(8,128)S(1)}, f32[4,2,128,256]{3,2,1,0:T(8,128)S(1)}, u32[]{:S(2)}, u32[]{:S(2)}) collective-permute-start(f32[4,2,128,256]{3,2,1,0:T(8,128)S(1)} %pad_maximum_fusion.1.refs_2_.refs_1_), channel_id=1, source_target_pairs={{0,64},{1,9},{2,66},{3,11},{4,68},{5,13},{6,70},{7,15},{8,72},{9,1... | collective-permute-start | bytes 3145736 | tf_op jit(solution)/shard_map/ppermute | solution.py:40
  26.2 19.8 %collective-permute-start.8 = (f32[4,2,128,256]{3,2,1,0:T(8,128)S(1)}, f32[4,2,128,256]{3,2,1,0:T(8,128)S(1)}, u32[]{:S(2)}, u32[]{:S(2)}) collective-permute-start(f32[4,2,128,256]{3,2,1,0:T(8,128)S(1)} %pad_maximum_fusion.1.refs_2_.refs_1_), channel_id=1, source_target_pairs={{0,192},{1,25},{2,194},{3,27},{4,196},{5,29},{6,198},{7,31},{8,200... | collective-permute-start | bytes 3145736 | tf_op jit(solution)/shard_map/ppermute | solution.py:40
  27.8 3.4 %copy-start = (f32[256,8192]{1,0:T(8,128)S(1)}, f32[256,8192]{1,0:T(8,128)}, u32[]{:S(2)}) copy-start(f32[256,8192]{1,0:T(8,128)} %block.1) | copy-start | bytes 25165828
  31.2 0.6 copy-start.3
  31.8 0.7 copy-start.5
  32.5 0.7 copy-start.6
  35.7 15.9 %collective-permute-start.13 = (f32[2,2,128,256]{3,2,1,0:T(8,128)S(1)}, f32[2,2,128,256]{3,2,1,0:T(8,128)S(1)}, u32[]{:S(2)}, u32[]{:S(2)}) collective-permute-start(f32[2,2,128,256]{3,2,1,0:T(8,128)S(1)} %slice.20), channel_id=1, source_target_pairs={{0,64},{1,9},{2,66},{3,11},{4,68},{5,13},{6,70},{7,15},{8,72},{9,1... | collective-permute-start | bytes 1572872 | tf_op jit(solution)/shard_map/ppermute | solution.py:40
  36.2 15.4 %collective-permute-start.14 = (f32[2,2,128,256]{3,2,1,0:T(8,128)S(1)}, f32[2,2,128,256]{3,2,1,0:T(8,128)S(1)}, u32[]{:S(2)}, u32[]{:S(2)}) collective-permute-start(f32[2,2,128,256]{3,2,1,0:T(8,128)S(1)} %slice.21), channel_id=1, source_target_pairs={{0,192},{1,25},{2,194},{3,27},{4,196},{5,29},{6,198},{7,31},{8,200... | collective-permute-start | bytes 1572872 | tf_op jit(solution)/shard_map/ppermute | solution.py:40
  46.0 12.7 %collective-permute-start.11 = (f32[2,2,128,256]{3,2,1,0:T(8,128)S(1)}, f32[2,2,128,256]{3,2,1,0:T(8,128)S(1)}, u32[]{:S(2)}, u32[]{:S(2)}) collective-permute-start(f32[2,2,128,256]{3,2,1,0:T(8,128)S(1)} %slice.18), channel_id=1, source_target_pairs={{0,64},{1,9},{2,66},{3,11},{4,68},{5,13},{6,70},{7,15},{8,72},{9,1... | collective-permute-start | bytes 1572872 | tf_op jit(solution)/shard_map/ppermute | solution.py:40
  46.2 12.5 %collective-permute-start.12 = (f32[2,2,128,256]{3,2,1,0:T(8,128)S(1)}, f32[2,2,128,256]{3,2,1,0:T(8,128)S(1)}, u32[]{:S(2)}, u32[]{:S(2)}) collective-permute-start(f32[2,2,128,256]{3,2,1,0:T(8,128)S(1)} %slice.19), channel_id=1, source_target_pairs={{0,192},{1,25},{2,194},{3,27},{4,196},{5,29},{6,198},{7,31},{8,200... | collective-permute-start | bytes 1572872 | tf_op jit(solution)/shard_map/ppermute | solution.py:40
  58.7 36.6 %copy-start.4 = (s32[16]{0:T(128)S(1)}, s32[16]{0:T(128)}, u32[]{:S(2)}) copy-start(s32[16]{0:T(128)} %get-tuple-element.53.info.pos) | copy-start | bytes 196
  61.4 35.7 %copy-start.1 = (f32[2,256,256]{2,1,0:T(8,128)}, f32[2,256,256]{2,1,0:T(8,128)S(1)}, u32[]{:S(2)}) copy-start(f32[2,256,256]{2,1,0:T(8,128)S(1)} %get-tuple-element.73.v) | copy-start | bytes 1572868
  61.4 18.9 %collective-permute-start.17 = (f32[264,256]{1,0:T(8,128)S(1)}, f32[264,256]{1,0:T(8,128)S(1)}, u32[]{:S(2)}, u32[]{:S(2)}) collective-permute-start(f32[264,256]{1,0:T(8,128)S(1)} %get-tuple-element.75.v0), channel_id=1, source_target_pairs={{0,8},{1,9},{2,10},{3,11},{4,12},{5,13},{6,14},{7,15},{8,0},{9,1},... | collective-permute-start | bytes 811016 | tf_op jit(solution)/shard_map/ppermute | solution.py:48
  62.2 18.1 %collective-permute-start.18 = (f32[264,256]{1,0:T(8,128)S(1)}, f32[264,256]{1,0:T(8,128)S(1)}, u32[]{:S(2)}, u32[]{:S(2)}) collective-permute-start(f32[264,256]{1,0:T(8,128)S(1)} %get-tuple-element.75.v0), channel_id=1, source_target_pairs={{0,16},{1,17},{2,18},{3,19},{4,20},{5,21},{6,22},{7,23},{8,24},{9,... | collective-permute-start | bytes 811016 | tf_op jit(solution)/shard_map/ppermute | solution.py:48
  63.9 12.1 %collective-permute-start.15 = (f32[8,64,128]{2,1,0:T(8,128)S(1)}, f32[8,64,128]{2,1,0:T(8,128)S(1)}, u32[]{:S(2)}, u32[]{:S(2)}) collective-permute-start(f32[8,64,128]{2,1,0:T(8,128)S(1)} %get-tuple-element.79), channel_id=1, source_target_pairs={{0,2},{1,3},{2,4},{3,5},{4,6},{5,7},{6,0},{7,1},{8,10},{9,11},{10,... | collective-permute-start | bytes 786440 | tf_op jit(solution)/shard_map/ppermute | solution.py:64
  67.2 13.1 %collective-permute-start.16 = (f32[8,64,128]{2,1,0:T(8,128)S(1)}, f32[8,64,128]{2,1,0:T(8,128)S(1)}, u32[]{:S(2)}, u32[]{:S(2)}) collective-permute-start(f32[8,64,128]{2,1,0:T(8,128)S(1)} %get-tuple-element.79), channel_id=1, source_target_pairs={{0,6},{1,7},{2,0},{3,1},{4,2},{5,3},{6,4},{7,5},{8,14},{9,15},{10,... | collective-permute-start | bytes 786440 | tf_op jit(solution)/shard_map/ppermute | solution.py:64
  80.3 15.0 %collective-permute-start.22 = (f32[3,8,64,128]{3,2,1,0:T(8,128)S(1)}, f32[3,8,64,128]{3,2,1,0:T(8,128)S(1)}, u32[]{:S(2)}, u32[]{:S(2)}) collective-permute-start(f32[3,8,64,128]{3,2,1,0:T(8,128)S(1)} %pad_maximum_fusion.2.near), channel_id=1, source_target_pairs={{0,1},{1,0},{2,3},{3,2},{4,5},{5,4},{6,7},{7,6},{8,9},{9,8},{10,11... | collective-permute-start | bytes 2359304 | tf_op jit(solution)/shard_map/ppermute | solution.py:60
  80.4 10.1 %collective-permute-start.20 = (f32[4,64,128]{2,1,0:T(8,128)S(1)}, f32[4,64,128]{2,1,0:T(8,128)S(1)}, u32[]{:S(2)}, u32[]{:S(2)}) collective-permute-start(f32[4,64,128]{2,1,0:T(8,128)S(1)} %slice.22), channel_id=1, source_target_pairs={{0,2},{1,3},{2,4},{3,5},{4,6},{5,7},{6,0},{7,1},{8,10},{9,11},{10,... | collective-permute-start | bytes 393224 | tf_op jit(solution)/shard_map/ppermute | solution.py:64
  84.3 9.3 %collective-permute-start.21 = (f32[4,64,128]{2,1,0:T(8,128)S(1)}, f32[4,64,128]{2,1,0:T(8,128)S(1)}, u32[]{:S(2)}, u32[]{:S(2)}) collective-permute-start(f32[4,64,128]{2,1,0:T(8,128)S(1)} %slice.23), channel_id=1, source_target_pairs={{0,6},{1,7},{2,0},{3,1},{4,2},{5,3},{6,4},{7,5},{8,14},{9,15},{10,... | collective-permute-start | bytes 393224 | tf_op jit(solution)/shard_map/ppermute | solution.py:64
  84.8 9.8 %collective-permute-start.19 = (f32[264,256]{1,0:T(8,128)S(1)}, f32[264,256]{1,0:T(8,128)S(1)}, u32[]{:S(2)}, u32[]{:S(2)}) collective-permute-start(f32[264,256]{1,0:T(8,128)S(1)} %collective-permute-done.17.v1), channel_id=1, source_target_pairs={{0,16},{1,17},{2,18},{3,19},{4,20},{5,21},{6,22},{7,23},{8,24},{9,... | collective-permute-start | bytes 811016 | tf_op jit(solution)/shard_map/ppermute | solution.py:48
  93.7 1.6 %collective-permute-start.23 = (f32[8,64,128]{2,1,0:T(8,128)S(1)}, f32[8,64,128]{2,1,0:T(8,128)S(1)}, u32[]{:S(2)}, u32[]{:S(2)}) collective-permute-start(f32[8,64,128]{2,1,0:T(8,128)S(1)} %constant_dynamic-update-slice_fusion.near2), channel_id=1, source_target_pairs={{0,1},{1,0},{2,3},{3,2},{4,5},{5,4},{6,7},{7,6},{8,9},{9,8},{10,11... | collective-permute-start | bytes 786440 | tf_op jit(solution)/shard_map/ppermute | solution.py:60
  97.1 10.0 %collective-permute-start.24 = (f32[272,256]{1,0:T(8,128)S(1)}, f32[272,256]{1,0:T(8,128)S(1)}, u32[]{:S(2)}, u32[]{:S(2)}) collective-permute-start(f32[272,256]{1,0:T(8,128)S(1)} %get-tuple-element.83), channel_id=1, source_target_pairs={{0,64},{1,65},{2,66},{3,67},{4,68},{5,69},{6,70},{7,71},{8,72},{9,... | collective-permute-start | bytes 835592 | tf_op jit(solution)/shard_map/ppermute | solution.py:52
  98.7 15.5 %collective-permute-start.25 = (f32[272,256]{1,0:T(8,128)S(1)}, f32[272,256]{1,0:T(8,128)S(1)}, u32[]{:S(2)}, u32[]{:S(2)}) collective-permute-start(f32[272,256]{1,0:T(8,128)S(1)} %get-tuple-element.84), channel_id=1, source_target_pairs={{0,128},{1,129},{2,130},{3,131},{4,132},{5,133},{6,134},{7,135},{8... | collective-permute-start | bytes 835592 | tf_op jit(solution)/shard_map/ppermute | solution.py:52
  101.6 12.6 %collective-permute-start.26 = (f32[272,256]{1,0:T(8,128)S(1)}, f32[272,256]{1,0:T(8,128)S(1)}, u32[]{:S(2)}, u32[]{:S(2)}) collective-permute-start(f32[272,256]{1,0:T(8,128)S(1)} %get-tuple-element.85), channel_id=1, source_target_pairs={{0,192},{1,193},{2,194},{3,195},{4,196},{5,197},{6,198},{7,199},{8... | collective-permute-start | bytes 835592 | tf_op jit(solution)/shard_map/ppermute | solution.py:52
  114.3 0.7 copy-start.2
  114.9 5.1 %collective-permute-start.27 = (f32[144,256]{1,0:T(8,128)S(1)}, f32[144,256]{1,0:T(8,128)S(1)}, u32[]{:S(2)}, u32[]{:S(2)}) collective-permute-start(f32[144,256]{1,0:T(8,128)S(1)} %get-tuple-element.87), channel_id=1, source_target_pairs={{0,32},{1,33},{2,34},{3,35},{4,36},{5,37},{6,38},{7,39},{8,40},{9,... | collective-permute-start | bytes 442376 | tf_op jit(solution)/shard_map/ppermute | solution.py:56
  120.1 0.7 copy-start.7

commit v4 on v3

--- a/solution.py
+++ b/solution.py
@@ -12,6 +12,7 @@
 VMEM = pltpu.VMEM
 SMEM = pltpu.SMEM
 VLIM = 24
+INFO = 144
 COST = 4
 
 
@@ -78,14 +79,14 @@
     return dg(ah, bh) + (dg(ah, bl) + dg(al, bh))
 
 
-def plan_kernel(tile_map, counts, assign, cb, meta, info):
+def plan_kernel(tile_map, counts, assign, plan):
     me, col = lax.axis_index("cube"), lax.axis_index("col")
     x, zl, y = lax.rem(me, 4), lax.rem(lax.div(me, 4), 2), lax.div(me, 8)
     zh, core = lax.div(col, 2), lax.rem(col, 2)
     group = (y * 2 + zl) * 4
     flip = jnp.where(assign[0] != 0, 1, 0)
     for i, value in enumerate((x, y, zl, zh, core)):
-        info[i] = value
+        plan[INFO + i] = value
 
     def fill(i, _):
         s, dp, dq, plane = i & 1, (i >> 1) & 3, (i >> 3) & 3, i >> 5
@@ -94,19 +95,19 @@
         src = (((y - dy) & 3) * 2 + ((zl + plane) & 1)) * 4 + ((x - dx) & 3)
         front = s ^ flip
         tile = tile_map[front, src >> 1]
-        cb[i] = tile * 2 + (src & 1)
+        plan[i] = tile * 2 + (src & 1)
         live = jnp.clip(counts[front] - src * 128, 0, 128)
-        meta[i] = live
+        plan[64 + i] = live
 
         @pl.when((tile >= group) & (tile < group + 4))
         def _():
             piece = (tile - group) * 2 + (src & 1)
-            meta[64 + piece] = i
-            meta[72 + piece] = live
+            plan[128 + piece] = i
+            plan[136 + piece] = live
 
         return 0
 
-    lax.fori_loop(0, 64, fill, 0)
+    lax.fori_loop(0, 64, fill, 0, unroll=8)
 
     def look(i, _):
         front, j = i >> 4, i & 15
@@ -114,18 +115,18 @@
 
         @pl.when((tile >= group) & (tile < group + 4))
         def _():
-            info[5 + ((x ^ tile) & 3)] = front ^ flip
+            plan[INFO + 5 + ((x ^ tile) & 3)] = front ^ flip
 
         @pl.when(tile == me)
         def _():
-            info[9] = front
-            info[10] = jnp.clip(counts[front] - j * 256, 0, 256)
+            plan[INFO + 9] = front
+            plan[INFO + 10] = jnp.clip(counts[front] - j * 256, 0, 256)
 
         return 0
 
-    lax.fori_loop(0, 32, look, 0)
-    info[11] = flip
-    info[12] = me
+    lax.fori_loop(0, 32, look, 0, unroll=8)
+    plan[INFO + 11] = flip
+    plan[INFO + 12] = me
 
 
 def plan_call(tile_map, counts, assign):
@@ -133,13 +134,14 @@
     return pl.pallas_call(
         plan_kernel,
         in_specs=[spec] * 3,
-        out_specs=[spec] * 3,
-        out_shape=[jax.ShapeDtypeStruct((size,), jnp.int32) for size in (64, 80, 16)],
+        out_specs=spec,
+        out_shape=jax.ShapeDtypeStruct((160,), jnp.int32),
+        compiler_params=pltpu.CompilerParams(vmem_limit_bytes=2**20),
         name="plan",
     )(tile_map, counts, assign)
 
 
-def u_kernel(first, groups, meta, info, *refs):
+def u_kernel(first, groups, plan, *refs):
     us, refs = refs[:len(groups)], refs[len(groups):]
     if not first:
         (own_in, ut_in), refs = refs[:2], refs[2:]
@@ -147,7 +149,7 @@
 
     def each(do):
         for piece in range(8):
-            place = meta[64 + piece]
+            place = plan[128 + piece]
             for u, (base, size) in zip(us, groups):
                 @pl.when((place >= base * 2) & (place < (base + size) * 2))
                 def _():
@@ -162,12 +164,12 @@
     else:
         own[...] = own_in[...]
         ut[...] = ut_in[...]
-    x = info[0]
+    x = plan[INFO]
     rows = lax.broadcasted_iota(jnp.int32, (128, 256), 0)
 
     def take(piece, copy):
         copy.wait()
-        part = jnp.where(rows < meta[72 + piece], buf[piece], 0.0)
+        part = jnp.where(rows < plan[136 + piece], buf[piece], 0.0)
         turned[...] = part.T
         ut[piece] = turned[pl.ds(pl.multiple_of(x * 64, 64), 64), :]
 
@@ -183,10 +185,10 @@
     groups = tuple((start, u.shape[0]) for start, u in zip(starts, us))
     first = carry is None
     smem, vmem, anywhere = (pl.BlockSpec(memory_space=m) for m in (SMEM, VMEM, pl.ANY))
-    at = 2 + len(us)
+    at = 1 + len(us)
     return pl.pallas_call(
         functools.partial(u_kernel, first, groups),
-        in_specs=[smem] * 2 + [anywhere] * len(us) + ([] if first else [vmem] * 2),
+        in_specs=[smem] + [anywhere] * len(us) + ([] if first else [vmem] * 2),
         out_specs=[vmem] * 2,
         out_shape=[jax.ShapeDtypeStruct((256, 256), F32), jax.ShapeDtypeStruct((8, 64, 128), F32)],
         scratch_shapes=[VMEM((8, 128, 256), F32), VMEM((256, 128), F32),
@@ -194,10 +196,10 @@
         input_output_aliases={} if first else {at: 0, at + 1: 1},
         compiler_params=pltpu.CompilerParams(vmem_limit_bytes=16 * 2**20),
         name="u_rows",
-    )(*plan[1:], *us, *(() if first else carry))
-
-
-def v_kernel(first, last, groups, cb, meta, info, *refs):
+    )(plan, *us, *(() if first else carry))
+
+
+def v_kernel(first, last, groups, plan, *refs):
     ginv, refs = refs[0], refs[1:]
     us, refs = refs[:len(groups)], refs[len(groups):]
     if not first:
@@ -212,7 +214,7 @@
         mine = [pltpu.make_async_copy(us[i], ubuf.at[pl.ds(at, size)], usem.at[i])]
         for b in range(size):
             for s in range(2):
-                column = pl.multiple_of(cb[(base + b) * 2 + s] * 128, 128)
+                column = pl.multiple_of(plan[(base + b) * 2 + s] * 128, 128)
                 mine.append(pltpu.make_async_copy(
                     ginv.at[:, pl.ds(column, 128)],
                     gbuf.at[s, :, pl.ds((at + b) * 128, 128)],
@@ -228,7 +230,7 @@
             c.wait()
         for s in range(2):
             uu = jnp.concatenate(
-                [jnp.where(rows < meta[(base + b) * 2 + s], ubuf[at + b, s], 0.0)
+                [jnp.where(rows < plan[64 + (base + b) * 2 + s], ubuf[at + b, s], 0.0)
                  for b in range(size)], axis=0)
             gg = gbuf[s, :, at * 128:(at + size) * 128]
             part = dot3(gg, uu, ((1,), (0,)))
@@ -240,7 +242,7 @@
         at += size
     if last:
         msg = refs[1]
-        v_own = v_out[info[9] ^ info[11]]
+        v_own = v_out[plan[INFO + 9] ^ plan[INFO + 11]]
         msg[:256, :] = v_own
         diag = jnp.sum(own[...] * v_own, axis=0, keepdims=True)
         msg[256:264, :] = jnp.broadcast_to(diag, (8, 256))
@@ -257,7 +259,7 @@
         shapes.append((264, 256))
     out = pl.pallas_call(
         functools.partial(v_kernel, first, last, groups),
-        in_specs=[smem] * 3 + [pl.BlockSpec(memory_space=pltpu.HBM)] + [anywhere] * len(us)
+        in_specs=[smem] + [pl.BlockSpec(memory_space=pltpu.HBM)] + [anywhere] * len(us)
         + [vmem] * len(extra),
         out_specs=[vmem] * len(shapes),
         out_shape=[jax.ShapeDtypeStruct(shape, F32) for shape in shapes],
@@ -267,14 +269,14 @@
         cost_estimate=pl.CostEstimate(flops=3 * 4 * 256 * 128 * n * 256,
                                       bytes_accessed=n * COST * 2**20, transcendentals=0),
         name="v_part",
-    )(*plan, ginv, *us, *extra)
+    )(plan, ginv, *us, *extra)
     return out if last else out[0]
 
 
-def prod_kernel(pos, v0, v1, v2, v3, near, near2, far, far2, m0, m1, m2, m3, acc):
-    x, y, zl, zh, core = pos[0], pos[1], pos[2], pos[3], pos[4]
+def prod_kernel(plan, v01, v23, near, near2, far, far2, m0, m1, m2, m3, acc):
+    x, y, zl, zh, core = plan[INFO], plan[INFO + 1], plan[INFO + 2], plan[INFO + 3], plan[INFO + 4]
     acc[...] = jnp.zeros_like(acc)
-    vs = (v0, v1, v2, v3)
+    vs = (v01.at[0], v01.at[1], v23.at[0], v23.at[1])
     order = [(k, side) for k in range(4) for side in range(2)]
     for t in range(4):
         tile = x ^ t
@@ -283,7 +285,7 @@
             u = (near2, far2)[side] if k == 2 else (near, far)[side].at[(0, 1, None, 2)[k]]
             left.append(jnp.concatenate([u[tile * 2 + h] for h in range(2)], axis=1))
         part = dot3(jnp.concatenate(left, axis=0), vs[t][:256, :], ((1,), (0,)))
-        s = pos[5 + t]
+        s = plan[INFO + 5 + t]
         for i, (k, side) in enumerate(order):
             block = lax.rem(zh + 4 - k, 4) * 2 + (core if side == 0 else 1 - core)
             acc[s, block] += part[i * 64:(i + 1) * 64, :]
@@ -291,7 +293,7 @@
     for s in range(2):
         total = None
         for t in range(4):
-            term = jnp.where(pos[5 + t] == s, vs[t][256:264, :], 0.0)
+            term = jnp.where(plan[INFO + 5 + t] == s, vs[t][256:264, :], 0.0)
             total = term if total is None else total + term
         diag.append(total)
     for k, m in enumerate((m0, m1, m2, m3)):
@@ -304,11 +306,11 @@
         m[264:272, :] = diag[1]
 
 
-def prod_call(pos, vs, pieces):
+def prod_call(plan, vs, pieces):
     spec = pl.BlockSpec(memory_space=VMEM)
     return pl.pallas_call(
         prod_kernel,
-        in_specs=[pl.BlockSpec(memory_space=SMEM)] + [spec] * 8,
+        in_specs=[pl.BlockSpec(memory_space=SMEM)] + [spec] * 6,
         out_specs=[spec] * 4,
         out_shape=[jax.ShapeDtypeStruct((272, 256), F32)] * 4,
         scratch_shapes=[VMEM((2, 8, 64, 256), F32)],
@@ -316,7 +318,7 @@
         cost_estimate=pl.CostEstimate(flops=3 * 2 * 512 * 1024 * 256, bytes_accessed=5 * 2**20,
                                       transcendentals=0),
         name="product",
-    )(pos, *vs, *pieces)
+    )(plan, *vs, *pieces)
 
 
 def sum2_kernel(r0, r1, r2, r3, keep, away):
@@ -340,8 +342,8 @@
     )(*rs)
 
 
-def cross_kernel(info, v, block, cross, base):
-    flip = info[11]
+def cross_kernel(plan, v, block, cross, base):
+    flip = plan[INFO + 11]
     eye = lax.broadcasted_iota(jnp.int32, (256, 256), 0) == lax.broadcasted_iota(
         jnp.int32, (256, 256), 1)
     g_diag = jnp.sum(jnp.where(eye, block[...], 0.0), axis=1, keepdims=True)
@@ -351,26 +353,27 @@
         base[f] = g_diag + 2.0 * vf
 
 
-def cross_call(info, v, ginv):
-    full = pl.BlockSpec((2, 256, 256), lambda _, info: (0, 0, 0))
+def cross_call(plan, v, ginv):
+    full = pl.BlockSpec((2, 256, 256), lambda _, plan: (0, 0, 0))
     return pl.pallas_call(
         cross_kernel,
         grid_spec=pltpu.PrefetchScalarGridSpec(
             num_scalar_prefetch=1, grid=(1,),
-            in_specs=[full, pl.BlockSpec((256, 256), lambda _, info: (0, info[12]))],
+            in_specs=[full, pl.BlockSpec((256, 256), lambda _, plan: (0, plan[INFO + 12]))],
             out_specs=[full, full],
         ),
         out_shape=[jax.ShapeDtypeStruct((2, 256, 256), F32)] * 2,
+        compiler_params=pltpu.CompilerParams(vmem_limit_bytes=12 * 2**20),
         name="cross",
-    )(info, v, ginv)
-
-
-def last_kernel(info, keep, came, dinv, base, resist, sigma):
-    flip = info[11]
+    )(plan, v, ginv)
+
+
+def last_kernel(plan, keep, came, dinv, base, resist, sigma):
+    flip = plan[INFO + 11]
     rows = lax.broadcasted_iota(jnp.int32, (256, 256), 0)
-    at = lax.broadcasted_iota(jnp.int32, (64, 256), 0) + lax.rem(info[12], 4) * 64
+    at = lax.broadcasted_iota(jnp.int32, (64, 256), 0) + lax.rem(plan[INFO + 12], 4) * 64
     on_diag = at == lax.broadcasted_iota(jnp.int32, (64, 256), 1)
-    on_diag = on_diag & (info[12] // 4 == info[3] * 2 + info[4])
+    on_diag = on_diag & (plan[INFO + 12] // 4 == plan[INFO + 3] * 2 + plan[INFO + 4])
     for f in range(2):
         s = f ^ flip
         d = dinv[pl.ds(s, 1), :]
@@ -379,19 +382,20 @@
         sigma[:, f, :] = total + jnp.where(on_diag, d, 0.0)
         deep = pl.ds(pl.multiple_of(128 + s * 8, 8), 8)
         diag = (keep[deep, :] + came[deep, :])[0:1, :] + d
-        live = jnp.where(info[9] == f, info[10], 0)
+        live = jnp.where(plan[INFO + 9] == f, plan[INFO + 10], 0)
         resist[f] = jnp.where(rows < live, diag + base[f], 0.0)
 
 
-def last_call(info, keep, came, dinv, base):
+def last_call(plan, keep, came, dinv, base):
     spec = pl.BlockSpec(memory_space=VMEM)
     return pl.pallas_call(
         last_kernel,
         in_specs=[pl.BlockSpec(memory_space=SMEM)] + [spec] * 4,
         out_specs=[spec] * 2,
         out_shape=[jax.ShapeDtypeStruct((2, 256, 256), F32), jax.ShapeDtypeStruct((64, 2, 256), F32)],
+        compiler_params=pltpu.CompilerParams(vmem_limit_bytes=12 * 2**20),
         name="last",
-    )(info, keep, came, dinv, base)
+    )(plan, keep, came, dinv, base)
 
 
 def body(ginv, ufactor, dinv, tile_map, counts, assign):
@@ -399,45 +403,50 @@
 
     a0 = ufactor
     b0 = send_pair(a0)
-    ga = jnp.stack([a0, send_pq(a0, 1, 0), send_pq(a0, 2, 0), send_pq(a0, -1, 0)])
-    ga, tile_map = pin((ga, tile_map))
+    plan = plan_call(tile_map, counts, assign)
+    a1, a2, a3 = send_pq(a0, 1, 0), send_pq(a0, 2, 0), send_pq(a0, -1, 0)
+    b1, b2, b3 = send_pq(b0, 1, 0), send_pq(b0, 2, 0), send_pq(b0, -1, 0)
+    a1, a2, a3, b0, b1, b2, b3 = pin((a1, a2, a3, b0, b1, b2, b3))
+    ga = jnp.stack([a0, a1, a2, a3])
     ga1 = send_pq(ga, 0, 1)
     ga3 = send_pq(ga, 0, -1)
-    plan = plan_call(tile_map, counts, assign)
-    info = plan[2]
-    *b, plan = pin([b0, send_pq(b0, 1, 0), send_pq(b0, 2, 0), send_pq(b0, -1, 0), plan])
-    gb = jnp.stack(b)
-    gb1 = send_pq(gb, 0, 1)
-    gb3 = send_pq(gb, 0, -1)
-    carry = v_call(ginv, plan, [ga, gb], [0, 16], None)
+    gb = jnp.stack([b0, b1, b2, b3])
+    gb1 = send_pq(gb[:3], 0, 1)
+    gb3 = send_pq(gb[1:], 0, -1)
+    carry = v_call(ginv, plan, [ga], [0], None)
     ga1, ga3, carry = pin((ga1, ga3, carry))
     ga2a = send_pq(ga1[:2], 0, 1)
     ga2b = send_pq(ga3[2:], 0, -1)
-    carry = v_call(ginv, plan, [ga1, ga3], [4, 12], carry)
+    gbr = send_pair(jnp.concatenate([ga1[3:], ga3[:1]]))
+    carry = v_call(ginv, plan, [gb, ga1, ga3], [16, 4, 12], carry)
     gb1, gb3, carry = pin((gb1, gb3, carry))
     gb2a = send_pq(gb1[:2], 0, 1)
-    gb2b = send_pq(gb3[2:], 0, -1)
-    carry = v_call(ginv, plan, [gb1, gb3, ga2a, ga2b], [20, 28, 8, 10], carry)
-    rows = u_call(plan, [ga, gb, ga1, ga3, gb1, gb3, ga2a, ga2b],
-                  [0, 16, 4, 12, 20, 28, 8, 10], None)
+    gb2b = send_pq(gb3[1:], 0, -1)
+    carry = v_call(ginv, plan, [gb1, gb3], [20, 29], carry)
+    ga2a, ga2b, gbr, carry = pin((ga2a, ga2b, gbr, carry))
+    gbr1, gbr3 = gbr[:1], gbr[1:]
+    rows = u_call(plan, [ga, gb, ga1, ga3, gb1, gbr1, gbr3, gb3, ga2a, ga2b],
+                  [0, 16, 4, 12, 20, 23, 28, 29, 8, 10], None)
     gb2a, gb2b, carry, rows = pin((gb2a, gb2b, carry, rows))
     own, ut = u_call(plan, [gb2a, gb2b], [24, 26], rows)
 
     c1, c3 = send_zh(ut, 1), send_zh(ut, -1)
-    v, msg = v_call(ginv, plan, [gb2a, gb2b], [24, 26], carry, own)
-    v1, v2 = send_x_flip(msg, 1), send_x_flip(msg, 2)
-    c1, c3, ut, v1, v2 = pin((c1, c3, ut, v1, v2))
-    vs = [msg, v1, v2, send_x_flip(v1, 2)]
+    v, msg = v_call(ginv, plan, [ga2a, ga2b, gbr1, gbr3, gb2a, gb2b], [8, 10, 23, 28, 24, 26],
+                    carry, own)
+    v01 = jnp.stack([msg, send_x_flip(msg, 1)])
+    v23 = send_x_flip(v01, 2)
+    c1, c3, ut, _ = pin((c1, c3, ut, msg))
     c2 = jnp.concatenate([send_zh(c1[:4], 1), send_zh(c3[4:], -1)])
     near = [jnp.stack([ut, c1, c3]), c2]
     far = [send_core(t) for t in near]
-    cross, base = cross_call(info, v, ginv)
-
-    m = prod_call(info, vs, near + far)
-    r = [m[0], send_y(m[1], 1), send_y(m[2], 2), send_y(m[3], -1)]
+    cross, base = cross_call(plan, v, ginv)
+
+    m = prod_call(plan, [v01, v23], near + far)
+    m2 = send_y(m[2], 2)
+    r = [m[0], send_y(m[1], 1), m2, send_y(m[3], -1)]
     keep, away = sum2_call(r)
     came = send_pair(away)
-    resist, sigma = last_call(info, keep, came, dinv, base)
+    resist, sigma = last_call(plan, keep, came, dinv, base)
     return cross, resist, sigma
 
 

time: 125 us -> 121 us (0.968)
  waiting for transfers between devices: 42.4 us -> 45 us
  Pallas kernels: 24.9 us -> 22.5 us
  starting transfers between devices: 45.6 us -> 44.2 us
    ppermute x4, waiting for transfers between devices: 18.2 us -> 12.1 us  [send_zh(): lax.ppermute(v, AXES, table(lambda x, y, zl, zh, core: (x, y, zl, (zh + d...]
    ppermute x3 -> x2, waiting for transfers between devices: 0.83 us -> 4.76 us  [send_x_flip(): lax.ppermute(v, AXES, table(lambda x, y, zl, zh, core: (x ^ bit, y, zl, z...]
    ppermute x14, waiting for transfers between devices: 8.23 us -> 10.2 us  [send_pq(): return lax.ppermute(v, AXES, table(move))]
    ppermute x3 -> x2, starting transfers between devices: 4.17 us -> 2.35 us  [send_x_flip(): lax.ppermute(v, AXES, table(lambda x, y, zl, zh, core: (x ^ bit, y, zl, z...]
    ppermute x2 -> x3, waiting for transfers between devices: 3.22 us -> 5.02 us  [send_pair(): lax.ppermute(v, AXES, table(lambda x, y, zl, zh, core: (x, y, 1 - zl, zh,...]
    ppermute x2 -> x3, starting transfers between devices: 2.9 us -> 4.38 us  [send_pair(): lax.ppermute(v, AXES, table(lambda x, y, zl, zh, core: (x, y, 1 - zl, zh,...]
    pallas_call x1, Pallas kernels: 2.79 us -> 1.41 us  [cross_call(): pl.pallas_call(cross_kernel, grid_spec=pltpu.PrefetchScalarGridSpec(num_s...]
    unnamed x17 -> x15, local copies, waits for them, and re-layouts: 6.62 us -> 5.39 us
  transfers between devices with their start and end apart: 28 -> 28, of which waited for: 14 -> 16; matrix products, arithmetic and copies ran while one was open for 2% -> 0% of each run, Pallas kernels for 15% -> 15%
where the time goes in v4:
time: 121 us; the launch traced here: 120 us
  waiting for transfers between devices  45 us (37%)
  starting transfers between devices  44.2 us (37%)
  Pallas kernels  22.5 us (19%)
  local copies, waits for them, and re-layouts  5.63 us (5%)
  other arithmetic  1.36 us (1%)
    ppermute x14, starting transfers between devices, send_pq(): return lax.ppermute(v, AXES, table(move))  22.4 us
    ppermute x4, waiting for transfers between devices, send_zh(): lax.ppermute(v, AXES, table(lambda x, y, zl, zh, core: (x, y, zl, (zh + d...  12.1 us
    ppermute x3, waiting for transfers between devices, send_y(): lax.ppermute(v, AXES, table(lambda x, y, zl, zh, core: (x, (y + d) % 4, z...  11.3 us
    pallas_call x4, Pallas kernels, v_call(): pl.pallas_call(functools.partial(v_kernel, first, last, groups), in_specs...  10.7 us
    ppermute x4, starting transfers between devices, send_zh(): lax.ppermute(v, AXES, table(lambda x, y, zl, zh, core: (x, y, zl, (zh + d...  10.2 us
    ppermute x14, waiting for transfers between devices, send_pq(): return lax.ppermute(v, AXES, table(move))  10.2 us
    unnamed x15, local copies, waits for them, and re-layouts  5.39 us
    ppermute x3, waiting for transfers between devices, send_pair(): lax.ppermute(v, AXES, table(lambda x, y, zl, zh, core: (x, y, 1 - zl, zh,...  5.02 us
  transfers between devices with their start and end apart: 28, of which 16 were waited for; matrix products, arithmetic and copies ran while one was open for 0% of the time, Pallas kernels for 15%

profile of v4, /device:TPU:2, one launch (start us, length us, event | category | flops | bytes accessed | tf_op | source)
XLA Modules:
  0.0 119.6 jit_solution(14091461673880080467)
XLA Ops:
  0.6 2.0 %collective-permute-start.3 = (f32[2,128,256]{2,1,0:T(8,128)}, f32[2,128,256]{2,1,0:T(8,128)S(1)}, u32[]{:S(2)}, u32[]{:S(2)}) collective-permute-start(f32[2,128,256]{2,1,0:T(8,128)} %param.7), channel_id=1, source_target_pairs={{0,32},{1,33},{2,34},{3,35},{4,36},{5,37},{6,38},{7,39},{8,40},{9,... | collective-permute-start | bytes 786440 | tf_op jit(solution)/shard_map/ppermute | solution.py:57
  2.6 1.5 %collective-permute-start = (f32[2,128,256]{2,1,0:T(8,128)}, f32[2,128,256]{2,1,0:T(8,128)S(1)}, u32[]{:S(2)}, u32[]{:S(2)}) collective-permute-start(f32[2,128,256]{2,1,0:T(8,128)} %param.7), channel_id=1, source_target_pairs={{0,8},{1,65},{2,10},{3,67},{4,12},{5,69},{6,14},{7,71},{8,16},{9,7... | collective-permute-start | bytes 786440 | tf_op jit(solution)/shard_map/ppermute | solution.py:41
  4.1 1.1 collective-permute-start.1
  5.2 2.2 %collective-permute-start.2 = (f32[2,128,256]{2,1,0:T(8,128)}, f32[2,128,256]{2,1,0:T(8,128)S(1)}, u32[]{:S(2)}, u32[]{:S(2)}) collective-permute-start(f32[2,128,256]{2,1,0:T(8,128)} %param.7), channel_id=1, source_target_pairs={{0,24},{1,193},{2,26},{3,195},{4,28},{5,197},{6,30},{7,199},{8,0},... | collective-permute-start | bytes 786440 | tf_op jit(solution)/shard_map/ppermute | solution.py:41
  7.4 1.8 %collective-permute-done.3 = f32[2,128,256]{2,1,0:T(8,128)S(1)} collective-permute-done((f32[2,128,256]{2,1,0:T(8,128)}, f32[2,128,256]{2,1,0:T(8,128)S(1)}, u32[]{:S(2)}, u32[]{:S(2)}) %collective-permute-start.3) | collective-permute-done | bytes 262176 | tf_op jit(solution)/shard_map/ppermute | solution.py:57
  9.2 1.5 %collective-permute-start.4 = (f32[2,128,256]{2,1,0:T(8,128)S(1)}, f32[2,128,256]{2,1,0:T(8,128)S(1)}, u32[]{:S(2)}, u32[]{:S(2)}) collective-permute-start(f32[2,128,256]{2,1,0:T(8,128)S(1)} %collective-permute-done.3), channel_id=1, source_target_pairs={{0,8},{1,65},{2,10},{3,67},{4,12},{5,69},{6,14},{7,71},{8,16},{9,7... | collective-permute-start | bytes 786440 | tf_op jit(solution)/shard_map/ppermute | solution.py:41
  10.6 1.1 collective-permute-start.5
  11.8 2.2 %collective-permute-start.6 = (f32[2,128,256]{2,1,0:T(8,128)S(1)}, f32[2,128,256]{2,1,0:T(8,128)S(1)}, u32[]{:S(2)}, u32[]{:S(2)}) collective-permute-start(f32[2,128,256]{2,1,0:T(8,128)S(1)} %collective-permute-done.3), channel_id=1, source_target_pairs={{0,24},{1,193},{2,26},{3,195},{4,28},{5,197},{6,30},{7,199},{8,0},... | collective-permute-start | bytes 786440 | tf_op jit(solution)/shard_map/ppermute | solution.py:41
  13.9 0.7 collective-permute-done.2
  14.6 0.9 collective-permute-done.4
  15.5 3.1 %collective-permute-done.5 = f32[2,128,256]{2,1,0:T(8,128)S(1)} collective-permute-done((f32[2,128,256]{2,1,0:T(8,128)S(1)}, f32[2,128,256]{2,1,0:T(8,128)S(1)}, u32[]{:S(2)}, u32[]{:S(2)}) %collective-permute-start.5) | collective-permute-done | bytes 262176 | tf_op jit(solution)/shard_map/ppermute | solution.py:41
  18.6 2.3 %collective-permute-done.6 = f32[2,128,256]{2,1,0:T(8,128)S(1)} collective-permute-done((f32[2,128,256]{2,1,0:T(8,128)S(1)}, f32[2,128,256]{2,1,0:T(8,128)S(1)}, u32[]{:S(2)}, u32[]{:S(2)}) %collective-permute-start.6) | collective-permute-done | bytes 262176 | tf_op jit(solution)/shard_map/ppermute | solution.py:41
  20.9 1.0 pad_maximum_fusion.refs_1_.refs_0_
  22.0 1.7 %collective-permute-start.7 = (f32[4,2,128,256]{3,2,1,0:T(8,128)S(1)}, f32[4,2,128,256]{3,2,1,0:T(8,128)S(1)}, u32[]{:S(2)}, u32[]{:S(2)}) collective-permute-start(f32[4,2,128,256]{3,2,1,0:T(8,128)S(1)} %pad_maximum_fusion.refs_1_.refs_0_), channel_id=1, source_target_pairs={{0,64},{1,9},{2,66},{3,11},{4,68},{5,13},{6,70},{7,15},{8,72},{9,1... | collective-permute-start | bytes 3145736 | tf_op jit(solution)/shard_map/ppermute | solution.py:41
  23.6 1.7 %collective-permute-start.8 = (f32[4,2,128,256]{3,2,1,0:T(8,128)S(1)}, f32[4,2,128,256]{3,2,1,0:T(8,128)S(1)}, u32[]{:S(2)}, u32[]{:S(2)}) collective-permute-start(f32[4,2,128,256]{3,2,1,0:T(8,128)S(1)} %pad_maximum_fusion.refs_1_.refs_0_), channel_id=1, source_target_pairs={{0,192},{1,25},{2,194},{3,27},{4,196},{5,29},{6,198},{7,31},{8,200... | collective-permute-start | bytes 3145736 | tf_op jit(solution)/shard_map/ppermute | solution.py:41
  25.3 0.1 pad_maximum_fusion.3
  25.4 0.4 collective-permute-start.12
  25.9 2.9 %collective-permute-start.13 = (f32[3,2,128,256]{3,2,1,0:T(8,128)S(1)}, f32[3,2,128,256]{3,2,1,0:T(8,128)S(1)}, u32[]{:S(2)}, u32[]{:S(2)}) collective-permute-start(f32[3,2,128,256]{3,2,1,0:T(8,128)S(1)} %get-tuple-element.87), channel_id=1, source_target_pairs={{0,192},{1,25},{2,194},{3,27},{4,196},{5,29},{6,198},{7,31},{8,200... | collective-permute-start | bytes 2359304 | tf_op jit(solution)/shard_map/ppermute | solution.py:41
  28.7 0.7 copy-done.2
  29.4 0.7 copy-done.3
  30.1 0.7 copy-done.4
  30.7 2.4 %plan.1 = s32[160]{0:T(256)S(1)} custom-call(s32[2,16]{1,0:T(2,128)S(1)} %copy-done.2, s32[2]{0:T(128)S(1)} %copy-done.3, s32[2]{0:T(128)S(1)} %copy-done.4), custom_call_target="tpu_custom_call" | custom-call | tf_op jit(solution)/shard_map/plan/pallas_call | solution.py:134
  33.2 0.0 copy-start
  33.2 3.4 %copy-done = f32[256,8192]{1,0:T(8,128)S(1)} copy-done((f32[256,8192]{1,0:T(8,128)S(1)}, f32[256,8192]{1,0:T(8,128)}, u32[]{:S(2)}) %copy-start) | copy-done | bytes 8388632
  36.5 1.6 %v_part.4.refs_4_ = f32[2,256,256]{2,1,0:T(8,128)S(1)} custom-call(s32[160]{0:T(256)S(1)} %plan.1, f32[256,8192]{1,0:T(8,128)S(1)} %copy-done, f32[4,2,128,256]{3,2,1,0:T(8,128)S(1)} %pad_maximum_fusion.refs_1_.refs_0_), custom_call_target="tpu_custom_call" | custom-call | flops 402653184 | bytes 16777216 | tf_op jit(solution)/shard_map/v_part/pallas_call | solution.py:260
  38.1 0.3 collective-permute-done.8.refs_3_
  38.6 1.8 %collective-permute-start.11 = (f32[2,2,128,256]{3,2,1,0:T(8,128)S(1)}, f32[2,2,128,256]{3,2,1,0:T(8,128)S(1)}, u32[]{:S(2)}, u32[]{:S(2)}) collective-permute-start(f32[2,2,128,256]{3,2,1,0:T(8,128)S(1)} %pad_maximum_fusion.6), channel_id=1, source_target_pairs={{0,32},{1,33},{2,34},{3,35},{4,36},{5,37},{6,38},{7,39},{8,40},{9,... | collective-permute-start | bytes 1572872 | tf_op jit(solution)/shard_map/ppermute | solution.py:57
  40.4 2.9 %collective-permute-start.10 = (f32[2,2,128,256]{3,2,1,0:T(8,128)S(1)}, f32[2,2,128,256]{3,2,1,0:T(8,128)S(1)}, u32[]{:S(2)}, u32[]{:S(2)}) collective-permute-start(f32[2,2,128,256]{3,2,1,0:T(8,128)S(1)} %slice.35), channel_id=1, source_target_pairs={{0,192},{1,25},{2,194},{3,27},{4,196},{5,29},{6,198},{7,31},{8,200... | collective-permute-start | bytes 1572872 | tf_op jit(solution)/shard_map/ppermute | solution.py:41
  43.3 0.0 collective-permute-start.9
  43.3 0.1 pad_maximum_fusion.1.refs_1_
  43.4 3.5 %v_part.5.refs_3_ = f32[2,256,256]{2,1,0:T(8,128)S(1)} custom-call(s32[160]{0:T(256)S(1)} %plan.1, f32[256,8192]{1,0:T(8,128)S(1)} %copy-done, f32[4,2,128,256]{3,2,1,0:T(8,128)S(1)} %pad_maximum_fusion.1.refs_1_, f32[4,2,128,256]{3,2,1,0:T(8,128)S(1)} %collective-permute-done.7.refs_2_, f32[4,2,128,256]{3,2,1,0:T(8,128)S(1)} %collective-permute-done.8.refs_3_, ...), custom_call_target="tpu_custom_call" | custom-call | flops 1207959552 | bytes 50331648 | tf_op jit(solution)/shard_map/v_part/pallas_call | solution.py:260
  46.9 1.6 %collective-permute-start.14 = (f32[2,2,128,256]{3,2,1,0:T(8,128)S(1)}, f32[2,2,128,256]{3,2,1,0:T(8,128)S(1)}, u32[]{:S(2)}, u32[]{:S(2)}) collective-permute-start(f32[2,2,128,256]{3,2,1,0:T(8,128)S(1)} %slice.40), channel_id=1, source_target_pairs={{0,64},{1,9},{2,66},{3,11},{4,68},{5,13},{6,70},{7,15},{8,72},{9,1... | collective-permute-start | bytes 1572872 | tf_op jit(solution)/shard_map/ppermute | solution.py:41
  48.6 1.8 %collective-permute-start.15 = (f32[2,2,128,256]{3,2,1,0:T(8,128)S(1)}, f32[2,2,128,256]{3,2,1,0:T(8,128)S(1)}, u32[]{:S(2)}, u32[]{:S(2)}) collective-permute-start(f32[2,2,128,256]{3,2,1,0:T(8,128)S(1)} %slice.41), channel_id=1, source_target_pairs={{0,192},{1,25},{2,194},{3,27},{4,196},{5,29},{6,198},{7,31},{8,200... | collective-permute-start | bytes 1572872 | tf_op jit(solution)/shard_map/ppermute | solution.py:41
  50.4 2.3 %v_part.6.refs_7_ = f32[2,256,256]{2,1,0:T(8,128)S(1)} custom-call(s32[160]{0:T(256)S(1)} %plan.1, f32[256,8192]{1,0:T(8,128)S(1)} %copy-done, f32[3,2,128,256]{3,2,1,0:T(8,128)S(1)} %collective-permute-done.12.refs_1_.refs_4_, f32[3,2,128,256]{3,2,1,0:T(8,128)S(1)} %collective-permute-done.13.refs_2_.refs_7_, f32[2,256,256]{2,1,0:T(8,128)S(1)} %v_part.5.refs_3_), custom_call_target="tpu_custom_call" | custom-call | flops 603979776 | bytes 25165824 | tf_op jit(solution)/shard_map/v_part/pallas_call | solution.py:260
  52.7 1.0 collective-permute-done.9.refs_8_.refs_1_
  53.7 3.7 %u_rows.2 = (f32[256,256]{1,0:T(8,128)S(1)}, f32[8,64,128]{2,1,0:T(8,128)S(1)}) custom-call(s32[160]{0:T(256)S(1)} %plan.1, f32[4,2,128,256]{3,2,1,0:T(8,128)S(1)} %pad_maximum_fusion.refs_1_.refs_0_, f32[4,2,128,256]{3,2,1,0:T(8,128)S(1)} %pad_maximum_fusion.1.refs_1_, f32[4,2,128,256]{3,2,1,0:T(8,128)S(1)} %collective-permute-done.7.refs_2_, ...), custom_call_target="tpu_custom_call" | custom-call | tf_op jit(solution)/shard_map/u_rows/pallas_call | solution.py:189
  57.4 1.9 %collective-permute-done.14.refs_0_.refs_5_ = f32[2,2,128,256]{3,2,1,0:T(8,128)S(1)} collective-permute-done((f32[2,2,128,256]{3,2,1,0:T(8,128)S(1)}, f32[2,2,128,256]{3,2,1,0:T(8,128)S(1)}, u32[]{:S(2)}, u32[]{:S(2)}) %collective-permute-start.14) | collective-permute-done | bytes 524320 | tf_op jit(solution)/shard_map/ppermute | solution.py:41
  59.3 0.9 u_rows.3
  60.2 3.3 %collective-permute-start.18 = (f32[8,64,128]{2,1,0:T(8,128)S(1)}, f32[8,64,128]{2,1,0:T(8,128)S(1)}, u32[]{:S(2)}, u32[]{:S(2)}) collective-permute-start(f32[8,64,128]{2,1,0:T(8,128)S(1)} %get-tuple-element.73), channel_id=1, source_target_pairs={{0,2},{1,3},{2,4},{3,5},{4,6},{5,7},{6,0},{7,1},{8,10},{9,11},{10,... | collective-permute-start | bytes 786440 | tf_op jit(solution)/shard_map/ppermute | solution.py:65
  63.6 2.4 %collective-permute-start.19 = (f32[8,64,128]{2,1,0:T(8,128)S(1)}, f32[8,64,128]{2,1,0:T(8,128)S(1)}, u32[]{:S(2)}, u32[]{:S(2)}) collective-permute-start(f32[8,64,128]{2,1,0:T(8,128)S(1)} %get-tuple-element.73), channel_id=1, source_target_pairs={{0,6},{1,7},{2,0},{3,1},{4,2},{5,3},{6,4},{7,5},{8,14},{9,15},{10,... | collective-permute-start | bytes 786440 | tf_op jit(solution)/shard_map/ppermute | solution.py:65
  66.0 3.4 %v_part.7 = (f32[2,256,256]{2,1,0:T(8,128)S(1)}, f32[264,256]{1,0:T(8,128)S(1)}) custom-call(s32[160]{0:T(256)S(1)} %plan.1, f32[256,8192]{1,0:T(8,128)S(1)} %copy-done, f32[2,2,128,256]{3,2,1,0:T(8,128)S(1)} %collective-permute-done.9.refs_8_.refs_1_, f32[2,2,128,256]{3,2,1,0:T(8,128)S(1)} %collective-permute-done.10.refs_9_.refs_2_, ...), custom_call_target="tpu_custom_call" | custom-call | flops 1006632960 | bytes 41943040 | tf_op jit(solution)/shard_map/v_part/pallas_call | solution.py:260
  69.4 0.2 collective-permute-start.16
  69.7 5.1 %collective-permute-done.18 = f32[8,64,128]{2,1,0:T(8,128)S(1)} collective-permute-done((f32[8,64,128]{2,1,0:T(8,128)S(1)}, f32[8,64,128]{2,1,0:T(8,128)S(1)}, u32[]{:S(2)}, u32[]{:S(2)}) %collective-permute-start.18) | collective-permute-done | bytes 262176 | tf_op jit(solution)/shard_map/ppermute | solution.py:65
  74.8 0.1 pad_maximum_fusion.4.near
  74.8 0.1 collective-permute-start.22
  74.9 4.1 %collective-permute-start.20 = (f32[4,64,128]{2,1,0:T(8,128)S(1)}, f32[4,64,128]{2,1,0:T(8,128)S(1)}, u32[]{:S(2)}, u32[]{:S(2)}) collective-permute-start(f32[4,64,128]{2,1,0:T(8,128)S(1)} %slice.42), channel_id=1, source_target_pairs={{0,2},{1,3},{2,4},{3,5},{4,6},{5,7},{6,0},{7,1},{8,10},{9,11},{10,... | collective-permute-start | bytes 393224 | tf_op jit(solution)/shard_map/ppermute | solution.py:65
  79.1 2.1 %collective-permute-start.17 = (f32[2,264,256]{2,1,0:T(8,128)S(1)}, f32[2,264,256]{2,1,0:T(8,128)S(1)}, u32[]{:S(2)}, u32[]{:S(2)}) collective-permute-start(f32[2,264,256]{2,1,0:T(8,128)S(1)} %pad_maximum_fusion.5.v01), channel_id=1, source_target_pairs={{0,16},{1,17},{2,18},{3,19},{4,20},{5,21},{6,22},{7,23},{8,24},{9,... | collective-permute-start | bytes 1622024 | tf_op jit(solution)/shard_map/ppermute | solution.py:49
  81.2 0.4 collective-permute-start.21
  81.6 3.4 %collective-permute-done.20 = f32[4,64,128]{2,1,0:T(8,128)S(1)} collective-permute-done((f32[4,64,128]{2,1,0:T(8,128)S(1)}, f32[4,64,128]{2,1,0:T(8,128)S(1)}, u32[]{:S(2)}, u32[]{:S(2)}) %collective-permute-start.20) | collective-permute-done | bytes 131104 | tf_op jit(solution)/shard_map/ppermute | solution.py:65
  85.0 3.6 %collective-permute-done.21 = f32[4,64,128]{2,1,0:T(8,128)S(1)} collective-permute-done((f32[4,64,128]{2,1,0:T(8,128)S(1)}, f32[4,64,128]{2,1,0:T(8,128)S(1)}, u32[]{:S(2)}, u32[]{:S(2)}) %collective-permute-start.21) | collective-permute-done | bytes 131104 | tf_op jit(solution)/shard_map/ppermute | solution.py:65
  88.7 0.1 collective-permute-start.23
  88.8 1.5 %collective-permute-done.23.far2 = f32[8,64,128]{2,1,0:T(8,128)S(1)} collective-permute-done((f32[8,64,128]{2,1,0:T(8,128)S(1)}, f32[8,64,128]{2,1,0:T(8,128)S(1)}, u32[]{:S(2)}, u32[]{:S(2)}) %collective-permute-start.23) | collective-permute-done | bytes 262176 | tf_op jit(solution)/shard_map/ppermute | solution.py:61
  90.3 4.8 %collective-permute-done.17.v23 = f32[2,264,256]{2,1,0:T(8,128)S(1)} collective-permute-done((f32[2,264,256]{2,1,0:T(8,128)S(1)}, f32[2,264,256]{2,1,0:T(8,128)S(1)}, u32[]{:S(2)}, u32[]{:S(2)}) %collective-permute-start.17) | collective-permute-done | bytes 540704 | tf_op jit(solution)/shard_map/ppermute | solution.py:49
  95.0 1.8 %product.1 = (f32[272,256]{1,0:T(8,128)S(1)}, f32[272,256]{1,0:T(8,128)S(1)}, f32[272,256]{1,0:T(8,128)S(1)}, f32[272,256]{1,0:T(8,128)S(1)}) custom-call(s32[160]{0:T(256)S(1)} %plan.1, f32[2,264,256]{2,1,0:T(8,128)S(1)} %pad_maximum_fusion.5.v01, f32[2,264,256]{2,1,0:T(8,128)S(1)} %collective-permute-done.17.v23, ...), custom_call_target="tpu_custom_call" | custom-call | flops 805306368 | bytes 5242880 | tf_op jit(solution)/shard_map/product/pallas_call | solution.py:311
  96.9 1.5 %collective-permute-start.24 = (f32[272,256]{1,0:T(8,128)S(1)}, f32[272,256]{1,0:T(8,128)S(1)}, u32[]{:S(2)}, u32[]{:S(2)}) collective-permute-start(f32[272,256]{1,0:T(8,128)S(1)} %get-tuple-element.77), channel_id=1, source_target_pairs={{0,64},{1,65},{2,66},{3,67},{4,68},{5,69},{6,70},{7,71},{8,72},{9,... | collective-permute-start | bytes 835592 | tf_op jit(solution)/shard_map/ppermute | solution.py:53
  98.4 2.5 %collective-permute-start.25 = (f32[272,256]{1,0:T(8,128)S(1)}, f32[272,256]{1,0:T(8,128)S(1)}, u32[]{:S(2)}, u32[]{:S(2)}) collective-permute-start(f32[272,256]{1,0:T(8,128)S(1)} %get-tuple-element.78), channel_id=1, source_target_pairs={{0,128},{1,129},{2,130},{3,131},{4,132},{5,133},{6,134},{7,135},{8... | collective-permute-start | bytes 835592 | tf_op jit(solution)/shard_map/ppermute | solution.py:53
  100.9 0.6 collective-permute-start.26
  101.5 5.6 %collective-permute-done.24.r1 = f32[272,256]{1,0:T(8,128)S(1)} collective-permute-done((f32[272,256]{1,0:T(8,128)S(1)}, f32[272,256]{1,0:T(8,128)S(1)}, u32[]{:S(2)}, u32[]{:S(2)}) %collective-permute-start.24) | collective-permute-done | bytes 278560 | tf_op jit(solution)/shard_map/ppermute | solution.py:53
  107.1 5.7 %collective-permute-done.25.r2 = f32[272,256]{1,0:T(8,128)S(1)} collective-permute-done((f32[272,256]{1,0:T(8,128)S(1)}, f32[272,256]{1,0:T(8,128)S(1)}, u32[]{:S(2)}, u32[]{:S(2)}) %collective-permute-start.25) | collective-permute-done | bytes 278560 | tf_op jit(solution)/shard_map/ppermute | solution.py:53
  112.8 0.1 sum_second.1
  112.8 0.6 collective-permute-start.27
  113.4 1.4 %cross.1 = (f32[2,256,256]{2,1,0:T(8,128)}, f32[2,256,256]{2,1,0:T(8,128)S(1)}) custom-call(s32[160]{0:T(256)S(1)} %plan.1, f32[2,256,256]{2,1,0:T(8,128)S(1)} %get-tuple-element.69.v, f32[256,8192]{1,0:T(8,128)S(1)} %bitcast.14), custom_call_target="tpu_custom_call" | custom-call | tf_op jit(solution)/shard_map/cross/pallas_call | solution.py:358
  114.8 3.3 %collective-permute-done.27.came = f32[144,256]{1,0:T(8,128)S(1)} collective-permute-done((f32[144,256]{1,0:T(8,128)S(1)}, f32[144,256]{1,0:T(8,128)S(1)}, u32[]{:S(2)}, u32[]{:S(2)}) %collective-permute-start.27) | collective-permute-done | bytes 147488 | tf_op jit(solution)/shard_map/ppermute | solution.py:57
  118.1 1.5 %last.1 = (f32[2,256,256]{2,1,0:T(8,128)}, f32[64,2,256]{2,1,0:T(2,128)}) custom-call(s32[160]{0:T(256)S(1)} %plan.1, f32[144,256]{1,0:T(8,128)S(1)} %get-tuple-element.80.keep, f32[144,256]{1,0:T(8,128)S(1)} %collective-permute-done.27.came, f32[2,256]{1,0:T(2,128)S(1)} %copy-done.1, f32[2,256,256]{2,1,0:T(8,128)S(1)} %get-tuple-element.82.base), custom_call_target="tpu_custom_call" | custom-call | tf_op jit(solution)/shard_map/last/pallas_call | solution.py:391
  (35 shorter events, 0.4 us)
Async XLA Ops:
  0.6 8.5 %collective-permute-start.3 = (f32[2,128,256]{2,1,0:T(8,128)}, f32[2,128,256]{2,1,0:T(8,128)S(1)}, u32[]{:S(2)}, u32[]{:S(2)}) collective-permute-start(f32[2,128,256]{2,1,0:T(8,128)} %param.7), channel_id=1, source_target_pairs={{0,32},{1,33},{2,34},{3,35},{4,36},{5,37},{6,38},{7,39},{8,40},{9,... | collective-permute-start | bytes 786440 | tf_op jit(solution)/shard_map/ppermute | solution.py:57
  2.6 9.1 %collective-permute-start = (f32[2,128,256]{2,1,0:T(8,128)}, f32[2,128,256]{2,1,0:T(8,128)S(1)}, u32[]{:S(2)}, u32[]{:S(2)}) collective-permute-start(f32[2,128,256]{2,1,0:T(8,128)} %param.7), channel_id=1, source_target_pairs={{0,8},{1,65},{2,10},{3,67},{4,12},{5,69},{6,14},{7,71},{8,16},{9,7... | collective-permute-start | bytes 786440 | tf_op jit(solution)/shard_map/ppermute | solution.py:41
  4.1 9.8 %collective-permute-start.1 = (f32[2,128,256]{2,1,0:T(8,128)}, f32[2,128,256]{2,1,0:T(8,128)S(1)}, u32[]{:S(2)}, u32[]{:S(2)}) collective-permute-start(f32[2,128,256]{2,1,0:T(8,128)} %param.7), channel_id=1, source_target_pairs={{0,16},{1,129},{2,18},{3,131},{4,20},{5,133},{6,22},{7,135},{8,24}... | collective-permute-start | bytes 786440 | tf_op jit(solution)/shard_map/ppermute | solution.py:41
  5.2 9.4 %collective-permute-start.2 = (f32[2,128,256]{2,1,0:T(8,128)}, f32[2,128,256]{2,1,0:T(8,128)S(1)}, u32[]{:S(2)}, u32[]{:S(2)}) collective-permute-start(f32[2,128,256]{2,1,0:T(8,128)} %param.7), channel_id=1, source_target_pairs={{0,24},{1,193},{2,26},{3,195},{4,28},{5,197},{6,30},{7,199},{8,0},... | collective-permute-start | bytes 786440 | tf_op jit(solution)/shard_map/ppermute | solution.py:41
  9.2 6.4 %collective-permute-start.4 = (f32[2,128,256]{2,1,0:T(8,128)S(1)}, f32[2,128,256]{2,1,0:T(8,128)S(1)}, u32[]{:S(2)}, u32[]{:S(2)}) collective-permute-start(f32[2,128,256]{2,1,0:T(8,128)S(1)} %collective-permute-done.3), channel_id=1, source_target_pairs={{0,8},{1,65},{2,10},{3,67},{4,12},{5,69},{6,14},{7,71},{8,16},{9,7... | collective-permute-start | bytes 786440 | tf_op jit(solution)/shard_map/ppermute | solution.py:41
  10.6 8.0 %collective-permute-start.5 = (f32[2,128,256]{2,1,0:T(8,128)S(1)}, f32[2,128,256]{2,1,0:T(8,128)S(1)}, u32[]{:S(2)}, u32[]{:S(2)}) collective-permute-start(f32[2,128,256]{2,1,0:T(8,128)S(1)} %collective-permute-done.3), channel_id=1, source_target_pairs={{0,16},{1,129},{2,18},{3,131},{4,20},{5,133},{6,22},{7,135},{8,24}... | collective-permute-start | bytes 786440 | tf_op jit(solution)/shard_map/ppermute | solution.py:41
  11.8 9.2 %collective-permute-start.6 = (f32[2,128,256]{2,1,0:T(8,128)S(1)}, f32[2,128,256]{2,1,0:T(8,128)S(1)}, u32[]{:S(2)}, u32[]{:S(2)}) collective-permute-start(f32[2,128,256]{2,1,0:T(8,128)S(1)} %collective-permute-done.3), channel_id=1, source_target_pairs={{0,24},{1,193},{2,26},{3,195},{4,28},{5,197},{6,30},{7,199},{8,0},... | collective-permute-start | bytes 786440 | tf_op jit(solution)/shard_map/ppermute | solution.py:41
  22.0 16.2 %collective-permute-start.7 = (f32[4,2,128,256]{3,2,1,0:T(8,128)S(1)}, f32[4,2,128,256]{3,2,1,0:T(8,128)S(1)}, u32[]{:S(2)}, u32[]{:S(2)}) collective-permute-start(f32[4,2,128,256]{3,2,1,0:T(8,128)S(1)} %pad_maximum_fusion.refs_1_.refs_0_), channel_id=1, source_target_pairs={{0,64},{1,9},{2,66},{3,11},{4,68},{5,13},{6,70},{7,15},{8,72},{9,1... | collective-permute-start | bytes 3145736 | tf_op jit(solution)/shard_map/ppermute | solution.py:41
  23.6 14.8 %collective-permute-start.8 = (f32[4,2,128,256]{3,2,1,0:T(8,128)S(1)}, f32[4,2,128,256]{3,2,1,0:T(8,128)S(1)}, u32[]{:S(2)}, u32[]{:S(2)}) collective-permute-start(f32[4,2,128,256]{3,2,1,0:T(8,128)S(1)} %pad_maximum_fusion.refs_1_.refs_0_), channel_id=1, source_target_pairs={{0,192},{1,25},{2,194},{3,27},{4,196},{5,29},{6,198},{7,31},{8,200... | collective-permute-start | bytes 3145736 | tf_op jit(solution)/shard_map/ppermute | solution.py:41
  25.4 21.4 %collective-permute-start.12 = (f32[3,2,128,256]{3,2,1,0:T(8,128)S(1)}, f32[3,2,128,256]{3,2,1,0:T(8,128)S(1)}, u32[]{:S(2)}, u32[]{:S(2)}) collective-permute-start(f32[3,2,128,256]{3,2,1,0:T(8,128)S(1)} %get-tuple-element.88), channel_id=1, source_target_pairs={{0,64},{1,9},{2,66},{3,11},{4,68},{5,13},{6,70},{7,15},{8,72},{9,1... | collective-permute-start | bytes 2359304 | tf_op jit(solution)/shard_map/ppermute | solution.py:41
  25.9 21.0 %collective-permute-start.13 = (f32[3,2,128,256]{3,2,1,0:T(8,128)S(1)}, f32[3,2,128,256]{3,2,1,0:T(8,128)S(1)}, u32[]{:S(2)}, u32[]{:S(2)}) collective-permute-start(f32[3,2,128,256]{3,2,1,0:T(8,128)S(1)} %get-tuple-element.87), channel_id=1, source_target_pairs={{0,192},{1,25},{2,194},{3,27},{4,196},{5,29},{6,198},{7,31},{8,200... | collective-permute-start | bytes 2359304 | tf_op jit(solution)/shard_map/ppermute | solution.py:41
  28.7 0.7 copy-start.2
  29.4 0.7 copy-start.3
  30.1 0.7 copy-start.4
  33.2 3.4 %copy-start = (f32[256,8192]{1,0:T(8,128)S(1)}, f32[256,8192]{1,0:T(8,128)}, u32[]{:S(2)}) copy-start(f32[256,8192]{1,0:T(8,128)} %block.1) | copy-start | bytes 25165828
  38.6 14.1 %collective-permute-start.11 = (f32[2,2,128,256]{3,2,1,0:T(8,128)S(1)}, f32[2,2,128,256]{3,2,1,0:T(8,128)S(1)}, u32[]{:S(2)}, u32[]{:S(2)}) collective-permute-start(f32[2,2,128,256]{3,2,1,0:T(8,128)S(1)} %pad_maximum_fusion.6), channel_id=1, source_target_pairs={{0,32},{1,33},{2,34},{3,35},{4,36},{5,37},{6,38},{7,39},{8,40},{9,... | collective-permute-start | bytes 1572872 | tf_op jit(solution)/shard_map/ppermute | solution.py:57
  40.4 12.2 %collective-permute-start.10 = (f32[2,2,128,256]{3,2,1,0:T(8,128)S(1)}, f32[2,2,128,256]{3,2,1,0:T(8,128)S(1)}, u32[]{:S(2)}, u32[]{:S(2)}) collective-permute-start(f32[2,2,128,256]{3,2,1,0:T(8,128)S(1)} %slice.35), channel_id=1, source_target_pairs={{0,192},{1,25},{2,194},{3,27},{4,196},{5,29},{6,198},{7,31},{8,200... | collective-permute-start | bytes 1572872 | tf_op jit(solution)/shard_map/ppermute | solution.py:41
  43.3 10.4 %collective-permute-start.9 = (f32[2,2,128,256]{3,2,1,0:T(8,128)S(1)}, f32[2,2,128,256]{3,2,1,0:T(8,128)S(1)}, u32[]{:S(2)}, u32[]{:S(2)}) collective-permute-start(f32[2,2,128,256]{3,2,1,0:T(8,128)S(1)} %slice.34), channel_id=1, source_target_pairs={{0,64},{1,9},{2,66},{3,11},{4,68},{5,13},{6,70},{7,15},{8,72},{9,1... | collective-permute-start | bytes 1572872 | tf_op jit(solution)/shard_map/ppermute | solution.py:41
  46.9 12.4 %collective-permute-start.14 = (f32[2,2,128,256]{3,2,1,0:T(8,128)S(1)}, f32[2,2,128,256]{3,2,1,0:T(8,128)S(1)}, u32[]{:S(2)}, u32[]{:S(2)}) collective-permute-start(f32[2,2,128,256]{3,2,1,0:T(8,128)S(1)} %slice.40), channel_id=1, source_target_pairs={{0,64},{1,9},{2,66},{3,11},{4,68},{5,13},{6,70},{7,15},{8,72},{9,1... | collective-permute-start | bytes 1572872 | tf_op jit(solution)/shard_map/ppermute | solution.py:41
  48.6 10.7 %collective-permute-start.15 = (f32[2,2,128,256]{3,2,1,0:T(8,128)S(1)}, f32[2,2,128,256]{3,2,1,0:T(8,128)S(1)}, u32[]{:S(2)}, u32[]{:S(2)}) collective-permute-start(f32[2,2,128,256]{3,2,1,0:T(8,128)S(1)} %slice.41), channel_id=1, source_target_pairs={{0,192},{1,25},{2,194},{3,27},{4,196},{5,29},{6,198},{7,31},{8,200... | collective-permute-start | bytes 1572872 | tf_op jit(solution)/shard_map/ppermute | solution.py:41
  60.2 14.5 %collective-permute-start.18 = (f32[8,64,128]{2,1,0:T(8,128)S(1)}, f32[8,64,128]{2,1,0:T(8,128)S(1)}, u32[]{:S(2)}, u32[]{:S(2)}) collective-permute-start(f32[8,64,128]{2,1,0:T(8,128)S(1)} %get-tuple-element.73), channel_id=1, source_target_pairs={{0,2},{1,3},{2,4},{3,5},{4,6},{5,7},{6,0},{7,1},{8,10},{9,11},{10,... | collective-permute-start | bytes 786440 | tf_op jit(solution)/shard_map/ppermute | solution.py:65
  63.6 11.2 %collective-permute-start.19 = (f32[8,64,128]{2,1,0:T(8,128)S(1)}, f32[8,64,128]{2,1,0:T(8,128)S(1)}, u32[]{:S(2)}, u32[]{:S(2)}) collective-permute-start(f32[8,64,128]{2,1,0:T(8,128)S(1)} %get-tuple-element.73), channel_id=1, source_target_pairs={{0,6},{1,7},{2,0},{3,1},{4,2},{5,3},{6,4},{7,5},{8,14},{9,15},{10,... | collective-permute-start | bytes 786440 | tf_op jit(solution)/shard_map/ppermute | solution.py:65
  66.0 47.4 %slice-start = ((s8[8388608]{0:T(1024)(128)(4,1)}), s8[4194304]{0:T(1024)(128)(4,1)S(1)}, s32[]{:S(2)}) async-start(s8[8388608]{0:T(1024)(128)(4,1)} %bitcast.13), calls=%async_computation | async-start | bytes 8388608
  66.0 47.4 %slice-start.1 = ((s8[8388608]{0:T(1024)(128)(4,1)}), s8[4194304]{0:T(1024)(128)(4,1)S(1)}, s32[]{:S(2)}) async-start(s8[8388608]{0:T(1024)(128)(4,1)} %bitcast.13), calls=%async_computation.1 | async-start | bytes 8388608
  69.4 9.6 %collective-permute-start.16 = (f32[264,256]{1,0:T(8,128)S(1)}, f32[264,256]{1,0:T(8,128)S(1)}, u32[]{:S(2)}, u32[]{:S(2)}) collective-permute-start(f32[264,256]{1,0:T(8,128)S(1)} %get-tuple-element.71), channel_id=1, source_target_pairs={{0,8},{1,9},{2,10},{3,11},{4,12},{5,13},{6,14},{7,15},{8,0},{9,1},... | collective-permute-start | bytes 811016 | tf_op jit(solution)/shard_map/ppermute | solution.py:49
  74.8 43.3 %copy-start.1 = (f32[2,256]{1,0:T(2,128)S(1)}, f32[2,256]{1,0:T(2,128)}, u32[]{:S(2)}) copy-start(f32[2,256]{1,0:T(2,128)} %dinv.1) | copy-start | bytes 6148
  74.8 20.2 %collective-permute-start.22 = (f32[3,8,64,128]{3,2,1,0:T(8,128)S(1)}, f32[3,8,64,128]{3,2,1,0:T(8,128)S(1)}, u32[]{:S(2)}, u32[]{:S(2)}) collective-permute-start(f32[3,8,64,128]{3,2,1,0:T(8,128)S(1)} %pad_maximum_fusion.4.near), channel_id=1, source_target_pairs={{0,1},{1,0},{2,3},{3,2},{4,5},{5,4},{6,7},{7,6},{8,9},{9,8},{10,11... | collective-permute-start | bytes 2359304 | tf_op jit(solution)/shard_map/ppermute | solution.py:61
  74.9 10.1 %collective-permute-start.20 = (f32[4,64,128]{2,1,0:T(8,128)S(1)}, f32[4,64,128]{2,1,0:T(8,128)S(1)}, u32[]{:S(2)}, u32[]{:S(2)}) collective-permute-start(f32[4,64,128]{2,1,0:T(8,128)S(1)} %slice.42), channel_id=1, source_target_pairs={{0,2},{1,3},{2,4},{3,5},{4,6},{5,7},{6,0},{7,1},{8,10},{9,11},{10,... | collective-permute-start | bytes 393224 | tf_op jit(solution)/shard_map/ppermute | solution.py:65
  79.1 16.0 %collective-permute-start.17 = (f32[2,264,256]{2,1,0:T(8,128)S(1)}, f32[2,264,256]{2,1,0:T(8,128)S(1)}, u32[]{:S(2)}, u32[]{:S(2)}) collective-permute-start(f32[2,264,256]{2,1,0:T(8,128)S(1)} %pad_maximum_fusion.5.v01), channel_id=1, source_target_pairs={{0,16},{1,17},{2,18},{3,19},{4,20},{5,21},{6,22},{7,23},{8,24},{9,... | collective-permute-start | bytes 1622024 | tf_op jit(solution)/shard_map/ppermute | solution.py:49
  81.2 7.4 %collective-permute-start.21 = (f32[4,64,128]{2,1,0:T(8,128)S(1)}, f32[4,64,128]{2,1,0:T(8,128)S(1)}, u32[]{:S(2)}, u32[]{:S(2)}) collective-permute-start(f32[4,64,128]{2,1,0:T(8,128)S(1)} %slice.43), channel_id=1, source_target_pairs={{0,6},{1,7},{2,0},{3,1},{4,2},{5,3},{6,4},{7,5},{8,14},{9,15},{10,... | collective-permute-start | bytes 393224 | tf_op jit(solution)/shard_map/ppermute | solution.py:65
  88.7 1.6 %collective-permute-start.23 = (f32[8,64,128]{2,1,0:T(8,128)S(1)}, f32[8,64,128]{2,1,0:T(8,128)S(1)}, u32[]{:S(2)}, u32[]{:S(2)}) collective-permute-start(f32[8,64,128]{2,1,0:T(8,128)S(1)} %constant_dynamic-update-slice_fusion.near2), channel_id=1, source_target_pairs={{0,1},{1,0},{2,3},{3,2},{4,5},{5,4},{6,7},{7,6},{8,9},{9,8},{10,11... | collective-permute-start | bytes 786440 | tf_op jit(solution)/shard_map/ppermute | solution.py:61
  96.9 10.2 %collective-permute-start.24 = (f32[272,256]{1,0:T(8,128)S(1)}, f32[272,256]{1,0:T(8,128)S(1)}, u32[]{:S(2)}, u32[]{:S(2)}) collective-permute-start(f32[272,256]{1,0:T(8,128)S(1)} %get-tuple-element.77), channel_id=1, source_target_pairs={{0,64},{1,65},{2,66},{3,67},{4,68},{5,69},{6,70},{7,71},{8,72},{9,... | collective-permute-start | bytes 835592 | tf_op jit(solution)/shard_map/ppermute | solution.py:53
  98.4 14.4 %collective-permute-start.25 = (f32[272,256]{1,0:T(8,128)S(1)}, f32[272,256]{1,0:T(8,128)S(1)}, u32[]{:S(2)}, u32[]{:S(2)}) collective-permute-start(f32[272,256]{1,0:T(8,128)S(1)} %get-tuple-element.78), channel_id=1, source_target_pairs={{0,128},{1,129},{2,130},{3,131},{4,132},{5,133},{6,134},{7,135},{8... | collective-permute-start | bytes 835592 | tf_op jit(solution)/shard_map/ppermute | solution.py:53
  100.9 11.9 %collective-permute-start.26 = (f32[272,256]{1,0:T(8,128)S(1)}, f32[272,256]{1,0:T(8,128)S(1)}, u32[]{:S(2)}, u32[]{:S(2)}) collective-permute-start(f32[272,256]{1,0:T(8,128)S(1)} %get-tuple-element.79), channel_id=1, source_target_pairs={{0,192},{1,193},{2,194},{3,195},{4,196},{5,197},{6,198},{7,199},{8... | collective-permute-start | bytes 835592 | tf_op jit(solution)/shard_map/ppermute | solution.py:53
  112.8 5.2 %collective-permute-start.27 = (f32[144,256]{1,0:T(8,128)S(1)}, f32[144,256]{1,0:T(8,128)S(1)}, u32[]{:S(2)}, u32[]{:S(2)}) collective-permute-start(f32[144,256]{1,0:T(8,128)S(1)} %get-tuple-element.81), channel_id=1, source_target_pairs={{0,32},{1,33},{2,34},{3,35},{4,36},{5,37},{6,38},{7,39},{8,40},{9,... | collective-permute-start | bytes 442376 | tf_op jit(solution)/shard_map/ppermute | solution.py:57

commit v5 on v4

--- a/solution.py
+++ b/solution.py
@@ -51,6 +51,10 @@
 
 def send_y(v, d):
     return lax.ppermute(v, AXES, table(lambda x, y, zl, zh, core: (x, (y + d) % 4, zl, zh, core)))
+
+
+def send_yz(v, dy, dz):
+    return lax.ppermute(v, AXES, table(lambda x, y, zl, zh, core: (x, (y + dy) % 4, zl ^ dz, zh, core)))
 
 
 def send_pair(v):
@@ -273,7 +277,8 @@
     return out if last else out[0]
 
 
-def prod_kernel(plan, v01, v23, near, near2, far, far2, m0, m1, m2, m3, acc):
+def prod_kernel(plan, v01, v23, near, near2, far, far2, *refs):
+    *ms, acc = refs
     x, y, zl, zh, core = plan[INFO], plan[INFO + 1], plan[INFO + 2], plan[INFO + 3], plan[INFO + 4]
     acc[...] = jnp.zeros_like(acc)
     vs = (v01.at[0], v01.at[1], v23.at[0], v23.at[1])
@@ -296,14 +301,12 @@
             term = jnp.where(plan[INFO + 5 + t] == s, vs[t][256:264, :], 0.0)
             total = term if total is None else total + term
         diag.append(total)
-    for k, m in enumerate((m0, m1, m2, m3)):
+    for k in range(4):
         for zrel in range(2):
+            m = ms[k * 2 + zrel]
             for s in range(2):
-                block = 2 * lax.rem(y + k, 4) + lax.rem(zl + zrel, 2)
-                at = (zrel * 2 + s) * 64
-                m[at:at + 64, :] = acc[s, block]
-        m[256:264, :] = diag[0]
-        m[264:272, :] = diag[1]
+                m[s * 64:(s + 1) * 64, :] = acc[s, 2 * lax.rem(y + k, 4) + (zl ^ zrel)]
+                m[128 + s * 8:136 + s * 8, :] = diag[s]
 
 
 def prod_call(plan, vs, pieces):
@@ -311,35 +314,14 @@
     return pl.pallas_call(
         prod_kernel,
         in_specs=[pl.BlockSpec(memory_space=SMEM)] + [spec] * 6,
-        out_specs=[spec] * 4,
-        out_shape=[jax.ShapeDtypeStruct((272, 256), F32)] * 4,
+        out_specs=[spec] * 8,
+        out_shape=[jax.ShapeDtypeStruct((144, 256), F32)] * 8,
         scratch_shapes=[VMEM((2, 8, 64, 256), F32)],
         compiler_params=pltpu.CompilerParams(vmem_limit_bytes=24 * 2**20),
         cost_estimate=pl.CostEstimate(flops=3 * 2 * 512 * 1024 * 256, bytes_accessed=5 * 2**20,
                                       transcendentals=0),
         name="product",
     )(plan, *vs, *pieces)
-
-
-def sum2_kernel(r0, r1, r2, r3, keep, away):
-    for rows, o, to in ((0, keep, 0), (128, away, 0)):
-        o[to:to + 128, :] = (r0[rows:rows + 128, :] + r1[rows:rows + 128, :]) + (
-            r2[rows:rows + 128, :] + r3[rows:rows + 128, :])
-    d = (r0[256:272, :] + r1[256:272, :]) + (r2[256:272, :] + r3[256:272, :])
-    keep[128:144, :] = d
-    away[128:144, :] = d
-
-
-def sum2_call(rs):
-    spec = pl.BlockSpec(memory_space=VMEM)
-    return pl.pallas_call(
-        sum2_kernel,
-        in_specs=[spec] * 4,
-        out_specs=[spec] * 2,
-        out_shape=[jax.ShapeDtypeStruct((144, 256), F32)] * 2,
-        compiler_params=pltpu.CompilerParams(vmem_limit_bytes=16 * 2**20),
-        name="sum_second",
-    )(*rs)
 
 
 def cross_kernel(plan, v, block, cross, base):
@@ -368,7 +350,10 @@
     )(plan, v, ginv)
 
 
-def last_kernel(plan, keep, came, dinv, base, resist, sigma):
+def last_kernel(plan, dinv, base, *refs):
+    *ms, resist, sigma, total = refs
+    sums = [ms[i][...] + ms[i + 1][...] for i in range(0, 8, 2)]
+    total[...] = (sums[0] + sums[1]) + (sums[2] + sums[3])
     flip = plan[INFO + 11]
     rows = lax.broadcasted_iota(jnp.int32, (256, 256), 0)
     at = lax.broadcasted_iota(jnp.int32, (64, 256), 0) + lax.rem(plan[INFO + 12], 4) * 64
@@ -377,25 +362,24 @@
     for f in range(2):
         s = f ^ flip
         d = dinv[pl.ds(s, 1), :]
-        total = keep[pl.ds(pl.multiple_of(s * 64, 64), 64), :] + came[
-            pl.ds(pl.multiple_of(s * 64, 64), 64), :]
-        sigma[:, f, :] = total + jnp.where(on_diag, d, 0.0)
+        sigma[:, f, :] = total[pl.ds(pl.multiple_of(s * 64, 64), 64), :] + jnp.where(on_diag, d, 0.0)
         deep = pl.ds(pl.multiple_of(128 + s * 8, 8), 8)
-        diag = (keep[deep, :] + came[deep, :])[0:1, :] + d
+        diag = total[deep, :][0:1, :] + d
         live = jnp.where(plan[INFO + 9] == f, plan[INFO + 10], 0)
         resist[f] = jnp.where(rows < live, diag + base[f], 0.0)
 
 
-def last_call(plan, keep, came, dinv, base):
+def last_call(plan, dinv, base, ms):
     spec = pl.BlockSpec(memory_space=VMEM)
     return pl.pallas_call(
         last_kernel,
-        in_specs=[pl.BlockSpec(memory_space=SMEM)] + [spec] * 4,
+        in_specs=[pl.BlockSpec(memory_space=SMEM)] + [spec] * 10,
         out_specs=[spec] * 2,
+        scratch_shapes=[VMEM((144, 256), F32)],
         out_shape=[jax.ShapeDtypeStruct((2, 256, 256), F32), jax.ShapeDtypeStruct((64, 2, 256), F32)],
         compiler_params=pltpu.CompilerParams(vmem_limit_bytes=12 * 2**20),
         name="last",
-    )(plan, keep, came, dinv, base)
+    )(plan, dinv, base, *ms)
 
 
 def body(ginv, ufactor, dinv, tile_map, counts, assign):
@@ -405,11 +389,12 @@
     b0 = send_pair(a0)
     plan = plan_call(tile_map, counts, assign)
     a1, a2, a3 = send_pq(a0, 1, 0), send_pq(a0, 2, 0), send_pq(a0, -1, 0)
-    b1, b2, b3 = send_pq(b0, 1, 0), send_pq(b0, 2, 0), send_pq(b0, -1, 0)
-    a1, a2, a3, b0, b1, b2, b3 = pin((a1, a2, a3, b0, b1, b2, b3))
+    b1, b3 = send_pq(b0, 1, 0), send_pq(b0, -1, 0)
+    a1, a2, a3, b0, b1, b3 = pin((a1, a2, a3, b0, b1, b3))
     ga = jnp.stack([a0, a1, a2, a3])
     ga1 = send_pq(ga, 0, 1)
     ga3 = send_pq(ga, 0, -1)
+    b2, plan = pin((send_pair(a2), plan))
     gb = jnp.stack([b0, b1, b2, b3])
     gb1 = send_pq(gb[:3], 0, 1)
     gb3 = send_pq(gb[1:], 0, -1)
@@ -442,11 +427,8 @@
     cross, base = cross_call(plan, v, ginv)
 
     m = prod_call(plan, [v01, v23], near + far)
-    m2 = send_y(m[2], 2)
-    r = [m[0], send_y(m[1], 1), m2, send_y(m[3], -1)]
-    keep, away = sum2_call(r)
-    came = send_pair(away)
-    resist, sigma = last_call(plan, keep, came, dinv, base)
+    r = [m[0]] + [send_yz(m[k * 2 + dz], k, dz) for k in (2, 1, 3, 0) for dz in (1, 0) if k or dz]
+    resist, sigma = last_call(plan, dinv, base, r)
     return cross, resist, sigma
 
 

time: 121 us -> 115 us (0.950)
  waiting for transfers between devices: 45 us -> 30.6 us
  starting transfers between devices: 44.2 us -> 53.1 us
    ppermute x3 -> x7, starting transfers between devices: 4.6 us -> 14.6 us  [send_yz(): lax.ppermute(v, AXES, table(lambda x, y, zl, zh, core: (x, (y + dy) % 4,...]
    ppermute x3 -> x7, waiting for transfers between devices: 11.3 us -> 4.35 us  [send_yz(): lax.ppermute(v, AXES, table(lambda x, y, zl, zh, core: (x, (y + dy) % 4,...]
    ppermute x14 -> x13, starting transfers between devices: 22.4 us -> 18.8 us  [send_pq(): return lax.ppermute(v, AXES, table(move))]
    ppermute x4, waiting for transfers between devices: 12.1 us -> 8.54 us  [send_zh(): lax.ppermute(v, AXES, table(lambda x, y, zl, zh, core: (x, y, zl, (zh + d...]
    ppermute x3, waiting for transfers between devices: 5.02 us -> 2.41 us  [send_pair(): lax.ppermute(v, AXES, table(lambda x, y, zl, zh, core: (x, y, 1 - zl, zh,...]
    ppermute x14 -> x13, waiting for transfers between devices: 10.2 us -> 8.86 us  [send_pq(): return lax.ppermute(v, AXES, table(move))]
  transfers between devices with their start and end apart: 28 -> 31, of which waited for: 16 -> 14; matrix products, arithmetic and copies ran while one was open for 0% -> 1% of each run, Pallas kernels for 15% -> 16%
where the time goes in v5:
time: 115 us; the launch traced here: 114 us
  starting transfers between devices  53.1 us (46%)
  waiting for transfers between devices  30.6 us (27%)
  Pallas kernels  22.5 us (20%)
  local copies, waits for them, and re-layouts  5.64 us (5%)
  other arithmetic  1.36 us (1%)
    ppermute x13, starting transfers between devices, send_pq(): return lax.ppermute(v, AXES, table(move))  18.8 us
    ppermute x7, starting transfers between devices, send_yz(): lax.ppermute(v, AXES, table(lambda x, y, zl, zh, core: (x, (y + dy) % 4,...  14.6 us
    ppermute x4, starting transfers between devices, send_zh(): lax.ppermute(v, AXES, table(lambda x, y, zl, zh, core: (x, y, zl, (zh + d...  11.1 us
    pallas_call x4, Pallas kernels, v_call(): pl.pallas_call(functools.partial(v_kernel, first, last, groups), in_specs...  10.7 us
    ppermute x13, waiting for transfers between devices, send_pq(): return lax.ppermute(v, AXES, table(move))  8.86 us
    ppermute x4, waiting for transfers between devices, send_zh(): lax.ppermute(v, AXES, table(lambda x, y, zl, zh, core: (x, y, zl, (zh + d...  8.54 us
    unnamed x15, local copies, waits for them, and re-layouts  5.39 us
    ppermute x2, waiting for transfers between devices, send_x_flip(): lax.ppermute(v, AXES, table(lambda x, y, zl, zh, core: (x ^ bit, y, zl, z...  4.96 us
  transfers between devices with their start and end apart: 31, of which 14 were waited for; matrix products, arithmetic and copies ran while one was open for 1% of the time, Pallas kernels for 16%

profile of v5, /device:TPU:2, one launch (start us, length us, event | category | flops | bytes accessed | tf_op | source)
XLA Modules:
  0.0 114.2 jit_solution(10794026098308201679)
XLA Ops:
  0.6 2.0 %collective-permute-start.3 = (f32[2,128,256]{2,1,0:T(8,128)}, f32[2,128,256]{2,1,0:T(8,128)S(1)}, u32[]{:S(2)}, u32[]{:S(2)}) collective-permute-start(f32[2,128,256]{2,1,0:T(8,128)} %param.7), channel_id=1, source_target_pairs={{0,32},{1,33},{2,34},{3,35},{4,36},{5,37},{6,38},{7,39},{8,40},{9,... | collective-permute-start | bytes 786440 | tf_op jit(solution)/shard_map/ppermute | solution.py:61
  2.6 1.5 %collective-permute-start = (f32[2,128,256]{2,1,0:T(8,128)}, f32[2,128,256]{2,1,0:T(8,128)S(1)}, u32[]{:S(2)}, u32[]{:S(2)}) collective-permute-start(f32[2,128,256]{2,1,0:T(8,128)} %param.7), channel_id=1, source_target_pairs={{0,8},{1,65},{2,10},{3,67},{4,12},{5,69},{6,14},{7,71},{8,16},{9,7... | collective-permute-start | bytes 786440 | tf_op jit(solution)/shard_map/ppermute | solution.py:41
  4.1 1.1 collective-permute-start.1
  5.2 2.2 %collective-permute-start.2 = (f32[2,128,256]{2,1,0:T(8,128)}, f32[2,128,256]{2,1,0:T(8,128)S(1)}, u32[]{:S(2)}, u32[]{:S(2)}) collective-permute-start(f32[2,128,256]{2,1,0:T(8,128)} %param.7), channel_id=1, source_target_pairs={{0,24},{1,193},{2,26},{3,195},{4,28},{5,197},{6,30},{7,199},{8,0},... | collective-permute-start | bytes 786440 | tf_op jit(solution)/shard_map/ppermute | solution.py:41
  7.4 1.8 %collective-permute-done.3 = f32[2,128,256]{2,1,0:T(8,128)S(1)} collective-permute-done((f32[2,128,256]{2,1,0:T(8,128)}, f32[2,128,256]{2,1,0:T(8,128)S(1)}, u32[]{:S(2)}, u32[]{:S(2)}) %collective-permute-start.3) | collective-permute-done | bytes 262176 | tf_op jit(solution)/shard_map/ppermute | solution.py:61
  9.2 1.5 %collective-permute-start.4 = (f32[2,128,256]{2,1,0:T(8,128)S(1)}, f32[2,128,256]{2,1,0:T(8,128)S(1)}, u32[]{:S(2)}, u32[]{:S(2)}) collective-permute-start(f32[2,128,256]{2,1,0:T(8,128)S(1)} %collective-permute-done.3), channel_id=1, source_target_pairs={{0,8},{1,65},{2,10},{3,67},{4,12},{5,69},{6,14},{7,71},{8,16},{9,7... | collective-permute-start | bytes 786440 | tf_op jit(solution)/shard_map/ppermute | solution.py:41
  10.6 0.5 collective-permute-start.5
  11.2 1.1 collective-permute-done.1
  12.3 2.3 %collective-permute-done.2 = f32[2,128,256]{2,1,0:T(8,128)S(1)} collective-permute-done((f32[2,128,256]{2,1,0:T(8,128)}, f32[2,128,256]{2,1,0:T(8,128)S(1)}, u32[]{:S(2)}, u32[]{:S(2)}) %collective-permute-start.2) | collective-permute-done | bytes 262176 | tf_op jit(solution)/shard_map/ppermute | solution.py:41
  14.6 0.9 collective-permute-done.4
  15.5 1.9 %collective-permute-done.5 = f32[2,128,256]{2,1,0:T(8,128)S(1)} collective-permute-done((f32[2,128,256]{2,1,0:T(8,128)S(1)}, f32[2,128,256]{2,1,0:T(8,128)S(1)}, u32[]{:S(2)}, u32[]{:S(2)}) %collective-permute-start.5) | collective-permute-done | bytes 262176 | tf_op jit(solution)/shard_map/ppermute | solution.py:41
  17.4 1.0 pad_maximum_fusion.refs_1_.refs_0_
  18.5 1.7 %collective-permute-start.7 = (f32[4,2,128,256]{3,2,1,0:T(8,128)S(1)}, f32[4,2,128,256]{3,2,1,0:T(8,128)S(1)}, u32[]{:S(2)}, u32[]{:S(2)}) collective-permute-start(f32[4,2,128,256]{3,2,1,0:T(8,128)S(1)} %pad_maximum_fusion.refs_1_.refs_0_), channel_id=1, source_target_pairs={{0,64},{1,9},{2,66},{3,11},{4,68},{5,13},{6,70},{7,15},{8,72},{9,1... | collective-permute-start | bytes 3145736 | tf_op jit(solution)/shard_map/ppermute | solution.py:41
  20.1 1.7 %collective-permute-start.8 = (f32[4,2,128,256]{3,2,1,0:T(8,128)S(1)}, f32[4,2,128,256]{3,2,1,0:T(8,128)S(1)}, u32[]{:S(2)}, u32[]{:S(2)}) collective-permute-start(f32[4,2,128,256]{3,2,1,0:T(8,128)S(1)} %pad_maximum_fusion.refs_1_.refs_0_), channel_id=1, source_target_pairs={{0,192},{1,25},{2,194},{3,27},{4,196},{5,29},{6,198},{7,31},{8,200... | collective-permute-start | bytes 3145736 | tf_op jit(solution)/shard_map/ppermute | solution.py:41
  21.8 1.3 %collective-permute-start.6 = (f32[2,128,256]{2,1,0:T(8,128)S(1)}, f32[2,128,256]{2,1,0:T(8,128)S(1)}, u32[]{:S(2)}, u32[]{:S(2)}) collective-permute-start(f32[2,128,256]{2,1,0:T(8,128)S(1)} %collective-permute-done.1), channel_id=1, source_target_pairs={{0,32},{1,33},{2,34},{3,35},{4,36},{5,37},{6,38},{7,39},{8,40},{9,... | collective-permute-start | bytes 786440 | tf_op jit(solution)/shard_map/ppermute | solution.py:61
  23.1 0.7 copy-done.2
  23.8 0.7 copy-done.3
  24.4 0.7 copy-done.4
  25.1 2.4 %plan.1 = s32[160]{0:T(256)S(1)} custom-call(s32[2,16]{1,0:T(2,128)S(1)} %copy-done.2, s32[2]{0:T(128)S(1)} %copy-done.3, s32[2]{0:T(128)S(1)} %copy-done.4), custom_call_target="tpu_custom_call" | custom-call | tf_op jit(solution)/shard_map/plan/pallas_call | solution.py:138
  27.5 0.7 collective-permute-done.6
  28.2 0.1 pad_maximum_fusion.3
  28.3 0.4 collective-permute-start.12
  28.8 2.9 %collective-permute-start.13 = (f32[3,2,128,256]{3,2,1,0:T(8,128)S(1)}, f32[3,2,128,256]{3,2,1,0:T(8,128)S(1)}, u32[]{:S(2)}, u32[]{:S(2)}) collective-permute-start(f32[3,2,128,256]{3,2,1,0:T(8,128)S(1)} %get-tuple-element.93), channel_id=1, source_target_pairs={{0,192},{1,25},{2,194},{3,27},{4,196},{5,29},{6,198},{7,31},{8,200... | collective-permute-start | bytes 2359304 | tf_op jit(solution)/shard_map/ppermute | solution.py:41
  31.6 3.4 %copy-done = f32[256,8192]{1,0:T(8,128)S(1)} copy-done((f32[256,8192]{1,0:T(8,128)S(1)}, f32[256,8192]{1,0:T(8,128)}, u32[]{:S(2)}) %copy-start) | copy-done | bytes 8388632
  35.0 1.6 %v_part.4.refs_4_ = f32[2,256,256]{2,1,0:T(8,128)S(1)} custom-call(s32[160]{0:T(256)S(1)} %plan.1, f32[256,8192]{1,0:T(8,128)S(1)} %copy-done, f32[4,2,128,256]{3,2,1,0:T(8,128)S(1)} %pad_maximum_fusion.refs_1_.refs_0_), custom_call_target="tpu_custom_call" | custom-call | flops 402653184 | bytes 16777216 | tf_op jit(solution)/shard_map/v_part/pallas_call | solution.py:264
  36.8 1.4 %collective-permute-start.11 = (f32[2,2,128,256]{3,2,1,0:T(8,128)S(1)}, f32[2,2,128,256]{3,2,1,0:T(8,128)S(1)}, u32[]{:S(2)}, u32[]{:S(2)}) collective-permute-start(f32[2,2,128,256]{3,2,1,0:T(8,128)S(1)} %pad_maximum_fusion.6), channel_id=1, source_target_pairs={{0,32},{1,33},{2,34},{3,35},{4,36},{5,37},{6,38},{7,39},{8,40},{9,... | collective-permute-start | bytes 1572872 | tf_op jit(solution)/shard_map/ppermute | solution.py:61
  38.2 1.2 %collective-permute-start.10 = (f32[2,2,128,256]{3,2,1,0:T(8,128)S(1)}, f32[2,2,128,256]{3,2,1,0:T(8,128)S(1)}, u32[]{:S(2)}, u32[]{:S(2)}) collective-permute-start(f32[2,2,128,256]{3,2,1,0:T(8,128)S(1)} %slice.35), channel_id=1, source_target_pairs={{0,192},{1,25},{2,194},{3,27},{4,196},{5,29},{6,198},{7,31},{8,200... | collective-permute-start | bytes 1572872 | tf_op jit(solution)/shard_map/ppermute | solution.py:41
  39.4 0.9 collective-permute-start.9
  40.2 0.1 pad_maximum_fusion.1.refs_1_
  40.3 3.5 %v_part.5.refs_3_ = f32[2,256,256]{2,1,0:T(8,128)S(1)} custom-call(s32[160]{0:T(256)S(1)} %plan.1, f32[256,8192]{1,0:T(8,128)S(1)} %copy-done, f32[4,2,128,256]{3,2,1,0:T(8,128)S(1)} %pad_maximum_fusion.1.refs_1_, f32[4,2,128,256]{3,2,1,0:T(8,128)S(1)} %collective-permute-done.7.refs_2_, f32[4,2,128,256]{3,2,1,0:T(8,128)S(1)} %collective-permute-done.8.refs_3_, ...), custom_call_target="tpu_custom_call" | custom-call | flops 1207959552 | bytes 50331648 | tf_op jit(solution)/shard_map/v_part/pallas_call | solution.py:264
  43.9 1.2 %collective-permute-start.14 = (f32[2,2,128,256]{3,2,1,0:T(8,128)S(1)}, f32[2,2,128,256]{3,2,1,0:T(8,128)S(1)}, u32[]{:S(2)}, u32[]{:S(2)}) collective-permute-start(f32[2,2,128,256]{3,2,1,0:T(8,128)S(1)} %slice.40), channel_id=1, source_target_pairs={{0,64},{1,9},{2,66},{3,11},{4,68},{5,13},{6,70},{7,15},{8,72},{9,1... | collective-permute-start | bytes 1572872 | tf_op jit(solution)/shard_map/ppermute | solution.py:41
  45.1 2.2 %collective-permute-start.15 = (f32[2,2,128,256]{3,2,1,0:T(8,128)S(1)}, f32[2,2,128,256]{3,2,1,0:T(8,128)S(1)}, u32[]{:S(2)}, u32[]{:S(2)}) collective-permute-start(f32[2,2,128,256]{3,2,1,0:T(8,128)S(1)} %slice.41), channel_id=1, source_target_pairs={{0,192},{1,25},{2,194},{3,27},{4,196},{5,29},{6,198},{7,31},{8,200... | collective-permute-start | bytes 1572872 | tf_op jit(solution)/shard_map/ppermute | solution.py:41
  47.3 2.3 %v_part.6.refs_7_ = f32[2,256,256]{2,1,0:T(8,128)S(1)} custom-call(s32[160]{0:T(256)S(1)} %plan.1, f32[256,8192]{1,0:T(8,128)S(1)} %copy-done, f32[3,2,128,256]{3,2,1,0:T(8,128)S(1)} %collective-permute-done.12.refs_1_.refs_4_, f32[3,2,128,256]{3,2,1,0:T(8,128)S(1)} %collective-permute-done.13.refs_2_.refs_7_, f32[2,256,256]{2,1,0:T(8,128)S(1)} %v_part.5.refs_3_), custom_call_target="tpu_custom_call" | custom-call | flops 603979776 | bytes 25165824 | tf_op jit(solution)/shard_map/v_part/pallas_call | solution.py:264
  49.6 0.2 collective-permute-done.9.refs_8_.refs_1_
  49.8 3.2 %u_rows.2 = (f32[256,256]{1,0:T(8,128)S(1)}, f32[8,64,128]{2,1,0:T(8,128)S(1)}) custom-call(s32[160]{0:T(256)S(1)} %plan.1, f32[4,2,128,256]{3,2,1,0:T(8,128)S(1)} %pad_maximum_fusion.refs_1_.refs_0_, f32[4,2,128,256]{3,2,1,0:T(8,128)S(1)} %pad_maximum_fusion.1.refs_1_, f32[4,2,128,256]{3,2,1,0:T(8,128)S(1)} %collective-permute-done.7.refs_2_, ...), custom_call_target="tpu_custom_call" | custom-call | tf_op jit(solution)/shard_map/u_rows/pallas_call | solution.py:193
  53.0 2.4 %collective-permute-done.14.refs_0_.refs_5_ = f32[2,2,128,256]{3,2,1,0:T(8,128)S(1)} collective-permute-done((f32[2,2,128,256]{3,2,1,0:T(8,128)S(1)}, f32[2,2,128,256]{3,2,1,0:T(8,128)S(1)}, u32[]{:S(2)}, u32[]{:S(2)}) %collective-permute-start.14) | collective-permute-done | bytes 524320 | tf_op jit(solution)/shard_map/ppermute | solution.py:41
  55.4 1.4 %u_rows.3 = (f32[256,256]{1,0:T(8,128)S(1)}, f32[8,64,128]{2,1,0:T(8,128)S(1)}) custom-call(s32[160]{0:T(256)S(1)} %plan.1, f32[2,2,128,256]{3,2,1,0:T(8,128)S(1)} %collective-permute-done.14.refs_0_.refs_5_, f32[2,2,128,256]{3,2,1,0:T(8,128)S(1)} %collective-permute-done.15.refs_1_.refs_6_, ...), custom_call_target="tpu_custom_call", output_to_operand_aliasing={{0}: (3, {}), {1}: (4, {})} | custom-call | tf_op jit(solution)/shard_map/u_rows/pallas_call | solution.py:193
  56.8 3.3 %collective-permute-start.18 = (f32[8,64,128]{2,1,0:T(8,128)S(1)}, f32[8,64,128]{2,1,0:T(8,128)S(1)}, u32[]{:S(2)}, u32[]{:S(2)}) collective-permute-start(f32[8,64,128]{2,1,0:T(8,128)S(1)} %get-tuple-element.78), channel_id=1, source_target_pairs={{0,2},{1,3},{2,4},{3,5},{4,6},{5,7},{6,0},{7,1},{8,10},{9,11},{10,... | collective-permute-start | bytes 786440 | tf_op jit(solution)/shard_map/ppermute | solution.py:69
  60.2 2.4 %collective-permute-start.19 = (f32[8,64,128]{2,1,0:T(8,128)S(1)}, f32[8,64,128]{2,1,0:T(8,128)S(1)}, u32[]{:S(2)}, u32[]{:S(2)}) collective-permute-start(f32[8,64,128]{2,1,0:T(8,128)S(1)} %get-tuple-element.78), channel_id=1, source_target_pairs={{0,6},{1,7},{2,0},{3,1},{4,2},{5,3},{6,4},{7,5},{8,14},{9,15},{10,... | collective-permute-start | bytes 786440 | tf_op jit(solution)/shard_map/ppermute | solution.py:69
  62.6 3.4 %v_part.7 = (f32[2,256,256]{2,1,0:T(8,128)S(1)}, f32[264,256]{1,0:T(8,128)S(1)}) custom-call(s32[160]{0:T(256)S(1)} %plan.1, f32[256,8192]{1,0:T(8,128)S(1)} %copy-done, f32[2,2,128,256]{3,2,1,0:T(8,128)S(1)} %collective-permute-done.9.refs_8_.refs_1_, f32[2,2,128,256]{3,2,1,0:T(8,128)S(1)} %collective-permute-done.10.refs_9_.refs_2_, ...), custom_call_target="tpu_custom_call" | custom-call | flops 1006632960 | bytes 41943040 | tf_op jit(solution)/shard_map/v_part/pallas_call | solution.py:264
  66.1 0.0 copy-start.1
  66.1 0.6 collective-permute-start.16
  66.7 3.6 %collective-permute-done.18 = f32[8,64,128]{2,1,0:T(8,128)S(1)} collective-permute-done((f32[8,64,128]{2,1,0:T(8,128)S(1)}, f32[8,64,128]{2,1,0:T(8,128)S(1)}, u32[]{:S(2)}, u32[]{:S(2)}) %collective-permute-start.18) | collective-permute-done | bytes 262176 | tf_op jit(solution)/shard_map/ppermute | solution.py:69
  70.2 0.1 pad_maximum_fusion.4.near
  70.3 0.1 collective-permute-start.22
  70.4 3.9 %collective-permute-start.20 = (f32[4,64,128]{2,1,0:T(8,128)S(1)}, f32[4,64,128]{2,1,0:T(8,128)S(1)}, u32[]{:S(2)}, u32[]{:S(2)}) collective-permute-start(f32[4,64,128]{2,1,0:T(8,128)S(1)} %slice.42), channel_id=1, source_target_pairs={{0,2},{1,3},{2,4},{3,5},{4,6},{5,7},{6,0},{7,1},{8,10},{9,11},{10,... | collective-permute-start | bytes 393224 | tf_op jit(solution)/shard_map/ppermute | solution.py:69
  74.4 2.9 %collective-permute-start.17 = (f32[2,264,256]{2,1,0:T(8,128)S(1)}, f32[2,264,256]{2,1,0:T(8,128)S(1)}, u32[]{:S(2)}, u32[]{:S(2)}) collective-permute-start(f32[2,264,256]{2,1,0:T(8,128)S(1)} %pad_maximum_fusion.5.v01), channel_id=1, source_target_pairs={{0,16},{1,17},{2,18},{3,19},{4,20},{5,21},{6,22},{7,23},{8,24},{9,... | collective-permute-start | bytes 1622024 | tf_op jit(solution)/shard_map/ppermute | solution.py:49
  77.3 1.5 %collective-permute-start.21 = (f32[4,64,128]{2,1,0:T(8,128)S(1)}, f32[4,64,128]{2,1,0:T(8,128)S(1)}, u32[]{:S(2)}, u32[]{:S(2)}) collective-permute-start(f32[4,64,128]{2,1,0:T(8,128)S(1)} %slice.43), channel_id=1, source_target_pairs={{0,6},{1,7},{2,0},{3,1},{4,2},{5,3},{6,4},{7,5},{8,14},{9,15},{10,... | collective-permute-start | bytes 393224 | tf_op jit(solution)/shard_map/ppermute | solution.py:69
  78.8 5.0 %collective-permute-done.21 = f32[4,64,128]{2,1,0:T(8,128)S(1)} collective-permute-done((f32[4,64,128]{2,1,0:T(8,128)S(1)}, f32[4,64,128]{2,1,0:T(8,128)S(1)}, u32[]{:S(2)}, u32[]{:S(2)}) %collective-permute-start.21) | collective-permute-done | bytes 131104 | tf_op jit(solution)/shard_map/ppermute | solution.py:69
  83.8 0.1 collective-permute-start.23
  83.9 1.5 %collective-permute-done.23.far2 = f32[8,64,128]{2,1,0:T(8,128)S(1)} collective-permute-done((f32[8,64,128]{2,1,0:T(8,128)S(1)}, f32[8,64,128]{2,1,0:T(8,128)S(1)}, u32[]{:S(2)}, u32[]{:S(2)}) %collective-permute-start.23) | collective-permute-done | bytes 262176 | tf_op jit(solution)/shard_map/ppermute | solution.py:65
  85.4 5.0 %collective-permute-done.17.v23 = f32[2,264,256]{2,1,0:T(8,128)S(1)} collective-permute-done((f32[2,264,256]{2,1,0:T(8,128)S(1)}, f32[2,264,256]{2,1,0:T(8,128)S(1)}, u32[]{:S(2)}, u32[]{:S(2)}) %collective-permute-start.17) | collective-permute-done | bytes 540704 | tf_op jit(solution)/shard_map/ppermute | solution.py:49
  90.3 1.8 %product.1 = (f32[144,256]{1,0:T(8,128)S(1)}, f32[144,256]{1,0:T(8,128)S(1)}, f32[144,256]{1,0:T(8,128)S(1)}, f32[144,256]{1,0:T(8,128)S(1)}, f32[144,256]{1,0:T...) custom-call(s32[160]{0:T(256)S(1)} %plan.1, ...), custom_call_target="tpu_custom_call" | custom-call | flops 805306368 | bytes 5242880 | tf_op jit(solution)/shard_map/product/pallas_call | solution.py:314
  92.2 3.8 %collective-permute-start.24 = (f32[144,256]{1,0:T(8,128)S(1)}, f32[144,256]{1,0:T(8,128)S(1)}, u32[]{:S(2)}, u32[]{:S(2)}) collective-permute-start(f32[144,256]{1,0:T(8,128)S(1)} %get-tuple-element.82), channel_id=1, source_target_pairs={{0,160},{1,161},{2,162},{3,163},{4,164},{5,165},{6,166},{7,167},{8... | collective-permute-start | bytes 442376 | tf_op jit(solution)/shard_map/ppermute | solution.py:57
  96.0 1.1 collective-permute-start.25
  97.1 1.5 %collective-permute-start.26 = (f32[144,256]{1,0:T(8,128)S(1)}, f32[144,256]{1,0:T(8,128)S(1)}, u32[]{:S(2)}, u32[]{:S(2)}) collective-permute-start(f32[144,256]{1,0:T(8,128)S(1)} %get-tuple-element.84), channel_id=1, source_target_pairs={{0,96},{1,97},{2,98},{3,99},{4,100},{5,101},{6,102},{7,103},{8,104... | collective-permute-start | bytes 442376 | tf_op jit(solution)/shard_map/ppermute | solution.py:57
  98.6 2.0 %collective-permute-start.27 = (f32[144,256]{1,0:T(8,128)S(1)}, f32[144,256]{1,0:T(8,128)S(1)}, u32[]{:S(2)}, u32[]{:S(2)}) collective-permute-start(f32[144,256]{1,0:T(8,128)S(1)} %get-tuple-element.85), channel_id=1, source_target_pairs={{0,64},{1,65},{2,66},{3,67},{4,68},{5,69},{6,70},{7,71},{8,72},{9,... | collective-permute-start | bytes 442376 | tf_op jit(solution)/shard_map/ppermute | solution.py:57
  100.6 2.2 %collective-permute-start.28 = (f32[144,256]{1,0:T(8,128)S(1)}, f32[144,256]{1,0:T(8,128)S(1)}, u32[]{:S(2)}, u32[]{:S(2)}) collective-permute-start(f32[144,256]{1,0:T(8,128)S(1)} %get-tuple-element.86), channel_id=1, source_target_pairs={{0,224},{1,225},{2,226},{3,227},{4,228},{5,229},{6,230},{7,231},{8... | collective-permute-start | bytes 442376 | tf_op jit(solution)/shard_map/ppermute | solution.py:57
  102.8 2.3 %collective-permute-start.29 = (f32[144,256]{1,0:T(8,128)S(1)}, f32[144,256]{1,0:T(8,128)S(1)}, u32[]{:S(2)}, u32[]{:S(2)}) collective-permute-start(f32[144,256]{1,0:T(8,128)S(1)} %get-tuple-element.87), channel_id=1, source_target_pairs={{0,192},{1,193},{2,194},{3,195},{4,196},{5,197},{6,198},{7,199},{8... | collective-permute-start | bytes 442376 | tf_op jit(solution)/shard_map/ppermute | solution.py:57
  105.1 2.4 %collective-permute-done.25.refs_2_ = f32[144,256]{1,0:T(8,128)S(1)} collective-permute-done((f32[144,256]{1,0:T(8,128)S(1)}, f32[144,256]{1,0:T(8,128)S(1)}, u32[]{:S(2)}, u32[]{:S(2)}) %collective-permute-start.25) | collective-permute-done | bytes 147488 | tf_op jit(solution)/shard_map/ppermute | solution.py:57
  107.5 1.7 %collective-permute-start.30 = (f32[144,256]{1,0:T(8,128)S(1)}, f32[144,256]{1,0:T(8,128)S(1)}, u32[]{:S(2)}, u32[]{:S(2)}) collective-permute-start(f32[144,256]{1,0:T(8,128)S(1)} %get-tuple-element.88), channel_id=1, source_target_pairs={{0,32},{1,33},{2,34},{3,35},{4,36},{5,37},{6,38},{7,39},{8,40},{9,... | collective-permute-start | bytes 442376 | tf_op jit(solution)/shard_map/ppermute | solution.py:57
  109.2 1.4 %cross.1 = (f32[2,256,256]{2,1,0:T(8,128)}, f32[2,256,256]{2,1,0:T(8,128)S(1)}) custom-call(s32[160]{0:T(256)S(1)} %plan.1, f32[2,256,256]{2,1,0:T(8,128)S(1)} %get-tuple-element.73.v, f32[256,8192]{1,0:T(8,128)S(1)} %bitcast.14), custom_call_target="tpu_custom_call" | custom-call | tf_op jit(solution)/shard_map/cross/pallas_call | solution.py:340
  110.6 2.0 %collective-permute-done.30.refs_7_ = f32[144,256]{1,0:T(8,128)S(1)} collective-permute-done((f32[144,256]{1,0:T(8,128)S(1)}, f32[144,256]{1,0:T(8,128)S(1)}, u32[]{:S(2)}, u32[]{:S(2)}) %collective-permute-start.30) | collective-permute-done | bytes 147488 | tf_op jit(solution)/shard_map/ppermute | solution.py:57
  112.6 1.6 %last.1 = (f32[2,256,256]{2,1,0:T(8,128)}, f32[64,2,256]{2,1,0:T(2,128)}) custom-call(s32[160]{0:T(256)S(1)} %plan.1, f32[2,256]{1,0:T(2,128)S(1)} %copy-done.1, f32[2,256,256]{2,1,0:T(8,128)S(1)} %get-tuple-element.75.base, f32[144,256]{1,0:T(8,128)S(1)} %get-tuple-element.81.refs_0_, f32[144,256]{1,0:T(8,128)S(1)} %collective-permute-done.24.refs_1_, ...), custom_call_target="tpu_custom_call" | custom-call | tf_op jit(solution)/shard_map/last/pallas_call | solution.py:374
  (40 shorter events, 0.4 us)
Async XLA Ops:
  0.6 8.5 %collective-permute-start.3 = (f32[2,128,256]{2,1,0:T(8,128)}, f32[2,128,256]{2,1,0:T(8,128)S(1)}, u32[]{:S(2)}, u32[]{:S(2)}) collective-permute-start(f32[2,128,256]{2,1,0:T(8,128)} %param.7), channel_id=1, source_target_pairs={{0,32},{1,33},{2,34},{3,35},{4,36},{5,37},{6,38},{7,39},{8,40},{9,... | collective-permute-start | bytes 786440 | tf_op jit(solution)/shard_map/ppermute | solution.py:61
  2.6 8.5 %collective-permute-start = (f32[2,128,256]{2,1,0:T(8,128)}, f32[2,128,256]{2,1,0:T(8,128)S(1)}, u32[]{:S(2)}, u32[]{:S(2)}) collective-permute-start(f32[2,128,256]{2,1,0:T(8,128)} %param.7), channel_id=1, source_target_pairs={{0,8},{1,65},{2,10},{3,67},{4,12},{5,69},{6,14},{7,71},{8,16},{9,7... | collective-permute-start | bytes 786440 | tf_op jit(solution)/shard_map/ppermute | solution.py:41
  4.1 8.2 %collective-permute-start.1 = (f32[2,128,256]{2,1,0:T(8,128)}, f32[2,128,256]{2,1,0:T(8,128)S(1)}, u32[]{:S(2)}, u32[]{:S(2)}) collective-permute-start(f32[2,128,256]{2,1,0:T(8,128)} %param.7), channel_id=1, source_target_pairs={{0,16},{1,129},{2,18},{3,131},{4,20},{5,133},{6,22},{7,135},{8,24}... | collective-permute-start | bytes 786440 | tf_op jit(solution)/shard_map/ppermute | solution.py:41
  5.2 9.4 %collective-permute-start.2 = (f32[2,128,256]{2,1,0:T(8,128)}, f32[2,128,256]{2,1,0:T(8,128)S(1)}, u32[]{:S(2)}, u32[]{:S(2)}) collective-permute-start(f32[2,128,256]{2,1,0:T(8,128)} %param.7), channel_id=1, source_target_pairs={{0,24},{1,193},{2,26},{3,195},{4,28},{5,197},{6,30},{7,199},{8,0},... | collective-permute-start | bytes 786440 | tf_op jit(solution)/shard_map/ppermute | solution.py:41
  9.2 6.4 %collective-permute-start.4 = (f32[2,128,256]{2,1,0:T(8,128)S(1)}, f32[2,128,256]{2,1,0:T(8,128)S(1)}, u32[]{:S(2)}, u32[]{:S(2)}) collective-permute-start(f32[2,128,256]{2,1,0:T(8,128)S(1)} %collective-permute-done.3), channel_id=1, source_target_pairs={{0,8},{1,65},{2,10},{3,67},{4,12},{5,69},{6,14},{7,71},{8,16},{9,7... | collective-permute-start | bytes 786440 | tf_op jit(solution)/shard_map/ppermute | solution.py:41
  10.6 6.8 %collective-permute-start.5 = (f32[2,128,256]{2,1,0:T(8,128)S(1)}, f32[2,128,256]{2,1,0:T(8,128)S(1)}, u32[]{:S(2)}, u32[]{:S(2)}) collective-permute-start(f32[2,128,256]{2,1,0:T(8,128)S(1)} %collective-permute-done.3), channel_id=1, source_target_pairs={{0,24},{1,193},{2,26},{3,195},{4,28},{5,197},{6,30},{7,199},{8,0},... | collective-permute-start | bytes 786440 | tf_op jit(solution)/shard_map/ppermute | solution.py:41
  18.5 18.1 %collective-permute-start.7 = (f32[4,2,128,256]{3,2,1,0:T(8,128)S(1)}, f32[4,2,128,256]{3,2,1,0:T(8,128)S(1)}, u32[]{:S(2)}, u32[]{:S(2)}) collective-permute-start(f32[4,2,128,256]{3,2,1,0:T(8,128)S(1)} %pad_maximum_fusion.refs_1_.refs_0_), channel_id=1, source_target_pairs={{0,64},{1,9},{2,66},{3,11},{4,68},{5,13},{6,70},{7,15},{8,72},{9,1... | collective-permute-start | bytes 3145736 | tf_op jit(solution)/shard_map/ppermute | solution.py:41
  20.1 16.5 %collective-permute-start.8 = (f32[4,2,128,256]{3,2,1,0:T(8,128)S(1)}, f32[4,2,128,256]{3,2,1,0:T(8,128)S(1)}, u32[]{:S(2)}, u32[]{:S(2)}) collective-permute-start(f32[4,2,128,256]{3,2,1,0:T(8,128)S(1)} %pad_maximum_fusion.refs_1_.refs_0_), channel_id=1, source_target_pairs={{0,192},{1,25},{2,194},{3,27},{4,196},{5,29},{6,198},{7,31},{8,200... | collective-permute-start | bytes 3145736 | tf_op jit(solution)/shard_map/ppermute | solution.py:41
  21.8 6.4 %collective-permute-start.6 = (f32[2,128,256]{2,1,0:T(8,128)S(1)}, f32[2,128,256]{2,1,0:T(8,128)S(1)}, u32[]{:S(2)}, u32[]{:S(2)}) collective-permute-start(f32[2,128,256]{2,1,0:T(8,128)S(1)} %collective-permute-done.1), channel_id=1, source_target_pairs={{0,32},{1,33},{2,34},{3,35},{4,36},{5,37},{6,38},{7,39},{8,40},{9,... | collective-permute-start | bytes 786440 | tf_op jit(solution)/shard_map/ppermute | solution.py:61
  23.1 0.7 copy-start.2
  23.8 0.7 copy-start.3
  24.4 0.7 copy-start.4
  28.3 15.5 %collective-permute-start.12 = (f32[3,2,128,256]{3,2,1,0:T(8,128)S(1)}, f32[3,2,128,256]{3,2,1,0:T(8,128)S(1)}, u32[]{:S(2)}, u32[]{:S(2)}) collective-permute-start(f32[3,2,128,256]{3,2,1,0:T(8,128)S(1)} %get-tuple-element.94), channel_id=1, source_target_pairs={{0,64},{1,9},{2,66},{3,11},{4,68},{5,13},{6,70},{7,15},{8,72},{9,1... | collective-permute-start | bytes 2359304 | tf_op jit(solution)/shard_map/ppermute | solution.py:41
  28.8 15.1 %collective-permute-start.13 = (f32[3,2,128,256]{3,2,1,0:T(8,128)S(1)}, f32[3,2,128,256]{3,2,1,0:T(8,128)S(1)}, u32[]{:S(2)}, u32[]{:S(2)}) collective-permute-start(f32[3,2,128,256]{3,2,1,0:T(8,128)S(1)} %get-tuple-element.93), channel_id=1, source_target_pairs={{0,192},{1,25},{2,194},{3,27},{4,196},{5,29},{6,198},{7,31},{8,200... | collective-permute-start | bytes 2359304 | tf_op jit(solution)/shard_map/ppermute | solution.py:41
  31.6 3.4 %copy-start = (f32[256,8192]{1,0:T(8,128)S(1)}, f32[256,8192]{1,0:T(8,128)}, u32[]{:S(2)}) copy-start(f32[256,8192]{1,0:T(8,128)} %block.1) | copy-start | bytes 25165828
  36.8 12.8 %collective-permute-start.11 = (f32[2,2,128,256]{3,2,1,0:T(8,128)S(1)}, f32[2,2,128,256]{3,2,1,0:T(8,128)S(1)}, u32[]{:S(2)}, u32[]{:S(2)}) collective-permute-start(f32[2,2,128,256]{3,2,1,0:T(8,128)S(1)} %pad_maximum_fusion.6), channel_id=1, source_target_pairs={{0,32},{1,33},{2,34},{3,35},{4,36},{5,37},{6,38},{7,39},{8,40},{9,... | collective-permute-start | bytes 1572872 | tf_op jit(solution)/shard_map/ppermute | solution.py:61
  38.2 11.4 %collective-permute-start.10 = (f32[2,2,128,256]{3,2,1,0:T(8,128)S(1)}, f32[2,2,128,256]{3,2,1,0:T(8,128)S(1)}, u32[]{:S(2)}, u32[]{:S(2)}) collective-permute-start(f32[2,2,128,256]{3,2,1,0:T(8,128)S(1)} %slice.35), channel_id=1, source_target_pairs={{0,192},{1,25},{2,194},{3,27},{4,196},{5,29},{6,198},{7,31},{8,200... | collective-permute-start | bytes 1572872 | tf_op jit(solution)/shard_map/ppermute | solution.py:41
  39.4 10.4 %collective-permute-start.9 = (f32[2,2,128,256]{3,2,1,0:T(8,128)S(1)}, f32[2,2,128,256]{3,2,1,0:T(8,128)S(1)}, u32[]{:S(2)}, u32[]{:S(2)}) collective-permute-start(f32[2,2,128,256]{3,2,1,0:T(8,128)S(1)} %slice.34), channel_id=1, source_target_pairs={{0,64},{1,9},{2,66},{3,11},{4,68},{5,13},{6,70},{7,15},{8,72},{9,1... | collective-permute-start | bytes 1572872 | tf_op jit(solution)/shard_map/ppermute | solution.py:41
  43.9 11.5 %collective-permute-start.14 = (f32[2,2,128,256]{3,2,1,0:T(8,128)S(1)}, f32[2,2,128,256]{3,2,1,0:T(8,128)S(1)}, u32[]{:S(2)}, u32[]{:S(2)}) collective-permute-start(f32[2,2,128,256]{3,2,1,0:T(8,128)S(1)} %slice.40), channel_id=1, source_target_pairs={{0,64},{1,9},{2,66},{3,11},{4,68},{5,13},{6,70},{7,15},{8,72},{9,1... | collective-permute-start | bytes 1572872 | tf_op jit(solution)/shard_map/ppermute | solution.py:41
  45.1 10.3 %collective-permute-start.15 = (f32[2,2,128,256]{3,2,1,0:T(8,128)S(1)}, f32[2,2,128,256]{3,2,1,0:T(8,128)S(1)}, u32[]{:S(2)}, u32[]{:S(2)}) collective-permute-start(f32[2,2,128,256]{3,2,1,0:T(8,128)S(1)} %slice.41), channel_id=1, source_target_pairs={{0,192},{1,25},{2,194},{3,27},{4,196},{5,29},{6,198},{7,31},{8,200... | collective-permute-start | bytes 1572872 | tf_op jit(solution)/shard_map/ppermute | solution.py:41
  56.8 13.4 %collective-permute-start.18 = (f32[8,64,128]{2,1,0:T(8,128)S(1)}, f32[8,64,128]{2,1,0:T(8,128)S(1)}, u32[]{:S(2)}, u32[]{:S(2)}) collective-permute-start(f32[8,64,128]{2,1,0:T(8,128)S(1)} %get-tuple-element.78), channel_id=1, source_target_pairs={{0,2},{1,3},{2,4},{3,5},{4,6},{5,7},{6,0},{7,1},{8,10},{9,11},{10,... | collective-permute-start | bytes 786440 | tf_op jit(solution)/shard_map/ppermute | solution.py:69
  60.2 10.1 %collective-permute-start.19 = (f32[8,64,128]{2,1,0:T(8,128)S(1)}, f32[8,64,128]{2,1,0:T(8,128)S(1)}, u32[]{:S(2)}, u32[]{:S(2)}) collective-permute-start(f32[8,64,128]{2,1,0:T(8,128)S(1)} %get-tuple-element.78), channel_id=1, source_target_pairs={{0,6},{1,7},{2,0},{3,1},{4,2},{5,3},{6,4},{7,5},{8,14},{9,15},{10,... | collective-permute-start | bytes 786440 | tf_op jit(solution)/shard_map/ppermute | solution.py:69
  62.6 46.6 %slice-start = ((s8[8388608]{0:T(1024)(128)(4,1)}), s8[4194304]{0:T(1024)(128)(4,1)S(1)}, s32[]{:S(2)}) async-start(s8[8388608]{0:T(1024)(128)(4,1)} %bitcast.13), calls=%async_computation | async-start | bytes 8388608
  62.6 46.6 %slice-start.1 = ((s8[8388608]{0:T(1024)(128)(4,1)}), s8[4194304]{0:T(1024)(128)(4,1)S(1)}, s32[]{:S(2)}) async-start(s8[8388608]{0:T(1024)(128)(4,1)} %bitcast.13), calls=%async_computation.1 | async-start | bytes 8388608
  66.1 46.5 %copy-start.1 = (f32[2,256]{1,0:T(2,128)S(1)}, f32[2,256]{1,0:T(2,128)}, u32[]{:S(2)}) copy-start(f32[2,256]{1,0:T(2,128)} %dinv.1) | copy-start | bytes 6148
  66.1 8.3 %collective-permute-start.16 = (f32[264,256]{1,0:T(8,128)S(1)}, f32[264,256]{1,0:T(8,128)S(1)}, u32[]{:S(2)}, u32[]{:S(2)}) collective-permute-start(f32[264,256]{1,0:T(8,128)S(1)} %get-tuple-element.76), channel_id=1, source_target_pairs={{0,8},{1,9},{2,10},{3,11},{4,12},{5,13},{6,14},{7,15},{8,0},{9,1},... | collective-permute-start | bytes 811016 | tf_op jit(solution)/shard_map/ppermute | solution.py:49
  70.3 20.0 %collective-permute-start.22 = (f32[3,8,64,128]{3,2,1,0:T(8,128)S(1)}, f32[3,8,64,128]{3,2,1,0:T(8,128)S(1)}, u32[]{:S(2)}, u32[]{:S(2)}) collective-permute-start(f32[3,8,64,128]{3,2,1,0:T(8,128)S(1)} %pad_maximum_fusion.4.near), channel_id=1, source_target_pairs={{0,1},{1,0},{2,3},{3,2},{4,5},{5,4},{6,7},{7,6},{8,9},{9,8},{10,11... | collective-permute-start | bytes 2359304 | tf_op jit(solution)/shard_map/ppermute | solution.py:65
  70.4 8.3 %collective-permute-start.20 = (f32[4,64,128]{2,1,0:T(8,128)S(1)}, f32[4,64,128]{2,1,0:T(8,128)S(1)}, u32[]{:S(2)}, u32[]{:S(2)}) collective-permute-start(f32[4,64,128]{2,1,0:T(8,128)S(1)} %slice.42), channel_id=1, source_target_pairs={{0,2},{1,3},{2,4},{3,5},{4,6},{5,7},{6,0},{7,1},{8,10},{9,11},{10,... | collective-permute-start | bytes 393224 | tf_op jit(solution)/shard_map/ppermute | solution.py:69
  74.4 16.0 %collective-permute-start.17 = (f32[2,264,256]{2,1,0:T(8,128)S(1)}, f32[2,264,256]{2,1,0:T(8,128)S(1)}, u32[]{:S(2)}, u32[]{:S(2)}) collective-permute-start(f32[2,264,256]{2,1,0:T(8,128)S(1)} %pad_maximum_fusion.5.v01), channel_id=1, source_target_pairs={{0,16},{1,17},{2,18},{3,19},{4,20},{5,21},{6,22},{7,23},{8,24},{9,... | collective-permute-start | bytes 1622024 | tf_op jit(solution)/shard_map/ppermute | solution.py:49
  77.3 6.5 %collective-permute-start.21 = (f32[4,64,128]{2,1,0:T(8,128)S(1)}, f32[4,64,128]{2,1,0:T(8,128)S(1)}, u32[]{:S(2)}, u32[]{:S(2)}) collective-permute-start(f32[4,64,128]{2,1,0:T(8,128)S(1)} %slice.43), channel_id=1, source_target_pairs={{0,6},{1,7},{2,0},{3,1},{4,2},{5,3},{6,4},{7,5},{8,14},{9,15},{10,... | collective-permute-start | bytes 393224 | tf_op jit(solution)/shard_map/ppermute | solution.py:69
  83.8 1.6 %collective-permute-start.23 = (f32[8,64,128]{2,1,0:T(8,128)S(1)}, f32[8,64,128]{2,1,0:T(8,128)S(1)}, u32[]{:S(2)}, u32[]{:S(2)}) collective-permute-start(f32[8,64,128]{2,1,0:T(8,128)S(1)} %constant_dynamic-update-slice_fusion.near2), channel_id=1, source_target_pairs={{0,1},{1,0},{2,3},{3,2},{4,5},{5,4},{6,7},{7,6},{8,9},{9,8},{10,11... | collective-permute-start | bytes 786440 | tf_op jit(solution)/shard_map/ppermute | solution.py:65
  92.2 10.6 %collective-permute-start.24 = (f32[144,256]{1,0:T(8,128)S(1)}, f32[144,256]{1,0:T(8,128)S(1)}, u32[]{:S(2)}, u32[]{:S(2)}) collective-permute-start(f32[144,256]{1,0:T(8,128)S(1)} %get-tuple-element.82), channel_id=1, source_target_pairs={{0,160},{1,161},{2,162},{3,163},{4,164},{5,165},{6,166},{7,167},{8... | collective-permute-start | bytes 442376 | tf_op jit(solution)/shard_map/ppermute | solution.py:57
  96.0 11.4 %collective-permute-start.25 = (f32[144,256]{1,0:T(8,128)S(1)}, f32[144,256]{1,0:T(8,128)S(1)}, u32[]{:S(2)}, u32[]{:S(2)}) collective-permute-start(f32[144,256]{1,0:T(8,128)S(1)} %get-tuple-element.83), channel_id=1, source_target_pairs={{0,128},{1,129},{2,130},{3,131},{4,132},{5,133},{6,134},{7,135},{8... | collective-permute-start | bytes 442376 | tf_op jit(solution)/shard_map/ppermute | solution.py:57
  97.1 13.5 %collective-permute-start.26 = (f32[144,256]{1,0:T(8,128)S(1)}, f32[144,256]{1,0:T(8,128)S(1)}, u32[]{:S(2)}, u32[]{:S(2)}) collective-permute-start(f32[144,256]{1,0:T(8,128)S(1)} %get-tuple-element.84), channel_id=1, source_target_pairs={{0,96},{1,97},{2,98},{3,99},{4,100},{5,101},{6,102},{7,103},{8,104... | collective-permute-start | bytes 442376 | tf_op jit(solution)/shard_map/ppermute | solution.py:57
  98.6 12.0 %collective-permute-start.27 = (f32[144,256]{1,0:T(8,128)S(1)}, f32[144,256]{1,0:T(8,128)S(1)}, u32[]{:S(2)}, u32[]{:S(2)}) collective-permute-start(f32[144,256]{1,0:T(8,128)S(1)} %get-tuple-element.85), channel_id=1, source_target_pairs={{0,64},{1,65},{2,66},{3,67},{4,68},{5,69},{6,70},{7,71},{8,72},{9,... | collective-permute-start | bytes 442376 | tf_op jit(solution)/shard_map/ppermute | solution.py:57
  100.6 10.0 %collective-permute-start.28 = (f32[144,256]{1,0:T(8,128)S(1)}, f32[144,256]{1,0:T(8,128)S(1)}, u32[]{:S(2)}, u32[]{:S(2)}) collective-permute-start(f32[144,256]{1,0:T(8,128)S(1)} %get-tuple-element.86), channel_id=1, source_target_pairs={{0,224},{1,225},{2,226},{3,227},{4,228},{5,229},{6,230},{7,231},{8... | collective-permute-start | bytes 442376 | tf_op jit(solution)/shard_map/ppermute | solution.py:57
  102.8 7.8 %collective-permute-start.29 = (f32[144,256]{1,0:T(8,128)S(1)}, f32[144,256]{1,0:T(8,128)S(1)}, u32[]{:S(2)}, u32[]{:S(2)}) collective-permute-start(f32[144,256]{1,0:T(8,128)S(1)} %get-tuple-element.87), channel_id=1, source_target_pairs={{0,192},{1,193},{2,194},{3,195},{4,196},{5,197},{6,198},{7,199},{8... | collective-permute-start | bytes 442376 | tf_op jit(solution)/shard_map/ppermute | solution.py:57
  107.5 5.1 %collective-permute-start.30 = (f32[144,256]{1,0:T(8,128)S(1)}, f32[144,256]{1,0:T(8,128)S(1)}, u32[]{:S(2)}, u32[]{:S(2)}) collective-permute-start(f32[144,256]{1,0:T(8,128)S(1)} %get-tuple-element.88), channel_id=1, source_target_pairs={{0,32},{1,33},{2,34},{3,35},{4,36},{5,37},{6,38},{7,39},{8,40},{9,... | collective-permute-start | bytes 442376 | tf_op jit(solution)/shard_map/ppermute | solution.py:57
